TPU v7x, 256 devices: a whole 4x4x8 slice. The times are simulated.
256 devices in a mesh: ctx: 32 (over z_lo, y, core), kv: 8 (over x, z_hi).
Axes of the slice: x: 4, y: 4, z: 8 (z_hi: 2, z_lo: 4; z = z_hi * 4 + z_lo), core: 2. Of those that a mesh axis runs over, the one named last changes fastest.
Arguments:
- queries: bfloat16 [4096, 128, 128], P('ctx', 'kv'), may hold values from -6 to 6
- keys: bfloat16 [4096, 8, 128], P('ctx', 'kv'), may hold values from -6 to 6
- values: bfloat16 [4096, 8, 128], P('ctx', 'kv'), may hold values from -6 to 6
- outputs: bfloat16 [4096, 128, 128], P('ctx', 'kv'), may hold values from -6 to 6
- out_grad: bfloat16 [4096, 128, 128], P('ctx', 'kv'), may hold values from -6 to 6
- logsumexp: float32 [128, 4096], P('kv', 'ctx'), may hold values from 2 to 5
- doc_lengths: int32 [12], replicated, may hold values from 1 to 512, 4096 in all
- block_order: int32 [32], replicated, may hold values from 0 to 31, each once
Outputs:
- grad_queries: bfloat16 [4096, 128, 128], P('ctx', 'kv')
- grad_keys: bfloat16 [4096, 1024], P(('ctx', 'kv'))
- grad_values: bfloat16 [4096, 1024], P(('ctx', 'kv'))
Inputs may be any that keep to these rules, and one draw needn't show every extreme that they name: `doc_lengths`: the documents lie one after another and fill the 4096 tokens; the longest has exactly 512 tokens. A permutation of the 32 blocks: arranged rows i * 128 to i * 128 + 127 hold sequence positions block_order[i] * 128 onward.
All inputs are finite; a program needn't handle non-finite values.
Results may differ from a plain program's by a relative error of at most 0.0051.
Values may be sent and summed in bfloat16 or wider, within the bound.
No kernel may reach another device: no remote copies, remote signals or barrier semaphores. Data moves between devices by JAX's collectives and lax.ppermute only.
A program may use at most 64 MiB of HBM per device.

v0:
```python
import jax
import jax.numpy as jnp
from jax import lax
from jax.sharding import PartitionSpec as P

BLK = 128


def doc_index(positions, ends):
    return jnp.sum((ends[None, :] <= positions[:, None]).astype(jnp.int32), axis=1)


def local(queries, keys, values, outputs, out_grad, logsumexp, doc_lengths, block_order):
    tok_rows = queries.shape[0]
    head_count = queries.shape[1]
    head_size = queries.shape[2]
    total_rows = block_order.shape[0] * BLK
    local_blocks = tok_rows // BLK
    scale = head_size ** (-0.5)
    ends = jnp.cumsum(doc_lengths)
    first_block = lax.axis_index("ctx") * local_blocks
    my_blocks = lax.dynamic_slice_in_dim(block_order, first_block, local_blocks)
    offsets = jnp.arange(BLK, dtype=jnp.int32)
    query_pos = (my_blocks[:, None] * BLK + offsets[None, :]).reshape(-1)
    query_doc = doc_index(query_pos, ends)
    delta = jnp.sum(out_grad.astype(jnp.float32) * outputs.astype(jnp.float32), axis=2)
    lse_rows = jnp.transpose(logsumexp)
    key_local = keys[:, 0, :]
    value_local = values[:, 0, :]
    initial = (
        jnp.zeros((tok_rows, head_count, head_size), jnp.float32),
        jnp.zeros((total_rows, head_size), jnp.float32),
        jnp.zeros((total_rows, head_size), jnp.float32),
    )
    key_piece = lax.all_gather(key_local, "ctx", axis=0, tiled=True)
    value_piece = lax.all_gather(value_local, "ctx", axis=0, tiled=True)
    key_blocks = key_piece.shape[0] // BLK
    pair_count = local_blocks * key_blocks
    pair_ids = jnp.arange(pair_count, dtype=jnp.int32)
    query_block = pair_ids // key_blocks
    key_block = pair_ids % key_blocks
    q_first = my_blocks[query_block] * BLK
    q_last = q_first + BLK - 1
    k_first = key_block * BLK
    k_near = jnp.minimum(k_first + BLK - 1, q_last)
    useful = (k_first <= q_last) & (doc_index(k_near, ends) >= doc_index(q_first, ends))
    slot = jnp.cumsum(useful.astype(jnp.int32)) - 1
    worklist = (
        jnp.zeros((pair_count,), jnp.int32)
        .at[jnp.where(useful, slot, pair_count)]
        .set(pair_ids, mode="drop")
    )
    active = jnp.sum(useful.astype(jnp.int32))

    def one_tile(index, state):
        grad_q, grad_k, grad_v = state
        pair = worklist[index]
        k_index = pair % key_blocks
        local_key = k_index * BLK
        key_tile = lax.dynamic_slice_in_dim(key_piece, local_key, BLK)
        value_tile = lax.dynamic_slice_in_dim(value_piece, local_key, BLK)
        key_pos = local_key + offsets
        key_docs = doc_index(key_pos, ends)
        allowed = (query_doc[:, None] == key_docs[None, :]) & (
            key_pos[None, :] <= query_pos[:, None]
        )
        scores = (
            jnp.einsum("qhd,kd->qhk", queries, key_tile, preferred_element_type=jnp.float32) * scale
        )
        probs = jnp.where(
            allowed[:, None, :], jnp.exp(scores - lse_rows[:, :, None]), jnp.float32(0.0)
        )
        probs_low = probs.astype(jnp.bfloat16)
        value_part = jnp.einsum(
            "qhk,qhd->kd", probs_low, out_grad, preferred_element_type=jnp.float32
        )
        dprob = jnp.einsum("qhd,kd->qhk", out_grad, value_tile, preferred_element_type=jnp.float32)
        dscore = (probs * (dprob - delta[:, :, None])).astype(jnp.bfloat16)
        query_part = jnp.einsum("qhk,kd->qhd", dscore, key_tile, preferred_element_type=jnp.float32)
        key_part = jnp.einsum("qhk,qhd->kd", dscore, queries, preferred_element_type=jnp.float32)
        grad_q = grad_q + query_part
        grad_k = lax.dynamic_update_slice_in_dim(
            grad_k, lax.dynamic_slice_in_dim(grad_k, local_key, BLK) + key_part, local_key, 0
        )
        grad_v = lax.dynamic_update_slice_in_dim(
            grad_v, lax.dynamic_slice_in_dim(grad_v, local_key, BLK) + value_part, local_key, 0
        )
        return (grad_q, grad_k, grad_v)

    grad_q, grad_k, grad_v = lax.fori_loop(0, active, one_tile, initial)
    grad_queries = (grad_q * scale).astype(jnp.bfloat16)
    grad_k = grad_k * scale
    summed = (
        lax.psum_scatter(grad_k, "ctx", scatter_dimension=0, tiled=True),
        lax.psum_scatter(grad_v, "ctx", scatter_dimension=0, tiled=True),
    )
    grad_keys, grad_values = (
        lax.all_to_all(
            summed[0].astype(jnp.bfloat16), "kv", split_axis=0, concat_axis=1, tiled=True
        ),
        lax.all_to_all(
            summed[1].astype(jnp.bfloat16), "kv", split_axis=0, concat_axis=1, tiled=True
        ),
    )
    return (grad_queries, grad_keys, grad_values)


def solution(mesh):
    in_specs = (
        P("ctx", "kv", None),
        P("ctx", "kv", None),
        P("ctx", "kv", None),
        P("ctx", "kv", None),
        P("ctx", "kv", None),
        P("kv", "ctx"),
        P(),
        P(),
    )
    out_specs = (P("ctx", "kv", None), P(("ctx", "kv"), None), P(("ctx", "kv"), None))
    return jax.shard_map(local, mesh=mesh, in_specs=in_specs, out_specs=out_specs, check_vma=False)
```

profile of v0, /device:TPU:2, one launch (start us, length us, event | category | flops | bytes accessed | tf_op | source)
XLA Modules:
  0.0 501.0 jit_solution(11561959101815838074)
XLA Ops:
  7.2 0.7 all-gather.5.cloned.1.call-update
  8.0 0.7 all-gather.7.cloned.1.call-update
  8.7 0.8 reduce-window.13
  9.5 1.2 dynamic_slice.33
  13.0 1.2 copy.42
  14.2 1.5 multiply_reduce_fusion
  16.8 1.3 fusion.35
  18.1 53.6 %all-gather.5.cloned.1.call-done = bf16[4096,1,128]{2,0,1:T(8,128)(2,1)} async-done(((bf16[128,1,128]{2,0,1:T(8,128)(2,1)}), bf16[4096,1,128]{2,0,1:T(8,128)(2,1)}) %all-gather.5.cloned.1.call-update) | async-done | bytes 1048592 | tf_op jit(solution)/shard_map/all_gather | solution.py:35
  71.8 59.7 %all-gather.7.cloned.1.call-done = bf16[4096,1,128]{2,0,1:T(8,128)(2,1)} async-done(((bf16[128,1,128]{2,0,1:T(8,128)(2,1)}), bf16[4096,1,128]{2,0,1:T(8,128)(2,1)}) %all-gather.7.cloned.1.call-update) | async-done | bytes 1048592 | tf_op jit(solution)/shard_map/all_gather | solution.py:36
  131.6 1.4 broadcast.306.clone
  133.0 1.5 broadcast.306
  134.5 21.0 %while.17 = (s32[]{:T(128)}, f32[128,16,128]{2,0,1:T(8,128)S(1)}, f32[4096,128]{1,0:T(8,128)}, f32[4096,128]{1,0:T(8,128)}, s32[]{:T(128)}, /*index=5*/s32[128]{...) while((s32[]{:T(128)}, f32[128,16,128]{2,0,1:T(8,128)S(1)}, ...), condition=%wide.region_10.11_spmd.clone, body=%wide.region_8.10_spmd.clone.sunk | while | flops 337728128 | bytes 9327066 | solution.py:90
  137.8 1.1 fusion.71
  139.0 1.1 fusion.72
  140.0 1.8 fusion.74
  141.8 1.1 convolution_add_fusion.2
  142.9 1.8 fusion.73
  148.0 1.1 fusion.71
  149.2 1.1 fusion.72
  150.2 1.7 fusion.74
  152.0 1.1 convolution_add_fusion.2
  153.1 1.8 fusion.73
  155.5 1.5 copy-done
  157.0 1.5 broadcast_multiply_fusion
  158.6 172.2 %reduce-scatter.5.cloned.1.call-done = f32[128,128]{1,0:T(8,128)} async-done(((f32[4096,128]{1,0:T(8,128)}), f32[128,128]{1,0:T(8,128)}) %reduce-scatter.5.cloned.1.call-update) | async-done | bytes 65552 | tf_op jit(solution)/shard_map/reduce_scatter | solution.py:95
  330.8 1.5 convert_element_type.65
  332.2 7.3 %all-to-all-start.1 = ((bf16[8,16,128]{2,1,0:T(8,128)(2,1)}), bf16[8,16,128]{2,1,0:T(8,128)(2,1)S(1)}, u32[]{:S(2)}, u32[]{:S(2)}) async-start(bf16[8,16,128]{2,1,0:T(8,128)(2,1)} %bitcast.9), calls=%async_computation.3 | async-start | bytes 65536 | tf_op jit(solution)/shard_map/all_to_all | solution.py:101
  339.5 1.5 fusion.25
  341.0 135.4 %reduce-scatter.3.cloned.1.call-done = f32[128,128]{1,0:T(8,128)} async-done(((f32[4096,128]{1,0:T(8,128)}), f32[128,128]{1,0:T(8,128)}) %reduce-scatter.3.cloned.1.call-update) | async-done | bytes 65552 | tf_op jit(solution)/shard_map/reduce_scatter | solution.py:94
  476.3 1.5 convert_element_type.64
  477.8 7.3 %all-to-all-start = ((bf16[8,16,128]{2,1,0:T(8,128)(2,1)}), bf16[8,16,128]{2,1,0:T(8,128)(2,1)S(1)}, u32[]{:S(2)}, u32[]{:S(2)}) async-start(bf16[8,16,128]{2,1,0:T(8,128)(2,1)} %bitcast.7), calls=%async_computation.1 | async-start | bytes 65536 | tf_op jit(solution)/shard_map/all_to_all | solution.py:98
  485.7 8.1 %all-to-all-done = bf16[8,16,128]{2,1,0:T(8,128)(2,1)S(1)} async-done(((bf16[8,16,128]{2,1,0:T(8,128)(2,1)}), bf16[8,16,128]{2,1,0:T(8,128)(2,1)S(1)}, u32[]{:S(2)}, u32[]{:S(2)}) %all-to-all-start) | async-done | bytes 32800 | tf_op jit(solution)/shard_map/all_to_all | solution.py:98
  (39 shorter events, 5.7 us)
Async XLA Ops:
  7.2 8.6 %copy-start.1 = (bf16[128,16,128]{2,1,0:T(8,128)(2,1)S(1)}, bf16[128,16,128]{2,1,0:T(8,128)(2,1)}, u32[]{:S(2)}) copy-start(bf16[128,16,128]{2,1,0:T(8,128)(2,1)} %param.10) | copy-start | bytes 1572868
  7.2 64.6 %all-gather.5.cloned.1.call-start = ((), (), s32[]{:S(2)}) async-start(), calls=%async_computation.6 | async-start | bytes 1081344 | tf_op jit(solution)/shard_map/all_gather | solution.py:35
  7.9 123.5 %all-gather.7.cloned.1.call-start = ((), (), s32[]{:S(2)}) async-start(), calls=%async_computation.7 | async-start | bytes 1081344 | tf_op jit(solution)/shard_map/all_gather | solution.py:36
  8.7 322.1 %reduce-scatter.5.cloned.1.call-start = ((), (), s32[]{:S(2)}) async-start(), calls=%async_computation.5 | async-start | bytes 2162688 | tf_op jit(solution)/shard_map/reduce_scatter | solution.py:95
  131.5 2.9 copy-start.2
  155.4 1.6 copy-start
  155.5 320.9 %reduce-scatter.3.cloned.1.call-start = ((), (), s32[]{:S(2)}) async-start(), calls=%async_computation.4 | async-start | bytes 2162688 | tf_op jit(solution)/shard_map/reduce_scatter | solution.py:94
  332.2 145.6 %all-to-all-start.1 = ((bf16[8,16,128]{2,1,0:T(8,128)(2,1)}), bf16[8,16,128]{2,1,0:T(8,128)(2,1)S(1)}, u32[]{:S(2)}, u32[]{:S(2)}) async-start(bf16[8,16,128]{2,1,0:T(8,128)(2,1)} %bitcast.9), calls=%async_computation.3 | async-start | bytes 65536 | tf_op jit(solution)/shard_map/all_to_all | solution.py:101
  477.8 16.0 %all-to-all-start = ((bf16[8,16,128]{2,1,0:T(8,128)(2,1)}), bf16[8,16,128]{2,1,0:T(8,128)(2,1)S(1)}, u32[]{:S(2)}, u32[]{:S(2)}) async-start(bf16[8,16,128]{2,1,0:T(8,128)(2,1)} %bitcast.7), calls=%async_computation.1 | async-start | bytes 65536 | tf_op jit(solution)/shard_map/all_to_all | solution.py:98
Sparse Core Ops, SparseCore 0:
  9.9 61.8 all-gather.4
  73.6 57.7 all-gather.6
  155.6 175.1 reduce-scatter.4
  333.3 143.0 reduce-scatter.2
where the time goes:
time: 504 us; the launch traced here: 501 us
  waiting for transfers between devices  430 us (85%)
  starting transfers between devices  14.8 us (3%)
  between operations  14.5 us (3%)
  matrix products  13.6 us (3%)
  other arithmetic  11.6 us (2%)
  local copies, waits for them, and re-layouts  10.3 us (2%)
  loops' own time  5.76 us (1%)
    reduce_scatter x1, waiting for transfers between devices, local(): lax.psum_scatter(grad_v, 'ctx', scatter_dimension=0, tiled=True)  172 us
    reduce_scatter x1, waiting for transfers between devices, local(): lax.psum_scatter(grad_k, 'ctx', scatter_dimension=0, tiled=True)  135 us
    all_gather x1, waiting for transfers between devices, local(): value_piece = lax.all_gather(value_local, 'ctx', axis=0, tiled=True)  59.7 us
    all_gather x1, waiting for transfers between devices, local(): key_piece = lax.all_gather(key_local, 'ctx', axis=0, tiled=True)  53.6 us
  transfers between devices with their start and end apart: 6, of which 5 were waited for; matrix products, arithmetic and copies ran while one was open for 3% of the time, Pallas kernels for 0%

commit v1 on v0

v1 whole, which is shorter than its diff:
```python
import functools

import jax
import jax.numpy as jnp
from jax import lax
from jax.experimental import pallas as pl
from jax.experimental.pallas import tpu as pltpu
from jax.sharding import Mesh
from jax.sharding import PartitionSpec as P

BLK = 128
WIN = 5
ZL, NY, NCORE, NX, ZH = 4, 4, 2, 4, 2
LOG2E = 1.4426950408889634


def attention_kernel(
    info, ends, q_ref, do_ref, stats_ref, kv0, kv1, kv2, kv3,
    dq_ref, p0_ref, p1_ref, p2_ref, p3_ref,
    win_ref, kt_ref, acc_ref,
    *, chunk, group,
):
    rows, dh = q_ref.shape
    scale = dh ** (-0.5)
    q_block = info[0]
    slots = (kv0, kv1, kv2, kv3)
    outs = (p0_ref, p1_ref, p2_ref, p3_ref)
    for w in range(WIN):
        slot = info[1 + w]
        for s in range(4):
            for i in range(2):
                @pl.when(slot == 2 * s + i)
                def _():
                    win_ref[w * BLK : (w + 1) * BLK, :] = slots[s][i]
    kt_ref[...] = win_ref[:, :dh].T
    acc_ref[...] = jnp.zeros_like(acc_ref)

    def step(c, carry):
        at = pl.multiple_of(c * chunk, chunk)
        q = q_ref[pl.ds(at, chunk), :]
        do = do_ref[pl.ds(at, chunk), :]
        lse = stats_ref[0:1, pl.ds(at, chunk)]
        delta = stats_ref[1:2, pl.ds(at, chunk)]
        pos = q_block * BLK + (at + lax.broadcasted_iota(jnp.int32, (1, chunk), 1)) // group
        start = jnp.zeros((1, chunk), jnp.int32)
        for k in range(ends.shape[0]):
            start = jnp.where(ends[k] <= pos, ends[k], start)
        key_pos = (q_block - (WIN - 1)) * BLK + lax.broadcasted_iota(
            jnp.int32, (WIN * BLK, chunk), 0
        )
        allowed = (key_pos >= start) & (key_pos <= pos)
        keys = win_ref[:, :dh]
        vals = win_ref[:, dh:]
        nt = (((1,), (1,)), ((), ()))
        s = lax.dot_general(keys, q, nt, preferred_element_type=jnp.float32)
        p = jnp.where(allowed, jnp.exp2(s * (scale * LOG2E) - lse), 0.0)
        dp = lax.dot_general(vals, do, nt, preferred_element_type=jnp.float32)
        ds = (p * (dp - delta)).astype(jnp.bfloat16)
        acc_ref[:, dh:] += jnp.dot(p.astype(jnp.bfloat16), do, preferred_element_type=jnp.float32)
        acc_ref[:, :dh] += jnp.dot(ds, q, preferred_element_type=jnp.float32)
        dqt = jnp.dot(kt_ref[...], ds, preferred_element_type=jnp.float32)
        dq_ref[pl.ds(at, chunk), :] = (dqt * scale).T.astype(dq_ref.dtype)
        return carry

    lax.fori_loop(0, rows // chunk, step, 0)
    acc_ref[:, :dh] = acc_ref[:, :dh] * scale
    for s in range(4):
        for i in range(2):
            w = info[6 + 2 * s + i]

            @pl.when(w >= 0)
            def _():
                at = pl.multiple_of(jnp.maximum(w, 0) * BLK, BLK)
                outs[s][i] = acc_ref[pl.ds(at, BLK), :].astype(outs[s].dtype)

            @pl.when(w < 0)
            def _():
                outs[s][i] = jnp.zeros((BLK, 2 * dh), outs[s].dtype)


def attention(info, ends, q, do, stats, kvs):
    rows, dh = q.shape
    part = (2, BLK, 2 * dh)
    smem = pl.BlockSpec(memory_space=pltpu.SMEM)
    vmem = pl.BlockSpec(memory_space=pltpu.VMEM)
    return pl.pallas_call(
        functools.partial(attention_kernel, chunk=256, group=rows // BLK),
        out_shape=(
            jax.ShapeDtypeStruct((rows, dh), jnp.bfloat16),
            jax.ShapeDtypeStruct(part, jnp.float32),
            jax.ShapeDtypeStruct(part, jnp.bfloat16),
            jax.ShapeDtypeStruct(part, jnp.bfloat16),
            jax.ShapeDtypeStruct(part, jnp.bfloat16),
        ),
        in_specs=[smem, smem] + [vmem] * 7,
        out_specs=(vmem,) * 5,
        scratch_shapes=[
            pltpu.VMEM((WIN * BLK, 2 * dh), jnp.bfloat16),
            pltpu.VMEM((dh, WIN * BLK), jnp.bfloat16),
            pltpu.VMEM((WIN * BLK, 2 * dh), jnp.float32),
        ],
        compiler_params=pltpu.CompilerParams(vmem_limit_bytes=40 * 1024 * 1024),
        cost_estimate=pl.CostEstimate(
            flops=10 * rows * WIN * BLK * dh, bytes_accessed=4 * rows * dh * 2, transcendentals=rows * WIN * BLK
        ),
        name="attention_backward",
    )(info, ends, q, do, stats, *kvs)


def swap(x, axis, size, mask):
    return lax.ppermute(x, axis, [(i, i ^ mask) for i in range(size)])


def local(queries, keys, values, outputs, out_grad, logsumexp, doc_lengths, block_order):
    rows, heads, dh = queries.shape
    zl = lax.axis_index("zl")
    y = lax.axis_index("y")
    core = lax.axis_index("core")
    ends = jnp.cumsum(doc_lengths).astype(jnp.int32)
    xor4 = jnp.arange(4, dtype=jnp.int32)

    own = jnp.concatenate([keys[:, 0, :], values[:, 0, :]], axis=1)
    column = jnp.stack([own] + [swap(own, "zl", ZL, m) for m in (1, 2, 3)])
    other = swap(column, "core", NCORE, 1)
    pairs = jnp.stack([column, other], axis=1)

    order = block_order.reshape(ZL, NY, NCORE)
    near = order[zl, y ^ xor4, core]
    first = jnp.maximum(near // 2 - 2, 0)
    want = jnp.minimum(first + (y - first) % 4, 15) // 4
    sends = [lax.dynamic_index_in_dim(pairs, zl ^ want[m], 0, keepdims=False) for m in range(4)]
    got = [sends[0]] + [swap(sends[m], "y", NY, m) for m in (1, 2, 3)]

    q_block = near[0]
    win = jnp.maximum(q_block - (WIN - 1) + jnp.arange(WIN, dtype=jnp.int32), 0)
    slot = (((win // 2) % 4) ^ y) * 2 + ((win % 2) ^ core)
    cls = y ^ xor4
    pair_of = first[0] + (cls - first[0]) % 4
    block_of = pair_of[:, None] * 2 + (core ^ jnp.arange(2, dtype=jnp.int32))[None, :]
    place = block_of - (q_block - (WIN - 1))
    usable = (place >= 0) & (place < WIN) & (block_of >= 0)
    place = jnp.where(usable, place, -1).reshape(-1)
    info = jnp.concatenate([q_block[None], slot, place]).astype(jnp.int32)

    delta = jnp.sum(out_grad.astype(jnp.float32) * outputs.astype(jnp.float32), axis=2)
    stats = jnp.stack([(logsumexp * LOG2E).T.reshape(-1), delta.reshape(-1)])
    grad_q, part0, part1, part2, part3 = attention(
        info, ends, queries.reshape(rows * heads, dh), out_grad.reshape(rows * heads, dh), stats, got
    )

    parts = [part0] + [swap(p, "y", NY, m) for m, p in ((1, part1), (2, part2), (3, part3))]
    total = sum(
        jnp.where((want[m] == xor4)[:, None, None, None], parts[m].astype(jnp.float32)[None], 0.0)
        for m in range(4)
    )
    theirs = swap(total[:, 1].astype(jnp.bfloat16), "core", NCORE, 1)
    mine = (total[:, 0] + theirs.astype(jnp.float32)).astype(jnp.bfloat16)
    kvh = NX * ZH
    share = BLK // kvh
    moved = lax.all_to_all(
        mine.reshape(ZL * kvh, share, 2 * dh), ("zl", "x", "zh"), split_axis=0, concat_axis=0, tiled=True
    )
    summed = jnp.sum(moved.reshape(ZL, kvh, share, 2 * dh).astype(jnp.float32), axis=0)
    grads = jnp.transpose(summed.astype(jnp.bfloat16), (1, 0, 2))
    grad_keys = grads[:, :, :dh].reshape(share, kvh * dh)
    grad_values = grads[:, :, dh:].reshape(share, kvh * dh)
    return grad_q.reshape(rows, heads, dh), grad_keys, grad_values


def solution(mesh):
    fine = Mesh(mesh.devices.reshape(ZL, NY, NCORE, NX, ZH), ("zl", "y", "core", "x", "zh"))
    ctx, kv = ("zl", "y", "core"), ("x", "zh")
    in_specs = (P(ctx, kv, None),) * 5 + (P(kv, ctx), P(), P())
    out_specs = (P(ctx, kv, None), P(ctx + kv, None), P(ctx + kv, None))
    return jax.shard_map(local, mesh=fine, in_specs=in_specs, out_specs=out_specs, check_vma=False)
```

time: 504 us -> 72.1 us (0.14)
  the two profiles are of different devices: /device:TPU:2 before, /device:TPU:32 now
where the time goes in v1:
time: 72.1 us; the launch traced here: 71.8 us
  blocking collectives  24.2 us (34%)
  starting transfers between devices  13.7 us (19%)
  waiting for transfers between devices  12.1 us (17%)
  Pallas kernels  7.3 us (10%)
  other arithmetic  6.63 us (9%)
  local copies, waits for them, and re-layouts  4.44 us (6%)
  between operations  3.45 us (5%)
    all_to_all x1, blocking collectives, local(): lax.all_to_all(mine.reshape(ZL * kvh, share, 2 * dh), ('zl', 'x', 'zh'),...  24.2 us
    ppermute x11, starting transfers between devices, swap(): return lax.ppermute(x, axis, [(i, i ^ mask) for i in range(size)])  13.7 us
    ppermute x11, waiting for transfers between devices, swap(): return lax.ppermute(x, axis, [(i, i ^ mask) for i in range(size)])  12.1 us
    pallas_call x1, Pallas kernels, attention(): pl.pallas_call(functools.partial(attention_kernel, chunk=256, group=rows...  7.3 us
    eq x2, other arithmetic, local(): want[m] == xor4  2.54 us
  transfers between devices with their start and end apart: 11, of which 7 were waited for; matrix products, arithmetic and copies ran while one was open for 11% of the time, Pallas kernels for 0%

profile of v1, /device:TPU:32, one launch (start us, length us, event | category | flops | bytes accessed | tf_op | source)
XLA Modules:
  0.0 71.8 jit_solution(14576863390940914686)
XLA Ops:
  0.6 0.8 %fusion.26 = (bf16[1,128,256]{2,1,0:T(8,128)(2,1)S(1)}, bf16[128,256]{1,0:T(8,128)(2,1)S(1)}) fusion(bf16[128,128]{1,0:T(8,128)(2,1)} %bitcast.68, bf16[128,128]{1,0:T(8,128)(2,1)} %bitcast.69), kind=kLoop, calls=%fused_computation.77 | loop fusion | flops 131072 | bytes 196608 | tf_op jit(solution)/shard_map/stack | solution.py:123
  1.5 3.4 %collective-permute-start.1 = (bf16[128,256]{1,0:T(8,128)(2,1)S(1)}, bf16[128,256]{1,0:T(8,128)(2,1)S(1)}, u32[]{:S(2)}, u32[]{:S(2)}) collective-permute-start(bf16[128,256]{1,0:T(8,128)(2,1)S(1)} %get-tuple-element.24), channel_id=1, source_target_pairs={{0,128},{64,192},{128,0},{192,64},{1,129},{65,193},{129,1},{193,65... | collective-permute-start | bytes 196616 | tf_op jit(solution)/shard_map/ppermute | solution.py:111
  4.8 0.1 collective-permute-start
  5.0 0.6 collective-permute-start.2
  5.5 0.7 multiply_bitcast_fusion
  6.2 0.7 %reshape.124 = s32[4,4,2]{2,1,0:T(4,128)S(1)} reshape(s32[32]{0:T(128)} %param.15) | data formatting | bytes 256 | tf_op jit(solution)/shard_map/reshape | solution.py:127
  7.0 0.7 gather_fusion
  8.1 1.4 %multiply_reduce_fusion = f32[128,16]{1,0:T(8,128)S(1)} fusion(bf16[128,16,128]{2,1,0:T(8,128)(2,1)} %param.11, bf16[128,16,128]{2,1,0:T(8,128)(2,1)S(1)} %copy-done), kind=kLoop, calls=%fused_computation.2 | loop fusion | flops 1046528 | bytes 1056768 | tf_op jit(solution)/shard_map/reduce_sum | solution.py:145
  9.5 0.4 collective-permute-done.2
  10.1 0.7 fusion.28
  13.7 3.1 %collective-permute-start.6 = (bf16[2,128,256]{2,1,0:T(8,128)(2,1)S(1)}, bf16[2,128,256]{2,1,0:T(8,128)(2,1)S(1)}, u32[]{:S(2)}, u32[]{:S(2)}) collective-permute-start(bf16[2,128,256]{2,1,0:T(8,128)(2,1)S(1)} %get-tuple-element.15), channel_id=1, source_target_pairs={{0,48},{16,32},{32,16},{48,0},{1,49},{17,33},{33,17},{49,1},{2,50}... | collective-permute-start | bytes 393224 | tf_op jit(solution)/shard_map/ppermute | solution.py:111
  16.8 0.1 collective-permute-start.4
  17.0 1.6 %collective-permute-start.5 = (bf16[2,128,256]{2,1,0:T(8,128)(2,1)S(1)}, bf16[2,128,256]{2,1,0:T(8,128)(2,1)S(1)}, u32[]{:S(2)}, u32[]{:S(2)}) collective-permute-start(bf16[2,128,256]{2,1,0:T(8,128)(2,1)S(1)} %get-tuple-element.18), channel_id=1, source_target_pairs={{0,32},{16,48},{32,0},{48,16},{1,33},{17,49},{33,1},{49,17},{2,34}... | collective-permute-start | bytes 393224 | tf_op jit(solution)/shard_map/ppermute | solution.py:111
  18.6 0.6 copy-done.2
  19.2 0.2 reduce-window.9
  19.4 0.1 pad_add_fusion.info
  19.5 1.5 %collective-permute-done.6.kv3 = bf16[2,128,256]{2,1,0:T(8,128)(2,1)S(1)} collective-permute-done((bf16[2,128,256]{2,1,0:T(8,128)(2,1)S(1)}, bf16[2,128,256]{2,1,0:T(8,128)(2,1)S(1)}, u32[]{:S(2)}, u32[]{:S(2)}) %collective-permute-start.6) | collective-permute-done | bytes 131104 | tf_op jit(solution)/shard_map/ppermute | solution.py:111
  21.0 2.2 %collective-permute-done.4.kv1 = bf16[2,128,256]{2,1,0:T(8,128)(2,1)S(1)} collective-permute-done((bf16[2,128,256]{2,1,0:T(8,128)(2,1)S(1)}, bf16[2,128,256]{2,1,0:T(8,128)(2,1)S(1)}, u32[]{:S(2)}, u32[]{:S(2)}) %collective-permute-start.4) | collective-permute-done | bytes 131104 | tf_op jit(solution)/shard_map/ppermute | solution.py:111
  23.2 1.9 %collective-permute-done.5.kv2 = bf16[2,128,256]{2,1,0:T(8,128)(2,1)S(1)} collective-permute-done((bf16[2,128,256]{2,1,0:T(8,128)(2,1)S(1)}, bf16[2,128,256]{2,1,0:T(8,128)(2,1)S(1)}, u32[]{:S(2)}, u32[]{:S(2)}) %collective-permute-start.5) | collective-permute-done | bytes 131104 | tf_op jit(solution)/shard_map/ppermute | solution.py:111
  25.1 7.3 %attention_backward.1 = (bf16[2048,128]{1,0:T(8,128)(2,1)}, f32[2,128,256]{2,1,0:T(8,128)S(1)}, bf16[2,128,256]{2,1,0:T(8,128)(2,1)S(1)}, bf16[2,128,256]{2,1,0:T(8,128)(2,1)S(1)}, bf16[2,128,256]{2,1,0:T(8,128)(2,1)S(1)}) custom-call(s32[14]{0:T(128)S(1)} %pad_add_fusion.info, s32[12]{0:T(128)S(1)} %bitcast.58, bf16[2048,128]{1,0:T(8,128)(2,1)S(1)} %bitcast.57, ...), custom_call_target="tpu_custom_call" | custom-call | flops 1677721600 | bytes 2097152 | tf_op jit(solution)/shard_map/attention_backward/pallas_call | solution.py:86
  32.4 0.6 collective-permute-start.7
  33.0 3.7 %collective-permute-start.8 = (bf16[2,128,256]{2,1,0:T(8,128)(2,1)S(1)}, bf16[2,128,256]{2,1,0:T(8,128)(2,1)S(1)}, u32[]{:S(2)}, u32[]{:S(2)}) collective-permute-start(bf16[2,128,256]{2,1,0:T(8,128)(2,1)S(1)} %get-tuple-element.11), channel_id=1, source_target_pairs={{0,32},{16,48},{32,0},{48,16},{1,33},{17,49},{33,1},{49,17},{2,34}... | collective-permute-start | bytes 393224 | tf_op jit(solution)/shard_map/ppermute | solution.py:111
  36.7 0.4 collective-permute-start.9
  37.1 1.3 %iota_compare_fusion = (pred[4]{0:T(512)(128)(4,1)S(1)}, pred[4]{0:T(512)(128)(4,1)S(1)}) fusion(s32[]{:T(128)} %bitcast.22, s32[]{:T(128)} %bitcast.20), kind=kLoop, calls=%fused_computation.71 | loop fusion | flops 8 | bytes 16 | tf_op jit(solution)/shard_map/eq | solution.py:153
  38.4 1.3 %iota_compare_fusion.2 = (pred[4]{0:T(512)(128)(4,1)S(1)}, pred[4]{0:T(512)(128)(4,1)S(1)}) fusion(s32[]{:T(128)} %bitcast.18, s32[]{:T(128)} %bitcast.16), kind=kLoop, calls=%fused_computation.73 | loop fusion | flops 8 | bytes 16 | tf_op jit(solution)/shard_map/eq | solution.py:153
  39.7 2.7 %collective-permute-done.8 = bf16[2,128,256]{2,1,0:T(8,128)(2,1)S(1)} collective-permute-done((bf16[2,128,256]{2,1,0:T(8,128)(2,1)S(1)}, bf16[2,128,256]{2,1,0:T(8,128)(2,1)S(1)}, u32[]{:S(2)}, u32[]{:S(2)}) %collective-permute-start.8) | collective-permute-done | bytes 131104 | tf_op jit(solution)/shard_map/ppermute | solution.py:111
  42.4 1.8 %collective-permute-done.9 = bf16[2,128,256]{2,1,0:T(8,128)(2,1)S(1)} collective-permute-done((bf16[2,128,256]{2,1,0:T(8,128)(2,1)S(1)}, bf16[2,128,256]{2,1,0:T(8,128)(2,1)S(1)}, u32[]{:S(2)}, u32[]{:S(2)}) %collective-permute-start.9) | collective-permute-done | bytes 131104 | tf_op jit(solution)/shard_map/ppermute | solution.py:111
  44.2 0.3 select_add_fusion
  44.7 1.5 %collective-permute-done.10 = bf16[4,128,256]{2,1,0:T(8,128)(2,1)S(1)} collective-permute-done((bf16[4,128,256]{2,1,0:T(8,128)(2,1)S(1)}, bf16[4,128,256]{2,1,0:T(8,128)(2,1)S(1)}, u32[]{:S(2)}, u32[]{:S(2)}) %collective-permute-start.10) | collective-permute-done | bytes 262176 | tf_op jit(solution)/shard_map/ppermute | solution.py:111
  46.3 24.2 %all_to_all.5 = bf16[32,16,256]{2,1,0:T(8,128)(2,1)S(1)} all-to-all(bf16[32,16,256]{2,1,0:T(8,128)(2,1)S(1)} %bitcast.60), channel_id=1, replica_groups=mesh['zl'=4,'y'=4,'core'=2,'x'=4,'zh'=2] {'zl','x','zh'}, dimensions={0} | all-to-all | bytes 524288 | tf_op jit(solution)/shard_map/all_to_all | solution.py:160
  70.5 0.6 copy.23
  71.2 0.6 copy.24
  (34 shorter events, 1.3 us)
Async XLA Ops:
  0.6 7.5 %copy-start = (bf16[128,16,128]{2,1,0:T(8,128)(2,1)S(1)}, bf16[128,16,128]{2,1,0:T(8,128)(2,1)}, u32[]{:S(2)}) copy-start(bf16[128,16,128]{2,1,0:T(8,128)(2,1)} %param.12) | copy-start | bytes 1572868
  1.5 8.0 %collective-permute-start.1 = (bf16[128,256]{1,0:T(8,128)(2,1)S(1)}, bf16[128,256]{1,0:T(8,128)(2,1)S(1)}, u32[]{:S(2)}, u32[]{:S(2)}) collective-permute-start(bf16[128,256]{1,0:T(8,128)(2,1)S(1)} %get-tuple-element.24), channel_id=1, source_target_pairs={{0,128},{64,192},{128,0},{192,64},{1,129},{65,193},{129,1},{193,65... | collective-permute-start | bytes 196616 | tf_op jit(solution)/shard_map/ppermute | solution.py:111
  4.8 4.7 %collective-permute-start = (bf16[128,256]{1,0:T(8,128)(2,1)S(1)}, bf16[128,256]{1,0:T(8,128)(2,1)S(1)}, u32[]{:S(2)}, u32[]{:S(2)}) collective-permute-start(bf16[128,256]{1,0:T(8,128)(2,1)S(1)} %get-tuple-element.24), channel_id=1, source_target_pairs={{0,64},{64,0},{128,192},{192,128},{1,65},{65,1},{129,193},{193,129... | collective-permute-start | bytes 196616 | tf_op jit(solution)/shard_map/ppermute | solution.py:111
  5.0 5.0 %collective-permute-start.2 = (bf16[128,256]{1,0:T(8,128)(2,1)S(1)}, bf16[128,256]{1,0:T(8,128)(2,1)S(1)}, u32[]{:S(2)}, u32[]{:S(2)}) collective-permute-start(bf16[128,256]{1,0:T(8,128)(2,1)S(1)} %get-tuple-element.24), channel_id=1, source_target_pairs={{0,192},{64,128},{128,64},{192,0},{1,193},{65,129},{129,65},{193,1... | collective-permute-start | bytes 196616 | tf_op jit(solution)/shard_map/ppermute | solution.py:111
  10.0 3.6 %collective-permute-start.3 = (bf16[4,128,256]{2,1,0:T(8,128)(2,1)S(1)}, bf16[4,128,256]{2,1,0:T(8,128)(2,1)S(1)}, u32[]{:S(2)}, u32[]{:S(2)}) collective-permute-start(bf16[4,128,256]{2,1,0:T(8,128)(2,1)S(1)} %get-tuple-element.19), channel_id=1, source_target_pairs={{0,8},{8,0},{1,9},{9,1},{2,10},{10,2},{3,11},{11,3},{4,12},{12,4},... | collective-permute-start | bytes 786440 | tf_op jit(solution)/shard_map/ppermute | solution.py:111
  13.7 11.4 %copy-start.1 = (bf16[128,16,128]{2,1,0:T(8,128)(2,1)S(1)}, bf16[128,16,128]{2,1,0:T(8,128)(2,1)}, u32[]{:S(2)}) copy-start(bf16[128,16,128]{2,1,0:T(8,128)(2,1)} %param.8) | copy-start | bytes 1572868
  13.7 7.3 %collective-permute-start.6 = (bf16[2,128,256]{2,1,0:T(8,128)(2,1)S(1)}, bf16[2,128,256]{2,1,0:T(8,128)(2,1)S(1)}, u32[]{:S(2)}, u32[]{:S(2)}) collective-permute-start(bf16[2,128,256]{2,1,0:T(8,128)(2,1)S(1)} %get-tuple-element.15), channel_id=1, source_target_pairs={{0,48},{16,32},{32,16},{48,0},{1,49},{17,33},{33,17},{49,1},{2,50}... | collective-permute-start | bytes 393224 | tf_op jit(solution)/shard_map/ppermute | solution.py:111
  16.8 6.3 %collective-permute-start.4 = (bf16[2,128,256]{2,1,0:T(8,128)(2,1)S(1)}, bf16[2,128,256]{2,1,0:T(8,128)(2,1)S(1)}, u32[]{:S(2)}, u32[]{:S(2)}) collective-permute-start(bf16[2,128,256]{2,1,0:T(8,128)(2,1)S(1)} %get-tuple-element.17), channel_id=1, source_target_pairs={{0,16},{16,0},{32,48},{48,32},{1,17},{17,1},{33,49},{49,33},{2,18}... | collective-permute-start | bytes 393224 | tf_op jit(solution)/shard_map/ppermute | solution.py:111
  17.0 8.1 %collective-permute-start.5 = (bf16[2,128,256]{2,1,0:T(8,128)(2,1)S(1)}, bf16[2,128,256]{2,1,0:T(8,128)(2,1)S(1)}, u32[]{:S(2)}, u32[]{:S(2)}) collective-permute-start(bf16[2,128,256]{2,1,0:T(8,128)(2,1)S(1)} %get-tuple-element.18), channel_id=1, source_target_pairs={{0,32},{16,48},{32,0},{48,16},{1,33},{17,49},{33,1},{49,17},{2,34}... | collective-permute-start | bytes 393224 | tf_op jit(solution)/shard_map/ppermute | solution.py:111
  18.6 0.7 copy-start.2
  32.4 7.3 %collective-permute-start.7 = (bf16[2,128,256]{2,1,0:T(8,128)(2,1)S(1)}, bf16[2,128,256]{2,1,0:T(8,128)(2,1)S(1)}, u32[]{:S(2)}, u32[]{:S(2)}) collective-permute-start(bf16[2,128,256]{2,1,0:T(8,128)(2,1)S(1)} %get-tuple-element.10), channel_id=1, source_target_pairs={{0,16},{16,0},{32,48},{48,32},{1,17},{17,1},{33,49},{49,33},{2,18}... | collective-permute-start | bytes 393224 | tf_op jit(solution)/shard_map/ppermute | solution.py:111
  33.0 9.4 %collective-permute-start.8 = (bf16[2,128,256]{2,1,0:T(8,128)(2,1)S(1)}, bf16[2,128,256]{2,1,0:T(8,128)(2,1)S(1)}, u32[]{:S(2)}, u32[]{:S(2)}) collective-permute-start(bf16[2,128,256]{2,1,0:T(8,128)(2,1)S(1)} %get-tuple-element.11), channel_id=1, source_target_pairs={{0,32},{16,48},{32,0},{48,16},{1,33},{17,49},{33,1},{49,17},{2,34}... | collective-permute-start | bytes 393224 | tf_op jit(solution)/shard_map/ppermute | solution.py:111
  36.7 7.5 %collective-permute-start.9 = (bf16[2,128,256]{2,1,0:T(8,128)(2,1)S(1)}, bf16[2,128,256]{2,1,0:T(8,128)(2,1)S(1)}, u32[]{:S(2)}, u32[]{:S(2)}) collective-permute-start(bf16[2,128,256]{2,1,0:T(8,128)(2,1)S(1)} %get-tuple-element.12), channel_id=1, source_target_pairs={{0,48},{16,32},{32,16},{48,0},{1,49},{17,33},{33,17},{49,1},{2,50}... | collective-permute-start | bytes 393224 | tf_op jit(solution)/shard_map/ppermute | solution.py:111
  44.6 1.6 %collective-permute-start.10 = (bf16[4,128,256]{2,1,0:T(8,128)(2,1)S(1)}, bf16[4,128,256]{2,1,0:T(8,128)(2,1)S(1)}, u32[]{:S(2)}, u32[]{:S(2)}) collective-permute-start(bf16[4,128,256]{2,1,0:T(8,128)(2,1)S(1)} %fusion.2), channel_id=1, source_target_pairs={{0,8},{8,0},{1,9},{9,1},{2,10},{10,2},{3,11},{11,3},{4,12},{12,4},... | collective-permute-start | bytes 786440 | tf_op jit(solution)/shard_map/ppermute | solution.py:111

commit v2 on v0

v2 whole, which is shorter than its diff:
```python
import functools

import jax
import jax.numpy as jnp
from jax import lax
from jax.experimental import pallas as pl
from jax.experimental.pallas import tpu as pltpu
from jax.sharding import Mesh
from jax.sharding import PartitionSpec as P

BLK = 128
WIN = 5
ZL, NY, NCORE, NX, ZH = 4, 4, 2, 4, 2
KVH = NX * ZH
LOG2E = 1.4426950408889634
CHUNK = 1024
LANES = 128
SEND, WANT, BASE0, BASE1, ACTIVE = 0, 4, 8, 12, 16
NT = (((1,), (1,)), ((), ()))
TN = (((0,), (0,)), ((), ()))
SMEM = pl.BlockSpec(memory_space=pltpu.SMEM)
VMEM = pl.BlockSpec(memory_space=pltpu.VMEM)


def call(body, outs, inputs, name, scratch=(), specs=None, flops=0, moved=1 << 18):
    return pl.pallas_call(
        body,
        out_shape=outs,
        in_specs=specs or [VMEM] * len(inputs),
        out_specs=jax.tree.map(lambda _: VMEM, outs),
        scratch_shapes=scratch,
        compiler_params=pltpu.CompilerParams(vmem_limit_bytes=16 * 1024 * 1024),
        cost_estimate=pl.CostEstimate(flops=flops, bytes_accessed=moved, transcendentals=0),
        name=name,
    )(*inputs)


def plan_kernel(order, lengths, plan_ref, span_ref, *, group):
    zl, y, core = lax.axis_index("zl"), lax.axis_index("y"), lax.axis_index("core")
    ends, total = [], 0
    for k in range(lengths.shape[0]):
        total = total + lengths[k]
        ends.append(total)

    def put(row, value):
        plan_ref[row : row + 1, :] = jnp.full((1, LANES), value, jnp.int32)

    me = order[(zl * NY + y) * NCORE + core]
    q_first = me * BLK
    doc_first = 0
    for end in ends:
        doc_first = jnp.where(end <= q_first, end, doc_first)
    mine = jnp.maximum(lax.shift_right_logical(me, 1) - 2, 0)
    for m in range(4):
        near = order[(zl * NY + (y ^ m)) * NCORE + core]
        first = jnp.maximum(lax.shift_right_logical(near, 1) - 2, 0)
        pair = jnp.minimum(first + ((y - first) & 3), 15)
        want = lax.shift_right_logical(pair, 2)
        put(SEND + m, zl ^ want)
        put(WANT + m, want)
        offset = ((y ^ m) - mine) & 3
        low = (mine + offset) * (2 * BLK)
        put(BASE0 + m, low + core * BLK)
        put(BASE1 + m, low + (1 - core) * BLK)
        active = (offset < 3) & (low < q_first + BLK) & (low + 2 * BLK > doc_first)
        put(ACTIVE + m, active.astype(jnp.int32))
    cols = span_ref.shape[1]
    pos = q_first + lax.broadcasted_iota(jnp.int32, (1, cols), 1) // group
    start = jnp.zeros((1, cols), jnp.int32)
    for end in ends:
        start = jnp.where(end <= pos, end, start)
    span_ref[0:1, :] = start
    span_ref[1:2, :] = pos


def select_kernel(plan, own, col1, col2, col3, theirs, *outs):
    mine = (own, col1, col2, col3)
    for m in range(4):
        at = jnp.concatenate([plan[SEND + m : SEND + m + 1, :]] * (own.shape[1] // LANES), axis=1)
        one, two = mine[0][...], theirs[0]
        for s in range(1, 4):
            one = jnp.where(at == s, mine[s][...], one)
            two = jnp.where(at == s, theirs[s], two)
        outs[m][:BLK, :] = one
        outs[m][BLK:, :] = two


def class_kernel(plan, q_ref, do_ref, stats, span, kv, part_ref, ds_ref, acc, *, m):
    rows, dh = q_ref.shape
    keys = kv.shape[0]
    scale = dh ** (-0.5)
    active = jnp.max(plan[ACTIVE + m : ACTIVE + m + 1, :]) > 0

    @pl.when(jnp.logical_not(active))
    def _():
        part_ref[...] = jnp.zeros_like(part_ref)

    @pl.when(active)
    def _():
        acc[...] = jnp.zeros_like(acc)
        row = lax.broadcasted_iota(jnp.int32, (BLK, 1), 0)
        key_pos = jnp.concatenate(
            [row + plan[BASE0 + m : BASE0 + m + 1, 0:1], row + plan[BASE1 + m : BASE1 + m + 1, 0:1]], axis=0
        )

        def step(c, carry):
            at = pl.multiple_of(c * CHUNK, CHUNK)
            cols = pl.ds(at, CHUNK)
            q = q_ref[cols, :]
            do = do_ref[cols, :]
            allowed = (key_pos >= span[0:1, cols]) & (key_pos <= span[1:2, cols])
            s = lax.dot_general(kv[:, :dh], q, NT, preferred_element_type=jnp.float32)
            p = jnp.where(allowed, jnp.exp2(s * (scale * LOG2E) - stats[0:1, cols]), 0.0)
            dp = lax.dot_general(kv[:, dh:], do, NT, preferred_element_type=jnp.float32)
            ds = (p * (dp - stats[1:2, cols])).astype(jnp.bfloat16)
            acc[:, dh:] += jnp.dot(p.astype(jnp.bfloat16), do, preferred_element_type=jnp.float32)
            acc[:, :dh] += jnp.dot(ds, q, preferred_element_type=jnp.float32)
            ds_ref[:, cols] = ds
            return carry

        lax.fori_loop(0, rows // CHUNK, step, 0)
        part_ref[:, :dh] = (acc[:, :dh] * scale).astype(part_ref.dtype)
        part_ref[:, dh:] = acc[:, dh:].astype(part_ref.dtype)


def query_kernel(plan, kv0, kv1, kv2, kv3, ds0, ds1, ds2, ds3, dq_ref, acc):
    rows, dh = dq_ref.shape
    acc[...] = jnp.zeros_like(acc)
    for m, (kv, ds) in enumerate(((kv0, ds0), (kv1, ds1), (kv2, ds2), (kv3, ds3))):

        @pl.when(jnp.max(plan[ACTIVE + m : ACTIVE + m + 1, :]) > 0)
        def _():
            def step(c, carry):
                cols = pl.ds(pl.multiple_of(c * CHUNK, CHUNK), CHUNK)
                acc[:, cols] += lax.dot_general(
                    kv[:, :dh], ds[:, cols], TN, preferred_element_type=jnp.float32
                )
                return carry

            lax.fori_loop(0, rows // CHUNK, step, 0)

    def finish(c, carry):
        cols = pl.ds(pl.multiple_of(c * CHUNK, CHUNK), CHUNK)
        dq_ref[cols, :] = (acc[:, cols] * dh ** (-0.5)).T.astype(dq_ref.dtype)
        return carry

    lax.fori_loop(0, rows // CHUNK, finish, 0)


def total_kernel(plan, part0, part1, part2, part3, keep_ref, send_ref):
    parts = (part0, part1, part2, part3)
    wide = part0.shape[1] // LANES
    wants = [jnp.concatenate([plan[WANT + m : WANT + m + 1, :]] * wide, axis=1) for m in range(4)]
    for z in range(ZL):
        keep = jnp.zeros((BLK, wide * LANES), jnp.float32)
        send = jnp.zeros((BLK, wide * LANES), jnp.float32)
        for m in range(4):
            here = wants[m] == z
            keep += jnp.where(here, parts[m][:BLK, :].astype(jnp.float32), 0.0)
            send += jnp.where(here, parts[m][BLK:, :].astype(jnp.float32), 0.0)
        keep_ref[z] = keep
        send_ref[z] = send.astype(send_ref.dtype)


def finish_kernel(moved, gk_ref, gv_ref):
    dh = moved.shape[2] // 2
    for k in range(KVH):
        grad = moved[k].astype(jnp.float32)
        for z in range(1, ZL):
            grad += moved[z * KVH + k].astype(jnp.float32)
        gk_ref[:, k * dh : (k + 1) * dh] = grad[:, :dh].astype(gk_ref.dtype)
        gv_ref[:, k * dh : (k + 1) * dh] = grad[:, dh:].astype(gv_ref.dtype)


def swap(x, axis, size, mask):
    return lax.ppermute(x, axis, [(i, i ^ mask) for i in range(size)])


def local(queries, keys, values, outputs, out_grad, logsumexp, doc_lengths, block_order):
    rows, heads, dh = queries.shape
    cols = rows * heads
    wide = 2 * dh
    bf16, f32 = jnp.bfloat16, jnp.float32
    shape = jax.ShapeDtypeStruct

    own = jnp.concatenate([keys[:, 0, :], values[:, 0, :]], axis=1)
    column = [own] + [swap(own, "zl", ZL, m) for m in (1, 2, 3)]
    plan, span = call(
        functools.partial(plan_kernel, group=heads),
        (shape((24, LANES), jnp.int32), shape((2, cols), jnp.int32)),
        (block_order, doc_lengths), "plan", specs=[SMEM, SMEM],
    )
    delta = jnp.sum(out_grad.astype(f32) * outputs.astype(f32), axis=2)
    stats = jnp.stack([(logsumexp * LOG2E).T.reshape(-1), delta.reshape(-1)])
    q = queries.reshape(cols, dh)
    do = out_grad.reshape(cols, dh)
    theirs = swap(jnp.stack(column), "core", NCORE, 1)

    pair = shape((2 * BLK, wide), bf16)
    sends = call(select_kernel, (pair,) * 4, (plan, *column, theirs), "select")
    kvs, parts, dss = [None] * 4, [None] * 4, [None] * 4
    kvs[0] = sends[0]
    for m in (1, 3, 2):
        kvs[m] = swap(sends[m], "y", NY, m)
    for m in (0, 1, 3, 2):
        parts[m], dss[m] = call(
            functools.partial(class_kernel, m=m),
            (shape((2 * BLK, wide), f32 if m == 0 else bf16), shape((2 * BLK, cols), bf16)),
            (plan, q, do, stats, span, kvs[m]), "class" + str(m),
            scratch=[pltpu.VMEM((2 * BLK, wide), f32)],
            flops=8 * cols * 2 * BLK * dh, moved=3 * cols * dh * 2,
        )
    back = [parts[0]] + [swap(parts[m], "y", NY, m) for m in (1, 2, 3)]
    grad_q = call(
        query_kernel, shape((cols, dh), bf16), (plan, *kvs, *dss), "query",
        scratch=[pltpu.VMEM((dh, cols), f32)], flops=8 * cols * 2 * BLK * dh, moved=8 * cols * dh * 2,
    )

    keep, send = call(
        total_kernel, (shape((ZL, BLK, wide), f32), shape((ZL, BLK, wide), bf16)), (plan, *back), "total"
    )
    mine = (keep + swap(send, "core", NCORE, 1).astype(f32)).astype(bf16)
    share = BLK // KVH
    moved = lax.all_to_all(
        mine.reshape(ZL * KVH, share, wide), ("zl", "x", "zh"), split_axis=0, concat_axis=0, tiled=True
    )
    out = shape((share, KVH * dh), bf16)
    grad_keys, grad_values = call(finish_kernel, (out, out), (moved,), "finish")
    return grad_q.reshape(rows, heads, dh), grad_keys, grad_values


def solution(mesh):
    fine = Mesh(mesh.devices.reshape(ZL, NY, NCORE, NX, ZH), ("zl", "y", "core", "x", "zh"))
    ctx, kv = ("zl", "y", "core"), ("x", "zh")
    in_specs = (P(ctx, kv, None),) * 5 + (P(kv, ctx), P(), P())
    out_specs = (P(ctx, kv, None), P(ctx + kv, None), P(ctx + kv, None))
    return jax.shard_map(local, mesh=fine, in_specs=in_specs, out_specs=out_specs, check_vma=False)
```

time: 504 us -> 67.6 us (0.13)
  the two profiles are of different devices: /device:TPU:2 before, /device:TPU:32 now
where the time goes in v2:
time: 67.6 us; the launch traced here: 67.4 us
  starting transfers between devices  25.9 us (38%)
  waiting for transfers between devices  22.4 us (33%)
  Pallas kernels  8.88 us (13%)
  local copies, waits for them, and re-layouts  6.22 us (9%)
  other arithmetic  3.08 us (5%)
  between operations  0.92 us (1%)
    ppermute x11, waiting for transfers between devices, swap(): return lax.ppermute(x, axis, [(i, i ^ mask) for i in range(size)])  16.3 us
    ppermute x11, starting transfers between devices, swap(): return lax.ppermute(x, axis, [(i, i ^ mask) for i in range(size)])  14.1 us
    all_to_all x1, starting transfers between devices, local(): lax.all_to_all(mine.reshape(ZL * KVH, share, wide), ('zl', 'x', 'zh'), sp...  11.9 us
    pallas_call x9, Pallas kernels, call(): pl.pallas_call(body, out_shape=outs, in_specs=specs or [VMEM] * len(input...  8.88 us
    all_to_all x1, waiting for transfers between devices, local(): lax.all_to_all(mine.reshape(ZL * KVH, share, wide), ('zl', 'x', 'zh'), sp...  6.09 us
    unnamed x30, local copies, waits for them, and re-layouts  5.94 us
    reduce_sum x1, other arithmetic, local(): delta = jnp.sum(out_grad.astype(f32) * outputs.astype(f32), axis=2)  1.39 us
  transfers between devices with their start and end apart: 12, of which 8 were waited for; matrix products, arithmetic and copies ran while one was open for 3% of the time, Pallas kernels for 11%

profile of v2, /device:TPU:32, one launch (start us, length us, event | category | flops | bytes accessed | tf_op | source)
XLA Modules:
  0.0 67.4 jit_solution(2897800583520636557)
XLA Ops:
  0.6 0.8 %fusion = (bf16[1,128,256]{2,1,0:T(8,128)(2,1)S(1)}, bf16[128,256]{1,0:T(8,128)(2,1)S(1)}) fusion(bf16[128,128]{1,0:T(8,128)(2,1)} %bitcast.26, bf16[128,128]{1,0:T(8,128)(2,1)} %bitcast.27), kind=kLoop, calls=%fused_computation.6 | loop fusion | flops 131072 | bytes 196608 | tf_op jit(solution)/shard_map/stack | solution.py:197
  1.5 2.0 %collective-permute-start.2 = (bf16[128,256]{1,0:T(8,128)(2,1)S(1)}, bf16[128,256]{1,0:T(8,128)(2,1)S(1)}, u32[]{:S(2)}, u32[]{:S(2)}) collective-permute-start(bf16[128,256]{1,0:T(8,128)(2,1)S(1)} %get-tuple-element.40.own), channel_id=1, source_target_pairs={{0,192},{64,128},{128,64},{192,0},{1,193},{65,129},{129,65},{193,1... | collective-permute-start | bytes 196616 | tf_op jit(solution)/shard_map/ppermute | solution.py:176
  3.5 2.3 %collective-permute-start.1 = (bf16[128,256]{1,0:T(8,128)(2,1)S(1)}, bf16[128,256]{1,0:T(8,128)(2,1)S(1)}, u32[]{:S(2)}, u32[]{:S(2)}) collective-permute-start(bf16[128,256]{1,0:T(8,128)(2,1)S(1)} %get-tuple-element.40.own), channel_id=1, source_target_pairs={{0,128},{64,192},{128,0},{192,64},{1,129},{65,193},{129,1},{193,65... | collective-permute-start | bytes 196616 | tf_op jit(solution)/shard_map/ppermute | solution.py:176
  5.8 0.5 collective-permute-start
  6.3 0.2 collective-permute-done.2.col3
  6.5 3.0 %collective-permute-done.1.col2 = bf16[128,256]{1,0:T(8,128)(2,1)S(1)} collective-permute-done((bf16[128,256]{1,0:T(8,128)(2,1)S(1)}, bf16[128,256]{1,0:T(8,128)(2,1)S(1)}, u32[]{:S(2)}, u32[]{:S(2)}) %collective-permute-start.1) | collective-permute-done | bytes 65568 | tf_op jit(solution)/shard_map/ppermute | solution.py:176
  9.5 1.4 %collective-permute-done.col1 = bf16[128,256]{1,0:T(8,128)(2,1)S(1)} collective-permute-done((bf16[128,256]{1,0:T(8,128)(2,1)S(1)}, bf16[128,256]{1,0:T(8,128)(2,1)S(1)}, u32[]{:S(2)}, u32[]{:S(2)}) %collective-permute-start) | collective-permute-done | bytes 65568 | tf_op jit(solution)/shard_map/ppermute | solution.py:176
  11.1 0.6 copy-done.14
  11.9 1.4 %multiply_reduce_fusion = f32[128,16]{1,0:T(8,128)S(1)} fusion(bf16[128,16,128]{2,1,0:T(8,128)(2,1)} %param.11, bf16[128,16,128]{2,1,0:T(8,128)(2,1)S(1)} %copy-done.2), kind=kLoop, calls=%fused_computation | loop fusion | flops 1046528 | bytes 1056768 | tf_op jit(solution)/shard_map/reduce_sum | solution.py:193
  13.4 0.6 plan.1
  14.2 1.7 %collective-permute-start.4 = (bf16[256,256]{1,0:T(8,128)(2,1)S(1)}, bf16[256,256]{1,0:T(8,128)(2,1)S(1)}, u32[]{:S(2)}, u32[]{:S(2)}) collective-permute-start(bf16[256,256]{1,0:T(8,128)(2,1)S(1)} %get-tuple-element.23), channel_id=1, source_target_pairs={{0,16},{16,0},{32,48},{48,32},{1,17},{17,1},{33,49},{49,33},{2,18}... | collective-permute-start | bytes 393224 | tf_op jit(solution)/shard_map/ppermute | solution.py:176
  15.9 2.9 %collective-permute-start.5 = (bf16[256,256]{1,0:T(8,128)(2,1)S(1)}, bf16[256,256]{1,0:T(8,128)(2,1)S(1)}, u32[]{:S(2)}, u32[]{:S(2)}) collective-permute-start(bf16[256,256]{1,0:T(8,128)(2,1)S(1)} %get-tuple-element.24), channel_id=1, source_target_pairs={{0,32},{16,48},{32,0},{48,16},{1,33},{17,49},{33,1},{49,17},{2,34}... | collective-permute-start | bytes 393224 | tf_op jit(solution)/shard_map/ppermute | solution.py:176
  18.8 0.2 collective-permute-start.6
  19.0 8.1 %collective-permute-done.6.kv.kv3 = bf16[256,256]{1,0:T(8,128)(2,1)S(1)} collective-permute-done((bf16[256,256]{1,0:T(8,128)(2,1)S(1)}, bf16[256,256]{1,0:T(8,128)(2,1)S(1)}, u32[]{:S(2)}, u32[]{:S(2)}) %collective-permute-start.6) | collective-permute-done | bytes 131104 | tf_op jit(solution)/shard_map/ppermute | solution.py:176
  27.1 1.9 %class3.1 = (bf16[256,256]{1,0:T(8,128)(2,1)S(1)}, bf16[256,2048]{1,0:T(8,128)(2,1)S(1)}) custom-call(s32[24,128]{1,0:T(8,128)S(1)} %get-tuple-element.21.plan, bf16[2048,128]{1,0:T(8,128)(2,1)S(1)} %bitcast.20, bf16[2048,128]{1,0:T(8,128)(2,1)S(1)} %bitcast.13, f32[2,2048]{1,0:T(2,128)S(1)} %pad_maximum_fusion.2.stats, ...), custom_call_target="tpu_custom_call" | custom-call | flops 536870912 | bytes 1572864 | tf_op jit(solution)/shard_map/class3/pallas_call | solution.py:26
  29.2 1.9 %class2.1 = (bf16[256,256]{1,0:T(8,128)(2,1)S(1)}, bf16[256,2048]{1,0:T(8,128)(2,1)S(1)}) custom-call(s32[24,128]{1,0:T(8,128)S(1)} %get-tuple-element.21.plan, bf16[2048,128]{1,0:T(8,128)(2,1)S(1)} %bitcast.21, bf16[2048,128]{1,0:T(8,128)(2,1)S(1)} %bitcast.14, f32[2,2048]{1,0:T(2,128)S(1)} %pad_maximum_fusion.2.stats, ...), custom_call_target="tpu_custom_call" | custom-call | flops 536870912 | bytes 1572864 | tf_op jit(solution)/shard_map/class2/pallas_call | solution.py:26
  31.5 0.4 copy-done.4
  31.9 4.1 %collective-permute-start.7 = (bf16[256,256]{1,0:T(8,128)(2,1)S(1)}, bf16[256,256]{1,0:T(8,128)(2,1)S(1)}, u32[]{:S(2)}, u32[]{:S(2)}) collective-permute-start(bf16[256,256]{1,0:T(8,128)(2,1)S(1)} %get-tuple-element.32), channel_id=1, source_target_pairs={{0,16},{16,0},{32,48},{48,32},{1,17},{17,1},{33,49},{49,33},{2,18}... | collective-permute-start | bytes 393224 | tf_op jit(solution)/shard_map/ppermute | solution.py:176
  36.2 1.0 %copy-done = bf16[256,2048]{1,0:T(8,128)(2,1)} copy-done((bf16[256,2048]{1,0:T(8,128)(2,1)}, bf16[256,2048]{1,0:T(8,128)(2,1)S(1)}, u32[]{:S(2)}) %copy-start) | copy-done | bytes 1048600
  37.2 1.5 %collective-permute-done.8.part2 = bf16[256,256]{1,0:T(8,128)(2,1)S(1)} collective-permute-done((bf16[256,256]{1,0:T(8,128)(2,1)S(1)}, bf16[256,256]{1,0:T(8,128)(2,1)S(1)}, u32[]{:S(2)}, u32[]{:S(2)}) %collective-permute-start.8) | collective-permute-done | bytes 131104 | tf_op jit(solution)/shard_map/ppermute | solution.py:176
  38.7 0.4 collective-permute-done.7.part1
  39.2 0.4 total.1
  39.6 1.5 %collective-permute-done.10 = bf16[4,128,256]{2,1,0:T(8,128)(2,1)S(1)} collective-permute-done((bf16[4,128,256]{2,1,0:T(8,128)(2,1)S(1)}, bf16[4,128,256]{2,1,0:T(8,128)(2,1)S(1)}, u32[]{:S(2)}, u32[]{:S(2)}) %collective-permute-start.10) | collective-permute-done | bytes 262176 | tf_op jit(solution)/shard_map/ppermute | solution.py:176
  41.1 0.8 %add_convert_fusion = bf16[4,128,256]{2,1,0:T(8,128)(2,1)} fusion(f32[4,128,256]{2,1,0:T(8,128)S(1)} %get-tuple-element.35, bf16[4,128,256]{2,1,0:T(8,128)(2,1)S(1)} %collective-permute-done.10), kind=kLoop, calls=%fused_computation.1 | loop fusion | flops 393216 | bytes 1048576 | tf_op jit(solution)/shard_map/convert_element_type | solution.py:222
  41.9 11.9 %all-to-all-start = ((bf16[32,16,256]{2,1,0:T(8,128)(2,1)}), bf16[32,16,256]{2,1,0:T(8,128)(2,1)S(1)}, u32[]{:S(2)}, u32[]{:S(2)}) async-start(bf16[32,16,256]{2,1,0:T(8,128)(2,1)} %bitcast.24), calls=%async_computation | async-start | bytes 524288 | tf_op jit(solution)/shard_map/all_to_all | solution.py:224
  53.8 1.2 %copy-done.1 = bf16[256,2048]{1,0:T(8,128)(2,1)S(1)} copy-done((bf16[256,2048]{1,0:T(8,128)(2,1)S(1)}, bf16[256,2048]{1,0:T(8,128)(2,1)}, u32[]{:S(2)}) %copy-start.1) | copy-done | bytes 1048600
  55.0 0.9 %copy-done.5 = bf16[256,256]{1,0:T(8,128)(2,1)S(1)} copy-done((bf16[256,256]{1,0:T(8,128)(2,1)S(1)}, bf16[256,256]{1,0:T(8,128)(2,1)}, u32[]{:S(2)}) %copy-start.5) | copy-done | bytes 131096
  55.9 0.9 %copy-done.7 = bf16[256,256]{1,0:T(8,128)(2,1)S(1)} copy-done((bf16[256,256]{1,0:T(8,128)(2,1)S(1)}, bf16[256,256]{1,0:T(8,128)(2,1)}, u32[]{:S(2)}) %copy-start.7) | copy-done | bytes 131096
  56.8 0.9 %copy-done.9 = bf16[256,256]{1,0:T(8,128)(2,1)S(1)} copy-done((bf16[256,256]{1,0:T(8,128)(2,1)S(1)}, bf16[256,256]{1,0:T(8,128)(2,1)}, u32[]{:S(2)}) %copy-start.9) | copy-done | bytes 131096
  57.7 2.9 %query.1 = bf16[2048,128]{1,0:T(8,128)(2,1)} custom-call(s32[24,128]{1,0:T(8,128)S(1)} %get-tuple-element.21.plan, bf16[256,256]{1,0:T(8,128)(2,1)S(1)} %get-tuple-element.22.kv.kv0, bf16[256,256]{1,0:T(8,128)(2,1)S(1)} %copy-done.5, bf16[256,256]{1,0:T(8,128)(2,1)S(1)} %copy-done.7, bf16[256,256]{1,0:T(8,128)(2,1)S(1)} %copy-done.9, ...), custom_call_target="tpu_custom_call" | custom-call | flops 536870912 | bytes 4194304 | tf_op jit(solution)/shard_map/query/pallas_call | solution.py:26
  60.6 6.1 %all-to-all-done.moved = bf16[32,16,256]{2,1,0:T(8,128)(2,1)S(1)} async-done(((bf16[32,16,256]{2,1,0:T(8,128)(2,1)}), bf16[32,16,256]{2,1,0:T(8,128)(2,1)S(1)}, u32[]{:S(2)}, u32[]{:S(2)}) %all-to-all-start) | async-done | bytes 262176 | tf_op jit(solution)/shard_map/all_to_all | solution.py:224
  66.7 0.7 finish.1
  (40 shorter events, 1.3 us)
Async XLA Ops:
  0.6 11.2 %copy-start.2 = (bf16[128,16,128]{2,1,0:T(8,128)(2,1)S(1)}, bf16[128,16,128]{2,1,0:T(8,128)(2,1)}, u32[]{:S(2)}) copy-start(bf16[128,16,128]{2,1,0:T(8,128)(2,1)} %param.12) | copy-start | bytes 1572868
  1.5 5.1 %collective-permute-start.2 = (bf16[128,256]{1,0:T(8,128)(2,1)S(1)}, bf16[128,256]{1,0:T(8,128)(2,1)S(1)}, u32[]{:S(2)}, u32[]{:S(2)}) collective-permute-start(bf16[128,256]{1,0:T(8,128)(2,1)S(1)} %get-tuple-element.40.own), channel_id=1, source_target_pairs={{0,192},{64,128},{128,64},{192,0},{1,193},{65,129},{129,65},{193,1... | collective-permute-start | bytes 196616 | tf_op jit(solution)/shard_map/ppermute | solution.py:176
  3.5 6.0 %collective-permute-start.1 = (bf16[128,256]{1,0:T(8,128)(2,1)S(1)}, bf16[128,256]{1,0:T(8,128)(2,1)S(1)}, u32[]{:S(2)}, u32[]{:S(2)}) collective-permute-start(bf16[128,256]{1,0:T(8,128)(2,1)S(1)} %get-tuple-element.40.own), channel_id=1, source_target_pairs={{0,128},{64,192},{128,0},{192,64},{1,129},{65,193},{129,1},{193,65... | collective-permute-start | bytes 196616 | tf_op jit(solution)/shard_map/ppermute | solution.py:176
  5.8 5.2 %collective-permute-start = (bf16[128,256]{1,0:T(8,128)(2,1)S(1)}, bf16[128,256]{1,0:T(8,128)(2,1)S(1)}, u32[]{:S(2)}, u32[]{:S(2)}) collective-permute-start(bf16[128,256]{1,0:T(8,128)(2,1)S(1)} %get-tuple-element.40.own), channel_id=1, source_target_pairs={{0,64},{64,0},{128,192},{192,128},{1,65},{65,1},{129,193},{193,129... | collective-permute-start | bytes 196616 | tf_op jit(solution)/shard_map/ppermute | solution.py:176
  11.0 0.7 %copy-start.14 = (f32[16,128]{1,0:T(8,128)S(1)}, f32[16,128]{1,0:T(8,128)}, u32[]{:S(2)}) copy-start(f32[16,128]{1,0:T(8,128)} %param.13) | copy-start | bytes 24580
  11.0 3.1 %collective-permute-start.3 = (bf16[4,128,256]{2,1,0:T(8,128)(2,1)S(1)}, bf16[4,128,256]{2,1,0:T(8,128)(2,1)S(1)}, u32[]{:S(2)}, u32[]{:S(2)}) collective-permute-start(bf16[4,128,256]{2,1,0:T(8,128)(2,1)S(1)} %pad_maximum_fusion), channel_id=1, source_target_pairs={{0,8},{8,0},{1,9},{9,1},{2,10},{10,2},{3,11},{11,3},{4,12},{12,4},... | collective-permute-start | bytes 786440 | tf_op jit(solution)/shard_map/ppermute | solution.py:176
  11.9 1.5 %copy-start.12 = (s32[32]{0:T(128)S(1)}, s32[32]{0:T(128)}, u32[]{:S(2)}) copy-start(s32[32]{0:T(128)} %order.1) | copy-start | bytes 388
  11.9 1.5 %copy-start.13 = (s32[12]{0:T(128)S(1)}, s32[12]{0:T(128)}, u32[]{:S(2)}) copy-start(s32[12]{0:T(128)} %lengths.1) | copy-start | bytes 148
  13.3 13.8 %copy-start.10 = (bf16[128,16,128]{2,1,0:T(8,128)(2,1)S(1)}, bf16[128,16,128]{2,1,0:T(8,128)(2,1)}, u32[]{:S(2)}) copy-start(bf16[128,16,128]{2,1,0:T(8,128)(2,1)} %param.8) | copy-start | bytes 1572868
  14.2 17.0 %collective-permute-start.4 = (bf16[256,256]{1,0:T(8,128)(2,1)S(1)}, bf16[256,256]{1,0:T(8,128)(2,1)S(1)}, u32[]{:S(2)}, u32[]{:S(2)}) collective-permute-start(bf16[256,256]{1,0:T(8,128)(2,1)S(1)} %get-tuple-element.23), channel_id=1, source_target_pairs={{0,16},{16,0},{32,48},{48,32},{1,17},{17,1},{33,49},{49,33},{2,18}... | collective-permute-start | bytes 393224 | tf_op jit(solution)/shard_map/ppermute | solution.py:176
  15.9 13.3 %collective-permute-start.5 = (bf16[256,256]{1,0:T(8,128)(2,1)S(1)}, bf16[256,256]{1,0:T(8,128)(2,1)S(1)}, u32[]{:S(2)}, u32[]{:S(2)}) collective-permute-start(bf16[256,256]{1,0:T(8,128)(2,1)S(1)} %get-tuple-element.24), channel_id=1, source_target_pairs={{0,32},{16,48},{32,0},{48,16},{1,33},{17,49},{33,1},{49,17},{2,34}... | collective-permute-start | bytes 393224 | tf_op jit(solution)/shard_map/ppermute | solution.py:176
  18.8 8.4 %collective-permute-start.6 = (bf16[256,256]{1,0:T(8,128)(2,1)S(1)}, bf16[256,256]{1,0:T(8,128)(2,1)S(1)}, u32[]{:S(2)}, u32[]{:S(2)}) collective-permute-start(bf16[256,256]{1,0:T(8,128)(2,1)S(1)} %get-tuple-element.25), channel_id=1, source_target_pairs={{0,48},{16,32},{32,16},{48,0},{1,49},{17,33},{33,17},{49,1},{2,50}... | collective-permute-start | bytes 393224 | tf_op jit(solution)/shard_map/ppermute | solution.py:176
  27.1 1.9 %copy-start.8 = (bf16[256,256]{1,0:T(8,128)(2,1)}, bf16[256,256]{1,0:T(8,128)(2,1)S(1)}, u32[]{:S(2)}) copy-start(bf16[256,256]{1,0:T(8,128)(2,1)S(1)} %collective-permute-done.6.kv.kv3) | copy-start | bytes 393220
  29.0 2.2 %copy-start.3 = (bf16[128,16,128]{2,1,0:T(8,128)(2,1)S(1)}, bf16[128,16,128]{2,1,0:T(8,128)(2,1)}, u32[]{:S(2)}) copy-start(bf16[128,16,128]{2,1,0:T(8,128)(2,1)} %param.12) | copy-start | bytes 1572868
  29.0 2.2 %copy-start.11 = (bf16[128,16,128]{2,1,0:T(8,128)(2,1)S(1)}, bf16[128,16,128]{2,1,0:T(8,128)(2,1)}, u32[]{:S(2)}) copy-start(bf16[128,16,128]{2,1,0:T(8,128)(2,1)} %param.8) | copy-start | bytes 1572868
  29.1 8.1 %collective-permute-start.9 = (bf16[256,256]{1,0:T(8,128)(2,1)S(1)}, bf16[256,256]{1,0:T(8,128)(2,1)S(1)}, u32[]{:S(2)}, u32[]{:S(2)}) collective-permute-start(bf16[256,256]{1,0:T(8,128)(2,1)S(1)} %get-tuple-element.34), channel_id=1, source_target_pairs={{0,48},{16,32},{32,16},{48,0},{1,49},{17,33},{33,17},{49,1},{2,50}... | collective-permute-start | bytes 393224 | tf_op jit(solution)/shard_map/ppermute | solution.py:176
  29.2 1.9 %copy-start.6 = (bf16[256,256]{1,0:T(8,128)(2,1)}, bf16[256,256]{1,0:T(8,128)(2,1)S(1)}, u32[]{:S(2)}) copy-start(bf16[256,256]{1,0:T(8,128)(2,1)S(1)} %collective-permute-done.5.kv.kv2) | copy-start | bytes 393220
  31.1 7.6 %collective-permute-start.8 = (bf16[256,256]{1,0:T(8,128)(2,1)S(1)}, bf16[256,256]{1,0:T(8,128)(2,1)S(1)}, u32[]{:S(2)}, u32[]{:S(2)}) collective-permute-start(bf16[256,256]{1,0:T(8,128)(2,1)S(1)} %get-tuple-element.33), channel_id=1, source_target_pairs={{0,32},{16,48},{32,0},{48,16},{1,33},{17,49},{33,1},{49,17},{2,34}... | collective-permute-start | bytes 393224 | tf_op jit(solution)/shard_map/ppermute | solution.py:176
  31.2 0.7 copy-start.4
  31.9 7.3 %collective-permute-start.7 = (bf16[256,256]{1,0:T(8,128)(2,1)S(1)}, bf16[256,256]{1,0:T(8,128)(2,1)S(1)}, u32[]{:S(2)}, u32[]{:S(2)}) collective-permute-start(bf16[256,256]{1,0:T(8,128)(2,1)S(1)} %get-tuple-element.32), channel_id=1, source_target_pairs={{0,16},{16,0},{32,48},{48,32},{1,17},{17,1},{33,49},{49,33},{2,18}... | collective-permute-start | bytes 393224 | tf_op jit(solution)/shard_map/ppermute | solution.py:176
  36.2 1.0 %copy-start = (bf16[256,2048]{1,0:T(8,128)(2,1)}, bf16[256,2048]{1,0:T(8,128)(2,1)S(1)}, u32[]{:S(2)}) copy-start(bf16[256,2048]{1,0:T(8,128)(2,1)S(1)} %get-tuple-element.27.ds0) | copy-start | bytes 3145732
  39.5 1.6 %collective-permute-start.10 = (bf16[4,128,256]{2,1,0:T(8,128)(2,1)S(1)}, bf16[4,128,256]{2,1,0:T(8,128)(2,1)S(1)}, u32[]{:S(2)}, u32[]{:S(2)}) collective-permute-start(bf16[4,128,256]{2,1,0:T(8,128)(2,1)S(1)} %get-tuple-element.36), channel_id=1, source_target_pairs={{0,8},{8,0},{1,9},{9,1},{2,10},{10,2},{3,11},{11,3},{4,12},{12,4},... | collective-permute-start | bytes 786440 | tf_op jit(solution)/shard_map/ppermute | solution.py:176
  41.9 24.8 %all-to-all-start = ((bf16[32,16,256]{2,1,0:T(8,128)(2,1)}), bf16[32,16,256]{2,1,0:T(8,128)(2,1)S(1)}, u32[]{:S(2)}, u32[]{:S(2)}) async-start(bf16[32,16,256]{2,1,0:T(8,128)(2,1)} %bitcast.24), calls=%async_computation | async-start | bytes 524288 | tf_op jit(solution)/shard_map/all_to_all | solution.py:224
  53.8 1.2 %copy-start.1 = (bf16[256,2048]{1,0:T(8,128)(2,1)S(1)}, bf16[256,2048]{1,0:T(8,128)(2,1)}, u32[]{:S(2)}) copy-start(bf16[256,2048]{1,0:T(8,128)(2,1)} %copy-done) | copy-start | bytes 3145732
  55.0 0.9 %copy-start.5 = (bf16[256,256]{1,0:T(8,128)(2,1)S(1)}, bf16[256,256]{1,0:T(8,128)(2,1)}, u32[]{:S(2)}) copy-start(bf16[256,256]{1,0:T(8,128)(2,1)} %copy-done.4) | copy-start | bytes 393220
  55.9 0.9 %copy-start.7 = (bf16[256,256]{1,0:T(8,128)(2,1)S(1)}, bf16[256,256]{1,0:T(8,128)(2,1)}, u32[]{:S(2)}) copy-start(bf16[256,256]{1,0:T(8,128)(2,1)} %copy-done.6) | copy-start | bytes 393220
  56.8 0.9 %copy-start.9 = (bf16[256,256]{1,0:T(8,128)(2,1)S(1)}, bf16[256,256]{1,0:T(8,128)(2,1)}, u32[]{:S(2)}) copy-start(bf16[256,256]{1,0:T(8,128)(2,1)} %copy-done.8) | copy-start | bytes 393220

commit v3 on v2

--- a/solution.py
+++ b/solution.py
@@ -73,6 +73,16 @@
     span_ref[1:2, :] = pos
 
 
+def stack_kernel(own, col1, col2, col3, plan, span, stats, out, token):
+    for s, ref in enumerate((own, col1, col2, col3)):
+        out[s] = ref[...]
+    token[...] = jnp.zeros_like(token)
+
+
+def add_kernel(keep, theirs, out):
+    out[...] = (keep[...] + theirs[...].astype(jnp.float32)).astype(out.dtype)
+
+
 def select_kernel(plan, own, col1, col2, col3, theirs, *outs):
     mine = (own, col1, col2, col3)
     for m in range(4):
@@ -85,11 +95,12 @@
         outs[m][BLK:, :] = two
 
 
-def class_kernel(plan, q_ref, do_ref, stats, span, kv, part_ref, ds_ref, acc, *, m):
+def class_kernel(plan, q_ref, do_ref, stats, span, kv, before, part_ref, ds_ref, after, acc, *, m):
     rows, dh = q_ref.shape
     keys = kv.shape[0]
     scale = dh ** (-0.5)
     active = jnp.max(plan[ACTIVE + m : ACTIVE + m + 1, :]) > 0
+    after[...] = before[...]
 
     @pl.when(jnp.logical_not(active))
     def _():
@@ -123,8 +134,9 @@
         part_ref[:, dh:] = acc[:, dh:].astype(part_ref.dtype)
 
 
-def query_kernel(plan, kv0, kv1, kv2, kv3, ds0, ds1, ds2, ds3, dq_ref, acc):
+def query_kernel(plan, kv0, kv1, kv2, kv3, ds0, ds1, ds2, ds3, before, dq_ref, after, acc):
     rows, dh = dq_ref.shape
+    after[...] = before[...]
     acc[...] = jnp.zeros_like(acc)
     for m, (kv, ds) in enumerate(((kv0, ds0), (kv1, ds1), (kv2, ds2), (kv3, ds3))):
 
@@ -147,7 +159,7 @@
     lax.fori_loop(0, rows // CHUNK, finish, 0)
 
 
-def total_kernel(plan, part0, part1, part2, part3, keep_ref, send_ref):
+def total_kernel(plan, part0, part1, part2, part3, before, keep_ref, send_ref):
     parts = (part0, part1, part2, part3)
     wide = part0.shape[1] // LANES
     wants = [jnp.concatenate([plan[WANT + m : WANT + m + 1, :]] * wide, axis=1) for m in range(4)]
@@ -194,32 +206,36 @@
     stats = jnp.stack([(logsumexp * LOG2E).T.reshape(-1), delta.reshape(-1)])
     q = queries.reshape(cols, dh)
     do = out_grad.reshape(cols, dh)
-    theirs = swap(jnp.stack(column), "core", NCORE, 1)
+    stacked, token = call(
+        stack_kernel, (shape((4, BLK, wide), bf16), shape((8, LANES), f32)),
+        (*column, plan, span, stats), "stacked",
+    )
+    theirs = swap(stacked, "core", NCORE, 1)
 
     pair = shape((2 * BLK, wide), bf16)
     sends = call(select_kernel, (pair,) * 4, (plan, *column, theirs), "select")
-    kvs, parts, dss = [None] * 4, [None] * 4, [None] * 4
-    kvs[0] = sends[0]
-    for m in (1, 3, 2):
-        kvs[m] = swap(sends[m], "y", NY, m)
-    for m in (0, 1, 3, 2):
-        parts[m], dss[m] = call(
+    kvs = [sends[0]] + [swap(sends[m], "y", NY, m) for m in (1, 2, 3)]
+    parts, dss = [], []
+    for m in range(4):
+        part, ds, token = call(
             functools.partial(class_kernel, m=m),
-            (shape((2 * BLK, wide), f32 if m == 0 else bf16), shape((2 * BLK, cols), bf16)),
-            (plan, q, do, stats, span, kvs[m]), "class" + str(m),
+            (shape((2 * BLK, wide), f32 if m == 0 else bf16), shape((2 * BLK, cols), bf16), shape((8, LANES), f32)),
+            (plan, q, do, stats, span, kvs[m], token), "class" + str(m),
             scratch=[pltpu.VMEM((2 * BLK, wide), f32)],
             flops=8 * cols * 2 * BLK * dh, moved=3 * cols * dh * 2,
         )
+        parts.append(part)
+        dss.append(ds)
     back = [parts[0]] + [swap(parts[m], "y", NY, m) for m in (1, 2, 3)]
-    grad_q = call(
-        query_kernel, shape((cols, dh), bf16), (plan, *kvs, *dss), "query",
+    grad_q, token = call(
+        query_kernel, (shape((cols, dh), bf16), shape((8, LANES), f32)), (plan, *kvs, *dss, token), "query",
         scratch=[pltpu.VMEM((dh, cols), f32)], flops=8 * cols * 2 * BLK * dh, moved=8 * cols * dh * 2,
     )
 
     keep, send = call(
-        total_kernel, (shape((ZL, BLK, wide), f32), shape((ZL, BLK, wide), bf16)), (plan, *back), "total"
-    )
-    mine = (keep + swap(send, "core", NCORE, 1).astype(f32)).astype(bf16)
+        total_kernel, (shape((ZL, BLK, wide), f32), shape((ZL, BLK, wide), bf16)), (plan, *back, token), "total"
+    )
+    mine = call(add_kernel, shape((ZL, BLK, wide), bf16), (keep, swap(send, "core", NCORE, 1)), "add")
     share = BLK // KVH
     moved = lax.all_to_all(
         mine.reshape(ZL * KVH, share, wide), ("zl", "x", "zh"), split_axis=0, concat_axis=0, tiled=True

time: 67.6 us -> 61 us (0.902)
  blocking collectives: 0 us -> 23.5 us
  starting transfers between devices: 25.9 us -> 12.5 us
  waiting for transfers between devices: 22.4 us -> 12.3 us
  local copies, waits for them, and re-layouts: 6.22 us -> 0.31 us
    all_to_all x0 -> x1, blocking collectives: none -> 23.5 us  [local(): lax.all_to_all(mine.reshape(ZL * KVH, share, wide), ('zl', 'x', 'zh'), sp...]
    all_to_all x1 -> x0, starting transfers between devices: 11.9 us -> none  [local(): lax.all_to_all(mine.reshape(ZL * KVH, share, wide), ('zl', 'x', 'zh'), sp...]
    all_to_all x1 -> x0, waiting for transfers between devices: 6.09 us -> none  [local(): lax.all_to_all(mine.reshape(ZL * KVH, share, wide), ('zl', 'x', 'zh'), sp...]
    unnamed x30 -> x10, local copies, waits for them, and re-layouts: 5.94 us -> 0.03 us
    ppermute x11, waiting for transfers between devices: 16.3 us -> 12.3 us  [swap(): return lax.ppermute(x, axis, [(i, i ^ mask) for i in range(size)])]
    ppermute x11, starting transfers between devices: 14.1 us -> 12.5 us  [swap(): return lax.ppermute(x, axis, [(i, i ^ mask) for i in range(size)])]
    another operation x2 -> x0, other arithmetic: 0.88 us -> none  [local(): theirs = swap(jnp.stack(column), 'core', NCORE, 1)]
    concatenate x0 -> x1, other arithmetic: none -> 0.79 us  [local(): own = jnp.concatenate([keys[:, 0, :], values[:, 0, :]], axis=1)]
  transfers between devices with their start and end apart: 12 -> 11, of which waited for: 8 -> 8; matrix products, arithmetic and copies ran while one was open for 3% -> 3% of each run, Pallas kernels for 11% -> 13%
where the time goes in v3:
time: 61 us; the launch traced here: 60.8 us
  blocking collectives  23.5 us (39%)
  starting transfers between devices  12.5 us (20%)
  waiting for transfers between devices  12.3 us (20%)
  Pallas kernels  8.95 us (15%)
  other arithmetic  2.42 us (4%)
  between operations  0.8 us (1%)
    all_to_all x1, blocking collectives, local(): lax.all_to_all(mine.reshape(ZL * KVH, share, wide), ('zl', 'x', 'zh'), sp...  23.5 us
    ppermute x11, starting transfers between devices, swap(): return lax.ppermute(x, axis, [(i, i ^ mask) for i in range(size)])  12.5 us
    ppermute x11, waiting for transfers between devices, swap(): return lax.ppermute(x, axis, [(i, i ^ mask) for i in range(size)])  12.3 us
    pallas_call x11, Pallas kernels, call(): pl.pallas_call(body, out_shape=outs, in_specs=specs or [VMEM] * len(input...  8.95 us
    reduce_sum x1, other arithmetic, local(): delta = jnp.sum(out_grad.astype(f32) * outputs.astype(f32), axis=2)  1.61 us
  transfers between devices with their start and end apart: 11, of which 8 were waited for; matrix products, arithmetic and copies ran while one was open for 3% of the time, Pallas kernels for 13%

profile of v3, /device:TPU:32, one launch (start us, length us, event | category | flops | bytes accessed | tf_op | source)
XLA Modules:
  0.0 60.8 jit_solution(3596799484795987158)
XLA Ops:
  0.6 0.8 %pad_maximum_fusion.own = bf16[128,256]{1,0:T(8,128)(2,1)S(1)} fusion(bf16[128,128]{1,0:T(8,128)(2,1)} %bitcast.17, bf16[128,128]{1,0:T(8,128)(2,1)} %bitcast.18), kind=kLoop, calls=%fused_computation.1 | loop fusion | flops 131072 | bytes 131072 | tf_op jit(solution)/shard_map/concatenate | solution.py:198
  1.4 2.0 %collective-permute-start.2 = (bf16[128,256]{1,0:T(8,128)(2,1)S(1)}, bf16[128,256]{1,0:T(8,128)(2,1)S(1)}, u32[]{:S(2)}, u32[]{:S(2)}) collective-permute-start(bf16[128,256]{1,0:T(8,128)(2,1)S(1)} %pad_maximum_fusion.own), channel_id=1, source_target_pairs={{0,192},{64,128},{128,64},{192,0},{1,193},{65,129},{129,65},{193,1... | collective-permute-start | bytes 196616 | tf_op jit(solution)/shard_map/ppermute | solution.py:188
  3.4 2.3 %collective-permute-start.1 = (bf16[128,256]{1,0:T(8,128)(2,1)S(1)}, bf16[128,256]{1,0:T(8,128)(2,1)S(1)}, u32[]{:S(2)}, u32[]{:S(2)}) collective-permute-start(bf16[128,256]{1,0:T(8,128)(2,1)S(1)} %pad_maximum_fusion.own), channel_id=1, source_target_pairs={{0,128},{64,192},{128,0},{192,64},{1,129},{65,193},{129,1},{193,65... | collective-permute-start | bytes 196616 | tf_op jit(solution)/shard_map/ppermute | solution.py:188
  5.7 0.5 collective-permute-start
  6.3 0.1 copy.12
  6.5 1.6 %multiply_reduce_fusion = f32[128,16]{1,0:T(8,128)S(1)} fusion(bf16[128,16,128]{2,1,0:T(8,128)(2,1)} %param.11, bf16[128,16,128]{2,1,0:T(8,128)(2,1)} %param.12), kind=kLoop, calls=%fused_computation | loop fusion | flops 1046528 | bytes 1056768 | tf_op jit(solution)/shard_map/reduce_sum | solution.py:205
  8.3 0.6 %plan.1 = (s32[24,128]{1,0:T(8,128)S(1)}, s32[2,2048]{1,0:T(2,128)S(1)}) custom-call(s32[32]{0:T(128)S(1)} %copy-done.2, s32[12]{0:T(128)S(1)} %copy-done.3), custom_call_target="tpu_custom_call" | custom-call | bytes 262144 | tf_op jit(solution)/shard_map/plan/pallas_call | solution.py:26
  8.9 0.6 collective-permute-done.1.col2
  9.5 1.4 %collective-permute-done.col1 = bf16[128,256]{1,0:T(8,128)(2,1)S(1)} collective-permute-done((bf16[128,256]{1,0:T(8,128)(2,1)S(1)}, bf16[128,256]{1,0:T(8,128)(2,1)S(1)}, u32[]{:S(2)}, u32[]{:S(2)}) %collective-permute-start) | collective-permute-done | bytes 65568 | tf_op jit(solution)/shard_map/ppermute | solution.py:188
  10.9 0.1 collective-permute-start.3
  11.0 1.5 %collective-permute-done.3.theirs = bf16[4,128,256]{2,1,0:T(8,128)(2,1)S(1)} collective-permute-done((bf16[4,128,256]{2,1,0:T(8,128)(2,1)S(1)}, bf16[4,128,256]{2,1,0:T(8,128)(2,1)S(1)}, u32[]{:S(2)}, u32[]{:S(2)}) %collective-permute-start.3) | collective-permute-done | bytes 262176 | tf_op jit(solution)/shard_map/ppermute | solution.py:188
  12.6 0.1 select.1
  12.7 1.7 %collective-permute-start.4 = (bf16[256,256]{1,0:T(8,128)(2,1)S(1)}, bf16[256,256]{1,0:T(8,128)(2,1)S(1)}, u32[]{:S(2)}, u32[]{:S(2)}) collective-permute-start(bf16[256,256]{1,0:T(8,128)(2,1)S(1)} %get-tuple-element.33), channel_id=1, source_target_pairs={{0,16},{16,0},{32,48},{48,32},{1,17},{17,1},{33,49},{49,33},{2,18}... | collective-permute-start | bytes 393224 | tf_op jit(solution)/shard_map/ppermute | solution.py:188
  14.3 2.9 %collective-permute-start.5 = (bf16[256,256]{1,0:T(8,128)(2,1)S(1)}, bf16[256,256]{1,0:T(8,128)(2,1)S(1)}, u32[]{:S(2)}, u32[]{:S(2)}) collective-permute-start(bf16[256,256]{1,0:T(8,128)(2,1)S(1)} %get-tuple-element.34), channel_id=1, source_target_pairs={{0,32},{16,48},{32,0},{48,16},{1,33},{17,49},{33,1},{49,17},{2,34}... | collective-permute-start | bytes 393224 | tf_op jit(solution)/shard_map/ppermute | solution.py:188
  17.2 0.2 collective-permute-start.6
  17.5 0.2 class0.1
  17.7 1.0 %collective-permute-done.4.kv.kv1 = bf16[256,256]{1,0:T(8,128)(2,1)S(1)} collective-permute-done((bf16[256,256]{1,0:T(8,128)(2,1)S(1)}, bf16[256,256]{1,0:T(8,128)(2,1)S(1)}, u32[]{:S(2)}, u32[]{:S(2)}) %collective-permute-start.4) | collective-permute-done | bytes 131104 | tf_op jit(solution)/shard_map/ppermute | solution.py:188
  18.7 0.2 class1.1
  18.9 1.4 %collective-permute-start.7 = (bf16[256,256]{1,0:T(8,128)(2,1)S(1)}, bf16[256,256]{1,0:T(8,128)(2,1)S(1)}, u32[]{:S(2)}, u32[]{:S(2)}) collective-permute-start(bf16[256,256]{1,0:T(8,128)(2,1)S(1)} %get-tuple-element.47), channel_id=1, source_target_pairs={{0,16},{16,0},{32,48},{48,32},{1,17},{17,1},{33,49},{49,33},{2,18}... | collective-permute-start | bytes 393224 | tf_op jit(solution)/shard_map/ppermute | solution.py:188
  20.3 3.4 %collective-permute-done.5.kv.kv2 = bf16[256,256]{1,0:T(8,128)(2,1)S(1)} collective-permute-done((bf16[256,256]{1,0:T(8,128)(2,1)S(1)}, bf16[256,256]{1,0:T(8,128)(2,1)S(1)}, u32[]{:S(2)}, u32[]{:S(2)}) %collective-permute-start.5) | collective-permute-done | bytes 131104 | tf_op jit(solution)/shard_map/ppermute | solution.py:188
  23.7 1.9 %class2.1 = (bf16[256,256]{1,0:T(8,128)(2,1)S(1)}, bf16[256,2048]{1,0:T(8,128)(2,1)S(1)}, f32[8,128]{1,0:T(8,128)S(1)}) custom-call(s32[24,128]{1,0:T(8,128)S(1)} %get-tuple-element.29.plan, bf16[2048,128]{1,0:T(8,128)(2,1)S(1)} %bitcast.15, bf16[2048,128]{1,0:T(8,128)(2,1)S(1)} %bitcast.11, f32[2,2048]{1,0:T(2,128)S(1)} %pad_maximum_fusion.1.stats, ...), custom_call_target="tpu_custom_call" | custom-call | flops 536870912 | bytes 1572864 | tf_op jit(solution)/shard_map/class2/pallas_call | solution.py:26
  25.6 0.7 %collective-permute-start.8 = (bf16[256,256]{1,0:T(8,128)(2,1)S(1)}, bf16[256,256]{1,0:T(8,128)(2,1)S(1)}, u32[]{:S(2)}, u32[]{:S(2)}) collective-permute-start(bf16[256,256]{1,0:T(8,128)(2,1)S(1)} %get-tuple-element.48), channel_id=1, source_target_pairs={{0,32},{16,48},{32,0},{48,16},{1,33},{17,49},{33,1},{49,17},{2,34}... | collective-permute-start | bytes 393224 | tf_op jit(solution)/shard_map/ppermute | solution.py:188
  26.3 1.9 %class3.1 = (bf16[256,256]{1,0:T(8,128)(2,1)S(1)}, bf16[256,2048]{1,0:T(8,128)(2,1)S(1)}, f32[8,128]{1,0:T(8,128)S(1)}) custom-call(s32[24,128]{1,0:T(8,128)S(1)} %get-tuple-element.29.plan, bf16[2048,128]{1,0:T(8,128)(2,1)S(1)} %bitcast.16, bf16[2048,128]{1,0:T(8,128)(2,1)S(1)} %bitcast.12, f32[2,2048]{1,0:T(2,128)S(1)} %pad_maximum_fusion.1.stats, ...), custom_call_target="tpu_custom_call" | custom-call | flops 536870912 | bytes 1572864 | tf_op jit(solution)/shard_map/class3/pallas_call | solution.py:26
  28.2 0.7 %collective-permute-start.9 = (bf16[256,256]{1,0:T(8,128)(2,1)S(1)}, bf16[256,256]{1,0:T(8,128)(2,1)S(1)}, u32[]{:S(2)}, u32[]{:S(2)}) collective-permute-start(bf16[256,256]{1,0:T(8,128)(2,1)S(1)} %get-tuple-element.49), channel_id=1, source_target_pairs={{0,48},{16,32},{32,16},{48,0},{1,49},{17,33},{33,17},{49,1},{2,50}... | collective-permute-start | bytes 393224 | tf_op jit(solution)/shard_map/ppermute | solution.py:188
  28.9 2.9 %query.1 = (bf16[2048,128]{1,0:T(8,128)(2,1)}, f32[8,128]{1,0:T(8,128)S(1)}) custom-call(s32[24,128]{1,0:T(8,128)S(1)} %get-tuple-element.29.plan, bf16[256,256]{1,0:T(8,128)(2,1)S(1)} %get-tuple-element.32.kv.kv0, bf16[256,256]{1,0:T(8,128)(2,1)S(1)} %collective-permute-done.4.kv.kv1, bf16[256,256]{1,0:T(8,128)(2,1)S(1)} %collective-permute-done.5.kv.kv2, ...), custom_call_target="tpu_custom_call" | custom-call | flops 536870912 | bytes 4194304 | tf_op jit(solution)/shard_map/query/pallas_call | solution.py:26
  31.8 0.4 collective-permute-done.8.part2
  32.2 2.4 %collective-permute-done.9.part3 = bf16[256,256]{1,0:T(8,128)(2,1)S(1)} collective-permute-done((bf16[256,256]{1,0:T(8,128)(2,1)S(1)}, bf16[256,256]{1,0:T(8,128)(2,1)S(1)}, u32[]{:S(2)}, u32[]{:S(2)}) %collective-permute-start.9) | collective-permute-done | bytes 131104 | tf_op jit(solution)/shard_map/ppermute | solution.py:188
  34.6 0.4 total.1
  35.0 0.1 collective-permute-start.10
  35.1 1.5 %collective-permute-done.10.theirs = bf16[4,128,256]{2,1,0:T(8,128)(2,1)S(1)} collective-permute-done((bf16[4,128,256]{2,1,0:T(8,128)(2,1)S(1)}, bf16[4,128,256]{2,1,0:T(8,128)(2,1)S(1)}, u32[]{:S(2)}, u32[]{:S(2)}) %collective-permute-start.10) | collective-permute-done | bytes 262176 | tf_op jit(solution)/shard_map/ppermute | solution.py:188
  36.7 23.5 %all_to_all.5.moved = bf16[32,16,256]{2,1,0:T(8,128)(2,1)S(1)} all-to-all(bf16[32,16,256]{2,1,0:T(8,128)(2,1)S(1)} %bitcast.8), channel_id=1, replica_groups=mesh['zl'=4,'y'=4,'core'=2,'x'=4,'zh'=2] {'zl','x','zh'}, dimensions={0} | all-to-all | bytes 524288 | tf_op jit(solution)/shard_map/all_to_all | solution.py:240
  60.1 0.7 %finish.1 = (bf16[16,1024]{1,0:T(8,128)(2,1)}, bf16[16,1024]{1,0:T(8,128)(2,1)}) custom-call(bf16[32,16,256]{2,1,0:T(8,128)(2,1)S(1)} %all_to_all.5.moved), custom_call_target="tpu_custom_call" | custom-call | bytes 262144 | tf_op jit(solution)/shard_map/finish/pallas_call | solution.py:26
  (19 shorter events, 0.3 us)
Async XLA Ops:
  0.6 5.6 %copy-start.4 = (f32[16,128]{1,0:T(8,128)S(1)}, f32[16,128]{1,0:T(8,128)}, u32[]{:S(2)}) copy-start(f32[16,128]{1,0:T(8,128)} %param.13) | copy-start | bytes 24580
  1.4 7.5 %collective-permute-start.2 = (bf16[128,256]{1,0:T(8,128)(2,1)S(1)}, bf16[128,256]{1,0:T(8,128)(2,1)S(1)}, u32[]{:S(2)}, u32[]{:S(2)}) collective-permute-start(bf16[128,256]{1,0:T(8,128)(2,1)S(1)} %pad_maximum_fusion.own), channel_id=1, source_target_pairs={{0,192},{64,128},{128,64},{192,0},{1,193},{65,129},{129,65},{193,1... | collective-permute-start | bytes 196616 | tf_op jit(solution)/shard_map/ppermute | solution.py:188
  3.4 6.0 %collective-permute-start.1 = (bf16[128,256]{1,0:T(8,128)(2,1)S(1)}, bf16[128,256]{1,0:T(8,128)(2,1)S(1)}, u32[]{:S(2)}, u32[]{:S(2)}) collective-permute-start(bf16[128,256]{1,0:T(8,128)(2,1)S(1)} %pad_maximum_fusion.own), channel_id=1, source_target_pairs={{0,128},{64,192},{128,0},{192,64},{1,129},{65,193},{129,1},{193,65... | collective-permute-start | bytes 196616 | tf_op jit(solution)/shard_map/ppermute | solution.py:188
  5.7 5.2 %collective-permute-start = (bf16[128,256]{1,0:T(8,128)(2,1)S(1)}, bf16[128,256]{1,0:T(8,128)(2,1)S(1)}, u32[]{:S(2)}, u32[]{:S(2)}) collective-permute-start(bf16[128,256]{1,0:T(8,128)(2,1)S(1)} %pad_maximum_fusion.own), channel_id=1, source_target_pairs={{0,64},{64,0},{128,192},{192,128},{1,65},{65,1},{129,193},{193,129... | collective-permute-start | bytes 196616 | tf_op jit(solution)/shard_map/ppermute | solution.py:188
  6.5 1.8 %copy-start.2 = (s32[32]{0:T(128)S(1)}, s32[32]{0:T(128)}, u32[]{:S(2)}) copy-start(s32[32]{0:T(128)} %order.1) | copy-start | bytes 388
  6.5 1.8 %copy-start.3 = (s32[12]{0:T(128)S(1)}, s32[12]{0:T(128)}, u32[]{:S(2)}) copy-start(s32[12]{0:T(128)} %lengths.1) | copy-start | bytes 148
  6.5 11.0 %copy-start.1 = (bf16[128,16,128]{2,1,0:T(8,128)(2,1)S(1)}, bf16[128,16,128]{2,1,0:T(8,128)(2,1)}, u32[]{:S(2)}) copy-start(bf16[128,16,128]{2,1,0:T(8,128)(2,1)} %param.8) | copy-start | bytes 1572868
  8.1 9.4 %copy-start = (bf16[128,16,128]{2,1,0:T(8,128)(2,1)S(1)}, bf16[128,16,128]{2,1,0:T(8,128)(2,1)}, u32[]{:S(2)}) copy-start(bf16[128,16,128]{2,1,0:T(8,128)(2,1)} %param.12) | copy-start | bytes 1572868
  10.9 1.6 %collective-permute-start.3 = (bf16[4,128,256]{2,1,0:T(8,128)(2,1)S(1)}, bf16[4,128,256]{2,1,0:T(8,128)(2,1)S(1)}, u32[]{:S(2)}, u32[]{:S(2)}) collective-permute-start(bf16[4,128,256]{2,1,0:T(8,128)(2,1)S(1)} %get-tuple-element.31), channel_id=1, source_target_pairs={{0,8},{8,0},{1,9},{9,1},{2,10},{10,2},{3,11},{11,3},{4,12},{12,4},... | collective-permute-start | bytes 786440 | tf_op jit(solution)/shard_map/ppermute | solution.py:188
  12.7 6.1 %collective-permute-start.4 = (bf16[256,256]{1,0:T(8,128)(2,1)S(1)}, bf16[256,256]{1,0:T(8,128)(2,1)S(1)}, u32[]{:S(2)}, u32[]{:S(2)}) collective-permute-start(bf16[256,256]{1,0:T(8,128)(2,1)S(1)} %get-tuple-element.33), channel_id=1, source_target_pairs={{0,16},{16,0},{32,48},{48,32},{1,17},{17,1},{33,49},{49,33},{2,18}... | collective-permute-start | bytes 393224 | tf_op jit(solution)/shard_map/ppermute | solution.py:188
  14.3 9.3 %collective-permute-start.5 = (bf16[256,256]{1,0:T(8,128)(2,1)S(1)}, bf16[256,256]{1,0:T(8,128)(2,1)S(1)}, u32[]{:S(2)}, u32[]{:S(2)}) collective-permute-start(bf16[256,256]{1,0:T(8,128)(2,1)S(1)} %get-tuple-element.34), channel_id=1, source_target_pairs={{0,32},{16,48},{32,0},{48,16},{1,33},{17,49},{33,1},{49,17},{2,34}... | collective-permute-start | bytes 393224 | tf_op jit(solution)/shard_map/ppermute | solution.py:188
  17.2 9.1 %collective-permute-start.6 = (bf16[256,256]{1,0:T(8,128)(2,1)S(1)}, bf16[256,256]{1,0:T(8,128)(2,1)S(1)}, u32[]{:S(2)}, u32[]{:S(2)}) collective-permute-start(bf16[256,256]{1,0:T(8,128)(2,1)S(1)} %get-tuple-element.35), channel_id=1, source_target_pairs={{0,48},{16,32},{32,16},{48,0},{1,49},{17,33},{33,17},{49,1},{2,50}... | collective-permute-start | bytes 393224 | tf_op jit(solution)/shard_map/ppermute | solution.py:188
  18.9 12.8 %collective-permute-start.7 = (bf16[256,256]{1,0:T(8,128)(2,1)S(1)}, bf16[256,256]{1,0:T(8,128)(2,1)S(1)}, u32[]{:S(2)}, u32[]{:S(2)}) collective-permute-start(bf16[256,256]{1,0:T(8,128)(2,1)S(1)} %get-tuple-element.47), channel_id=1, source_target_pairs={{0,16},{16,0},{32,48},{48,32},{1,17},{17,1},{33,49},{49,33},{2,18}... | collective-permute-start | bytes 393224 | tf_op jit(solution)/shard_map/ppermute | solution.py:188
  25.6 6.6 %collective-permute-start.8 = (bf16[256,256]{1,0:T(8,128)(2,1)S(1)}, bf16[256,256]{1,0:T(8,128)(2,1)S(1)}, u32[]{:S(2)}, u32[]{:S(2)}) collective-permute-start(bf16[256,256]{1,0:T(8,128)(2,1)S(1)} %get-tuple-element.48), channel_id=1, source_target_pairs={{0,32},{16,48},{32,0},{48,16},{1,33},{17,49},{33,1},{49,17},{2,34}... | collective-permute-start | bytes 393224 | tf_op jit(solution)/shard_map/ppermute | solution.py:188
  28.2 6.4 %collective-permute-start.9 = (bf16[256,256]{1,0:T(8,128)(2,1)S(1)}, bf16[256,256]{1,0:T(8,128)(2,1)S(1)}, u32[]{:S(2)}, u32[]{:S(2)}) collective-permute-start(bf16[256,256]{1,0:T(8,128)(2,1)S(1)} %get-tuple-element.49), channel_id=1, source_target_pairs={{0,48},{16,32},{32,16},{48,0},{1,49},{17,33},{33,17},{49,1},{2,50}... | collective-permute-start | bytes 393224 | tf_op jit(solution)/shard_map/ppermute | solution.py:188
  35.0 1.6 %collective-permute-start.10 = (bf16[4,128,256]{2,1,0:T(8,128)(2,1)S(1)}, bf16[4,128,256]{2,1,0:T(8,128)(2,1)S(1)}, u32[]{:S(2)}, u32[]{:S(2)}) collective-permute-start(bf16[4,128,256]{2,1,0:T(8,128)(2,1)S(1)} %get-tuple-element.52), channel_id=1, source_target_pairs={{0,8},{8,0},{1,9},{9,1},{2,10},{10,2},{3,11},{11,3},{4,12},{12,4},... | collective-permute-start | bytes 786440 | tf_op jit(solution)/shard_map/ppermute | solution.py:188

commit v4 on v3

--- a/solution.py
+++ b/solution.py
@@ -215,17 +215,15 @@
     pair = shape((2 * BLK, wide), bf16)
     sends = call(select_kernel, (pair,) * 4, (plan, *column, theirs), "select")
     kvs = [sends[0]] + [swap(sends[m], "y", NY, m) for m in (1, 2, 3)]
-    parts, dss = [], []
-    for m in range(4):
-        part, ds, token = call(
+    parts, dss = [None] * 4, [None] * 4
+    for m in (0, 2, 1, 3):
+        parts[m], dss[m], token = call(
             functools.partial(class_kernel, m=m),
             (shape((2 * BLK, wide), f32 if m == 0 else bf16), shape((2 * BLK, cols), bf16), shape((8, LANES), f32)),
             (plan, q, do, stats, span, kvs[m], token), "class" + str(m),
             scratch=[pltpu.VMEM((2 * BLK, wide), f32)],
             flops=8 * cols * 2 * BLK * dh, moved=3 * cols * dh * 2,
         )
-        parts.append(part)
-        dss.append(ds)
     back = [parts[0]] + [swap(parts[m], "y", NY, m) for m in (1, 2, 3)]
     grad_q, token = call(
         query_kernel, (shape((cols, dh), bf16), shape((8, LANES), f32)), (plan, *kvs, *dss, token), "query",

time: 61 us -> 60 us (0.984)
  waiting for transfers between devices: 12.3 us -> 8.98 us
  starting transfers between devices: 12.5 us -> 15.5 us
  blocking collectives: 23.5 us -> 22.4 us
    ppermute x11, waiting for transfers between devices: 12.3 us -> 8.98 us  [swap(): return lax.ppermute(x, axis, [(i, i ^ mask) for i in range(size)])]
    ppermute x11, starting transfers between devices: 12.5 us -> 15.5 us  [swap(): return lax.ppermute(x, axis, [(i, i ^ mask) for i in range(size)])]
    all_to_all x1, blocking collectives: 23.5 us -> 22.4 us  [local(): lax.all_to_all(mine.reshape(ZL * KVH, share, wide), ('zl', 'x', 'zh'), sp...]
  transfers between devices with their start and end apart: 11 -> 11, of which waited for: 8 -> 7; matrix products, arithmetic and copies ran while one was open for 3% -> 3% of each run, Pallas kernels for 13% -> 13%
where the time goes in v4:
time: 60 us; the launch traced here: 59.4 us
  blocking collectives  22.4 us (37%)
  starting transfers between devices  15.5 us (26%)
  waiting for transfers between devices  8.98 us (15%)
  Pallas kernels  8.94 us (15%)
  other arithmetic  2.42 us (4%)
  between operations  0.81 us (1%)
    all_to_all x1, blocking collectives, local(): lax.all_to_all(mine.reshape(ZL * KVH, share, wide), ('zl', 'x', 'zh'), sp...  22.4 us
    ppermute x11, starting transfers between devices, swap(): return lax.ppermute(x, axis, [(i, i ^ mask) for i in range(size)])  15.5 us
    ppermute x11, waiting for transfers between devices, swap(): return lax.ppermute(x, axis, [(i, i ^ mask) for i in range(size)])  8.98 us
    pallas_call x11, Pallas kernels, call(): pl.pallas_call(body, out_shape=outs, in_specs=specs or [VMEM] * len(input...  8.94 us
    reduce_sum x1, other arithmetic, local(): delta = jnp.sum(out_grad.astype(f32) * outputs.astype(f32), axis=2)  1.61 us
  transfers between devices with their start and end apart: 11, of which 7 were waited for; matrix products, arithmetic and copies ran while one was open for 3% of the time, Pallas kernels for 13%

profile of v4, /device:TPU:32, one launch (start us, length us, event | category | flops | bytes accessed | tf_op | source)
XLA Modules:
  0.0 59.4 jit_solution(11861149425428075703)
XLA Ops:
  0.6 0.8 %pad_maximum_fusion.own = bf16[128,256]{1,0:T(8,128)(2,1)S(1)} fusion(bf16[128,128]{1,0:T(8,128)(2,1)} %bitcast.17, bf16[128,128]{1,0:T(8,128)(2,1)} %bitcast.18), kind=kLoop, calls=%fused_computation.1 | loop fusion | flops 131072 | bytes 131072 | tf_op jit(solution)/shard_map/concatenate | solution.py:198
  1.4 2.0 %collective-permute-start.2 = (bf16[128,256]{1,0:T(8,128)(2,1)S(1)}, bf16[128,256]{1,0:T(8,128)(2,1)S(1)}, u32[]{:S(2)}, u32[]{:S(2)}) collective-permute-start(bf16[128,256]{1,0:T(8,128)(2,1)S(1)} %pad_maximum_fusion.own), channel_id=1, source_target_pairs={{0,192},{64,128},{128,64},{192,0},{1,193},{65,129},{129,65},{193,1... | collective-permute-start | bytes 196616 | tf_op jit(solution)/shard_map/ppermute | solution.py:188
  3.4 2.3 %collective-permute-start.1 = (bf16[128,256]{1,0:T(8,128)(2,1)S(1)}, bf16[128,256]{1,0:T(8,128)(2,1)S(1)}, u32[]{:S(2)}, u32[]{:S(2)}) collective-permute-start(bf16[128,256]{1,0:T(8,128)(2,1)S(1)} %pad_maximum_fusion.own), channel_id=1, source_target_pairs={{0,128},{64,192},{128,0},{192,64},{1,129},{65,193},{129,1},{193,65... | collective-permute-start | bytes 196616 | tf_op jit(solution)/shard_map/ppermute | solution.py:188
  5.7 0.5 collective-permute-start
  6.3 0.1 copy.12
  6.4 0.1 stack_reshape.6
  6.5 1.6 %multiply_reduce_fusion = f32[128,16]{1,0:T(8,128)S(1)} fusion(bf16[128,16,128]{2,1,0:T(8,128)(2,1)} %param.11, bf16[128,16,128]{2,1,0:T(8,128)(2,1)} %param.12), kind=kLoop, calls=%fused_computation | loop fusion | flops 1046528 | bytes 1056768 | tf_op jit(solution)/shard_map/reduce_sum | solution.py:205
  8.3 0.6 %plan.1 = (s32[24,128]{1,0:T(8,128)S(1)}, s32[2,2048]{1,0:T(2,128)S(1)}) custom-call(s32[32]{0:T(128)S(1)} %copy-done.2, s32[12]{0:T(128)S(1)} %copy-done.3), custom_call_target="tpu_custom_call" | custom-call | bytes 262144 | tf_op jit(solution)/shard_map/plan/pallas_call | solution.py:26
  8.9 0.6 collective-permute-done.1.col2
  9.5 1.4 %collective-permute-done.col1 = bf16[128,256]{1,0:T(8,128)(2,1)S(1)} collective-permute-done((bf16[128,256]{1,0:T(8,128)(2,1)S(1)}, bf16[128,256]{1,0:T(8,128)(2,1)S(1)}, u32[]{:S(2)}, u32[]{:S(2)}) %collective-permute-start) | collective-permute-done | bytes 65568 | tf_op jit(solution)/shard_map/ppermute | solution.py:188
  10.9 0.1 collective-permute-start.3
  11.0 1.5 %collective-permute-done.3.theirs = bf16[4,128,256]{2,1,0:T(8,128)(2,1)S(1)} collective-permute-done((bf16[4,128,256]{2,1,0:T(8,128)(2,1)S(1)}, bf16[4,128,256]{2,1,0:T(8,128)(2,1)S(1)}, u32[]{:S(2)}, u32[]{:S(2)}) %collective-permute-start.3) | collective-permute-done | bytes 262176 | tf_op jit(solution)/shard_map/ppermute | solution.py:188
  12.6 0.1 select.1
  12.7 3.3 %collective-permute-start.5 = (bf16[256,256]{1,0:T(8,128)(2,1)S(1)}, bf16[256,256]{1,0:T(8,128)(2,1)S(1)}, u32[]{:S(2)}, u32[]{:S(2)}) collective-permute-start(bf16[256,256]{1,0:T(8,128)(2,1)S(1)} %get-tuple-element.34), channel_id=1, source_target_pairs={{0,32},{16,48},{32,0},{48,16},{1,33},{17,49},{33,1},{49,17},{2,34}... | collective-permute-start | bytes 393224 | tf_op jit(solution)/shard_map/ppermute | solution.py:188
  15.9 0.7 %collective-permute-start.4 = (bf16[256,256]{1,0:T(8,128)(2,1)S(1)}, bf16[256,256]{1,0:T(8,128)(2,1)S(1)}, u32[]{:S(2)}, u32[]{:S(2)}) collective-permute-start(bf16[256,256]{1,0:T(8,128)(2,1)S(1)} %get-tuple-element.33), channel_id=1, source_target_pairs={{0,16},{16,0},{32,48},{48,32},{1,17},{17,1},{33,49},{49,33},{2,18}... | collective-permute-start | bytes 393224 | tf_op jit(solution)/shard_map/ppermute | solution.py:188
  16.6 0.4 collective-permute-start.6
  17.0 1.9 %class0.1 = (f32[256,256]{1,0:T(8,128)S(1)}, bf16[256,2048]{1,0:T(8,128)(2,1)S(1)}, f32[8,128]{1,0:T(8,128)S(1)}) custom-call(s32[24,128]{1,0:T(8,128)S(1)} %get-tuple-element.29.plan, bf16[2048,128]{1,0:T(8,128)(2,1)S(1)} %bitcast.13, bf16[2048,128]{1,0:T(8,128)(2,1)S(1)} %bitcast.9, f32[2,2048]{1,0:T(2,128)S(1)} %pad_maximum_fusion.1.stats, ...), custom_call_target="tpu_custom_call" | custom-call | flops 536870912 | bytes 1572864 | tf_op jit(solution)/shard_map/class0/pallas_call | solution.py:26
  18.9 1.7 %collective-permute-done.5.kv.kv2 = bf16[256,256]{1,0:T(8,128)(2,1)S(1)} collective-permute-done((bf16[256,256]{1,0:T(8,128)(2,1)S(1)}, bf16[256,256]{1,0:T(8,128)(2,1)S(1)}, u32[]{:S(2)}, u32[]{:S(2)}) %collective-permute-start.5) | collective-permute-done | bytes 131104 | tf_op jit(solution)/shard_map/ppermute | solution.py:188
  20.6 0.2 class2.1
  20.8 5.0 %collective-permute-start.8 = (bf16[256,256]{1,0:T(8,128)(2,1)S(1)}, bf16[256,256]{1,0:T(8,128)(2,1)S(1)}, u32[]{:S(2)}, u32[]{:S(2)}) collective-permute-start(bf16[256,256]{1,0:T(8,128)(2,1)S(1)} %get-tuple-element.48), channel_id=1, source_target_pairs={{0,32},{16,48},{32,0},{48,16},{1,33},{17,49},{33,1},{49,17},{2,34}... | collective-permute-start | bytes 393224 | tf_op jit(solution)/shard_map/ppermute | solution.py:188
  25.8 1.9 %class1.1 = (bf16[256,256]{1,0:T(8,128)(2,1)S(1)}, bf16[256,2048]{1,0:T(8,128)(2,1)S(1)}, f32[8,128]{1,0:T(8,128)S(1)}) custom-call(s32[24,128]{1,0:T(8,128)S(1)} %get-tuple-element.29.plan, bf16[2048,128]{1,0:T(8,128)(2,1)S(1)} %bitcast.15, bf16[2048,128]{1,0:T(8,128)(2,1)S(1)} %bitcast.11, f32[2,2048]{1,0:T(2,128)S(1)} %pad_maximum_fusion.1.stats, ...), custom_call_target="tpu_custom_call" | custom-call | flops 536870912 | bytes 1572864 | tf_op jit(solution)/shard_map/class1/pallas_call | solution.py:26
  27.7 0.1 collective-permute-start.7
  27.8 0.2 class3.1
  28.0 1.1 %collective-permute-start.9 = (bf16[256,256]{1,0:T(8,128)(2,1)S(1)}, bf16[256,256]{1,0:T(8,128)(2,1)S(1)}, u32[]{:S(2)}, u32[]{:S(2)}) collective-permute-start(bf16[256,256]{1,0:T(8,128)(2,1)S(1)} %get-tuple-element.49), channel_id=1, source_target_pairs={{0,48},{16,32},{32,16},{48,0},{1,49},{17,33},{33,17},{49,1},{2,50}... | collective-permute-start | bytes 393224 | tf_op jit(solution)/shard_map/ppermute | solution.py:188
  29.2 2.9 %query.1 = (bf16[2048,128]{1,0:T(8,128)(2,1)}, f32[8,128]{1,0:T(8,128)S(1)}) custom-call(s32[24,128]{1,0:T(8,128)S(1)} %get-tuple-element.29.plan, bf16[256,256]{1,0:T(8,128)(2,1)S(1)} %get-tuple-element.32.kv.kv0, bf16[256,256]{1,0:T(8,128)(2,1)S(1)} %collective-permute-done.4.kv.kv1, bf16[256,256]{1,0:T(8,128)(2,1)S(1)} %collective-permute-done.5.kv.kv2, ...), custom_call_target="tpu_custom_call" | custom-call | flops 536870912 | bytes 4194304 | tf_op jit(solution)/shard_map/query/pallas_call | solution.py:26
  32.1 0.7 %collective-permute-done.7.part1 = bf16[256,256]{1,0:T(8,128)(2,1)S(1)} collective-permute-done((bf16[256,256]{1,0:T(8,128)(2,1)S(1)}, bf16[256,256]{1,0:T(8,128)(2,1)S(1)}, u32[]{:S(2)}, u32[]{:S(2)}) %collective-permute-start.7) | collective-permute-done | bytes 131104 | tf_op jit(solution)/shard_map/ppermute | solution.py:188
  32.8 1.5 %collective-permute-done.9.part3 = bf16[256,256]{1,0:T(8,128)(2,1)S(1)} collective-permute-done((bf16[256,256]{1,0:T(8,128)(2,1)S(1)}, bf16[256,256]{1,0:T(8,128)(2,1)S(1)}, u32[]{:S(2)}, u32[]{:S(2)}) %collective-permute-start.9) | collective-permute-done | bytes 131104 | tf_op jit(solution)/shard_map/ppermute | solution.py:188
  34.3 0.4 total.1
  34.7 0.1 collective-permute-start.10
  34.8 1.5 %collective-permute-done.10.theirs = bf16[4,128,256]{2,1,0:T(8,128)(2,1)S(1)} collective-permute-done((bf16[4,128,256]{2,1,0:T(8,128)(2,1)S(1)}, bf16[4,128,256]{2,1,0:T(8,128)(2,1)S(1)}, u32[]{:S(2)}, u32[]{:S(2)}) %collective-permute-start.10) | collective-permute-done | bytes 262176 | tf_op jit(solution)/shard_map/ppermute | solution.py:188
  36.3 22.4 %all_to_all.5.moved = bf16[32,16,256]{2,1,0:T(8,128)(2,1)S(1)} all-to-all(bf16[32,16,256]{2,1,0:T(8,128)(2,1)S(1)} %bitcast.8), channel_id=1, replica_groups=mesh['zl'=4,'y'=4,'core'=2,'x'=4,'zh'=2] {'zl','x','zh'}, dimensions={0} | all-to-all | bytes 524288 | tf_op jit(solution)/shard_map/all_to_all | solution.py:238
  58.8 0.7 %finish.1 = (bf16[16,1024]{1,0:T(8,128)(2,1)}, bf16[16,1024]{1,0:T(8,128)(2,1)}) custom-call(bf16[32,16,256]{2,1,0:T(8,128)(2,1)S(1)} %all_to_all.5.moved), custom_call_target="tpu_custom_call" | custom-call | bytes 262144 | tf_op jit(solution)/shard_map/finish/pallas_call | solution.py:26
  (19 shorter events, 0.2 us)
Async XLA Ops:
  0.6 5.6 %copy-start.4 = (f32[16,128]{1,0:T(8,128)S(1)}, f32[16,128]{1,0:T(8,128)}, u32[]{:S(2)}) copy-start(f32[16,128]{1,0:T(8,128)} %param.13) | copy-start | bytes 24580
  1.4 7.5 %collective-permute-start.2 = (bf16[128,256]{1,0:T(8,128)(2,1)S(1)}, bf16[128,256]{1,0:T(8,128)(2,1)S(1)}, u32[]{:S(2)}, u32[]{:S(2)}) collective-permute-start(bf16[128,256]{1,0:T(8,128)(2,1)S(1)} %pad_maximum_fusion.own), channel_id=1, source_target_pairs={{0,192},{64,128},{128,64},{192,0},{1,193},{65,129},{129,65},{193,1... | collective-permute-start | bytes 196616 | tf_op jit(solution)/shard_map/ppermute | solution.py:188
  3.4 6.0 %collective-permute-start.1 = (bf16[128,256]{1,0:T(8,128)(2,1)S(1)}, bf16[128,256]{1,0:T(8,128)(2,1)S(1)}, u32[]{:S(2)}, u32[]{:S(2)}) collective-permute-start(bf16[128,256]{1,0:T(8,128)(2,1)S(1)} %pad_maximum_fusion.own), channel_id=1, source_target_pairs={{0,128},{64,192},{128,0},{192,64},{1,129},{65,193},{129,1},{193,65... | collective-permute-start | bytes 196616 | tf_op jit(solution)/shard_map/ppermute | solution.py:188
  5.7 5.2 %collective-permute-start = (bf16[128,256]{1,0:T(8,128)(2,1)S(1)}, bf16[128,256]{1,0:T(8,128)(2,1)S(1)}, u32[]{:S(2)}, u32[]{:S(2)}) collective-permute-start(bf16[128,256]{1,0:T(8,128)(2,1)S(1)} %pad_maximum_fusion.own), channel_id=1, source_target_pairs={{0,64},{64,0},{128,192},{192,128},{1,65},{65,1},{129,193},{193,129... | collective-permute-start | bytes 196616 | tf_op jit(solution)/shard_map/ppermute | solution.py:188
  6.5 1.8 %copy-start.2 = (s32[32]{0:T(128)S(1)}, s32[32]{0:T(128)}, u32[]{:S(2)}) copy-start(s32[32]{0:T(128)} %order.1) | copy-start | bytes 388
  6.5 1.8 %copy-start.3 = (s32[12]{0:T(128)S(1)}, s32[12]{0:T(128)}, u32[]{:S(2)}) copy-start(s32[12]{0:T(128)} %lengths.1) | copy-start | bytes 148
  6.5 10.5 %copy-start.1 = (bf16[128,16,128]{2,1,0:T(8,128)(2,1)S(1)}, bf16[128,16,128]{2,1,0:T(8,128)(2,1)}, u32[]{:S(2)}) copy-start(bf16[128,16,128]{2,1,0:T(8,128)(2,1)} %param.8) | copy-start | bytes 1572868
  8.1 8.9 %copy-start = (bf16[128,16,128]{2,1,0:T(8,128)(2,1)S(1)}, bf16[128,16,128]{2,1,0:T(8,128)(2,1)}, u32[]{:S(2)}) copy-start(bf16[128,16,128]{2,1,0:T(8,128)(2,1)} %param.12) | copy-start | bytes 1572868
  10.9 1.6 %collective-permute-start.3 = (bf16[4,128,256]{2,1,0:T(8,128)(2,1)S(1)}, bf16[4,128,256]{2,1,0:T(8,128)(2,1)S(1)}, u32[]{:S(2)}, u32[]{:S(2)}) collective-permute-start(bf16[4,128,256]{2,1,0:T(8,128)(2,1)S(1)} %get-tuple-element.31), channel_id=1, source_target_pairs={{0,8},{8,0},{1,9},{9,1},{2,10},{10,2},{3,11},{11,3},{4,12},{12,4},... | collective-permute-start | bytes 786440 | tf_op jit(solution)/shard_map/ppermute | solution.py:188
  12.7 7.9 %collective-permute-start.5 = (bf16[256,256]{1,0:T(8,128)(2,1)S(1)}, bf16[256,256]{1,0:T(8,128)(2,1)S(1)}, u32[]{:S(2)}, u32[]{:S(2)}) collective-permute-start(bf16[256,256]{1,0:T(8,128)(2,1)S(1)} %get-tuple-element.34), channel_id=1, source_target_pairs={{0,32},{16,48},{32,0},{48,16},{1,33},{17,49},{33,1},{49,17},{2,34}... | collective-permute-start | bytes 393224 | tf_op jit(solution)/shard_map/ppermute | solution.py:188
  15.9 9.8 %collective-permute-start.4 = (bf16[256,256]{1,0:T(8,128)(2,1)S(1)}, bf16[256,256]{1,0:T(8,128)(2,1)S(1)}, u32[]{:S(2)}, u32[]{:S(2)}) collective-permute-start(bf16[256,256]{1,0:T(8,128)(2,1)S(1)} %get-tuple-element.33), channel_id=1, source_target_pairs={{0,16},{16,0},{32,48},{48,32},{1,17},{17,1},{33,49},{49,33},{2,18}... | collective-permute-start | bytes 393224 | tf_op jit(solution)/shard_map/ppermute | solution.py:188
  16.6 11.2 %collective-permute-start.6 = (bf16[256,256]{1,0:T(8,128)(2,1)S(1)}, bf16[256,256]{1,0:T(8,128)(2,1)S(1)}, u32[]{:S(2)}, u32[]{:S(2)}) collective-permute-start(bf16[256,256]{1,0:T(8,128)(2,1)S(1)} %get-tuple-element.35), channel_id=1, source_target_pairs={{0,48},{16,32},{32,16},{48,0},{1,49},{17,33},{33,17},{49,1},{2,50}... | collective-permute-start | bytes 393224 | tf_op jit(solution)/shard_map/ppermute | solution.py:188
  20.8 11.2 %collective-permute-start.8 = (bf16[256,256]{1,0:T(8,128)(2,1)S(1)}, bf16[256,256]{1,0:T(8,128)(2,1)S(1)}, u32[]{:S(2)}, u32[]{:S(2)}) collective-permute-start(bf16[256,256]{1,0:T(8,128)(2,1)S(1)} %get-tuple-element.48), channel_id=1, source_target_pairs={{0,32},{16,48},{32,0},{48,16},{1,33},{17,49},{33,1},{49,17},{2,34}... | collective-permute-start | bytes 393224 | tf_op jit(solution)/shard_map/ppermute | solution.py:188
  27.7 5.1 %collective-permute-start.7 = (bf16[256,256]{1,0:T(8,128)(2,1)S(1)}, bf16[256,256]{1,0:T(8,128)(2,1)S(1)}, u32[]{:S(2)}, u32[]{:S(2)}) collective-permute-start(bf16[256,256]{1,0:T(8,128)(2,1)S(1)} %get-tuple-element.47), channel_id=1, source_target_pairs={{0,16},{16,0},{32,48},{48,32},{1,17},{17,1},{33,49},{49,33},{2,18}... | collective-permute-start | bytes 393224 | tf_op jit(solution)/shard_map/ppermute | solution.py:188
  28.0 6.3 %collective-permute-start.9 = (bf16[256,256]{1,0:T(8,128)(2,1)S(1)}, bf16[256,256]{1,0:T(8,128)(2,1)S(1)}, u32[]{:S(2)}, u32[]{:S(2)}) collective-permute-start(bf16[256,256]{1,0:T(8,128)(2,1)S(1)} %get-tuple-element.49), channel_id=1, source_target_pairs={{0,48},{16,32},{32,16},{48,0},{1,49},{17,33},{33,17},{49,1},{2,50}... | collective-permute-start | bytes 393224 | tf_op jit(solution)/shard_map/ppermute | solution.py:188
  34.7 1.6 %collective-permute-start.10 = (bf16[4,128,256]{2,1,0:T(8,128)(2,1)S(1)}, bf16[4,128,256]{2,1,0:T(8,128)(2,1)S(1)}, u32[]{:S(2)}, u32[]{:S(2)}) collective-permute-start(bf16[4,128,256]{2,1,0:T(8,128)(2,1)S(1)} %get-tuple-element.52), channel_id=1, source_target_pairs={{0,8},{8,0},{1,9},{9,1},{2,10},{10,2},{3,11},{11,3},{4,12},{12,4},... | collective-permute-start | bytes 786440 | tf_op jit(solution)/shard_map/ppermute | solution.py:188

commit v5 on v2

v5 whole, which is shorter than its diff:
```python
import functools

import jax
import jax.numpy as jnp
from jax import lax
from jax.experimental import pallas as pl
from jax.experimental.pallas import tpu as pltpu
from jax.sharding import Mesh
from jax.sharding import PartitionSpec as P

BLK = 128
WIN = 5
ZL, NY, NCORE, NX, ZH = 4, 4, 2, 4, 2
KVH = NX * ZH
LOG2E = 1.4426950408889634
CHUNK = 1024
ORDER = (0, 2, 1, 3)
LANES = 128
SEND, WANT, BASE = 0, 8, 16
NT = (((1,), (1,)), ((), ()))
TN = (((0,), (0,)), ((), ()))
SMEM = pl.BlockSpec(memory_space=pltpu.SMEM)
VMEM = pl.BlockSpec(memory_space=pltpu.VMEM)


def call(body, outs, inputs, name, scratch=(), specs=None, flops=0, moved=1 << 18):
    return pl.pallas_call(
        body,
        out_shape=outs,
        in_specs=specs or [VMEM] * len(inputs),
        out_specs=jax.tree.map(lambda _: VMEM, outs),
        scratch_shapes=scratch,
        compiler_params=pltpu.CompilerParams(vmem_limit_bytes=16 * 1024 * 1024),
        cost_estimate=pl.CostEstimate(flops=flops, bytes_accessed=moved, transcendentals=0),
        name=name,
    )(*inputs)


def plan_kernel(order, lengths, plan_ref, span_ref, *, group):
    zl, y, core = lax.axis_index("zl"), lax.axis_index("y"), lax.axis_index("core")
    ends, total = [], 0
    for k in range(lengths.shape[0]):
        total = total + lengths[k]
        ends.append(total)

    def put(row, value):
        plan_ref[row : row + 1, :] = jnp.full((1, LANES), value, jnp.int32)

    cols = span_ref.shape[1]
    for j in range(2):
        me = order[(zl * NY + y) * NCORE + (core ^ j)]
        q_first = me * BLK
        mine = jnp.maximum(lax.shift_right_logical(me, 1) - 2, 0)
        for m in range(4):
            near = order[(zl * NY + (y ^ m)) * NCORE + (core ^ j)]
            first = jnp.maximum(lax.shift_right_logical(near, 1) - 2, 0)
            pair = jnp.minimum(first + ((y - first) & 3), 15)
            want = lax.shift_right_logical(pair, 2)
            put(SEND + 2 * m + j, zl ^ want)
            put(WANT + 2 * m + j, want)
            offset = ((y ^ m) - mine) & 3
            low = ((mine + offset) * 2 + core) * BLK
            put(BASE + 2 * m + j, low)
        pos = q_first + lax.broadcasted_iota(jnp.int32, (1, cols), 1) // group
        start = jnp.zeros((1, cols), jnp.int32)
        for end in ends:
            start = jnp.where(end <= pos, end, start)
        span_ref[2 * j : 2 * j + 1, :] = start
        span_ref[2 * j + 1 : 2 * j + 2, :] = pos


def select_kernel(plan, own, col1, col2, col3, *outs):
    column = (own, col1, col2, col3)
    for m in range(4):
        for j in range(2):
            row = SEND + 2 * m + j
            at = jnp.concatenate([plan[row : row + 1, :]] * (own.shape[1] // LANES), axis=1)
            block = own[...]
            for s in range(1, 4):
                block = jnp.where(at == s, column[s][...], block)
            outs[m][j * BLK : (j + 1) * BLK, :] = block


def class_kernel(plan, q0, do0, stats0, q1, do1, stats1, span, kv, before, part_ref, ds_ref, after, *, m):
    rows, dh = q0.shape
    scale = dh ** (-0.5)
    after[...] = before[...]
    sides = ((q0, do0, stats0), (q1, do1, stats1))
    grads = [None, None]
    for c in range(rows // CHUNK):
        cols = slice(c * CHUNK, (c + 1) * CHUNK)
        for j, (q_ref, do_ref, stats) in enumerate(sides):
            keys = slice(j * BLK, (j + 1) * BLK)
            row = BASE + 2 * m + j
            key_pos = lax.broadcasted_iota(jnp.int32, (BLK, 1), 0) + plan[row : row + 1, 0:1]
            allowed = (key_pos >= span[2 * j : 2 * j + 1, cols]) & (key_pos <= span[2 * j + 1 : 2 * j + 2, cols])
            q = q_ref[cols, :]
            do = do_ref[cols, :]
            s = lax.dot_general(kv[keys, :dh], q, NT, preferred_element_type=jnp.float32)
            dp = lax.dot_general(kv[keys, dh:], do, NT, preferred_element_type=jnp.float32)
            p = jnp.where(allowed, jnp.exp2(s * (scale * LOG2E) - stats[0:1, cols]), 0.0)
            ds = (p * (dp - stats[1:2, cols])).astype(jnp.bfloat16)
            ds_ref[keys, cols] = ds
            dv = jnp.dot(p.astype(jnp.bfloat16), do, preferred_element_type=jnp.float32)
            dk = jnp.dot(ds, q, preferred_element_type=jnp.float32)
            grads[j] = (dk, dv) if c == 0 else (grads[j][0] + dk, grads[j][1] + dv)
    for j, (dk, dv) in enumerate(grads):
        keys = slice(j * BLK, (j + 1) * BLK)
        part_ref[keys, :dh] = (dk * scale).astype(part_ref.dtype)
        part_ref[keys, dh:] = dv.astype(part_ref.dtype)


def query_kernel(kv0, kv1, kv2, kv3, ds0, ds1, ds2, ds3, before, mine, theirs, after, kt):
    rows, dh = mine.shape
    after[...] = before[...]
    for j, out in enumerate((mine, theirs)):
        keys = slice(j * BLK, (j + 1) * BLK)
        for m, kv in enumerate((kv0, kv1, kv2, kv3)):
            kt[:, m * BLK : (m + 1) * BLK] = kv[keys, :dh].T

        def step(c, carry):
            cols = pl.ds(pl.multiple_of(c * CHUNK, CHUNK), CHUNK)
            ds = jnp.concatenate([ref[keys, cols] for ref in (ds0, ds1, ds2, ds3)], axis=0)
            dq = jnp.dot(kt[...], ds, preferred_element_type=jnp.float32)
            out[cols, :] = (dq * dh ** (-0.5)).T.astype(out.dtype)
            return carry

        lax.fori_loop(0, rows // CHUNK, step, 0)


def join_kernel(mine, theirs, out):
    out[...] = (mine[...] + theirs[...].astype(jnp.float32)).astype(out.dtype)


def total_kernel(plan, part0, part1, part2, part3, before, out, acc):
    acc[...] = jnp.zeros_like(acc)
    for m, part in enumerate((part0, part1, part2, part3)):
        for j in range(2):
            row = WANT + 2 * m + j
            z = jnp.max(plan[row : row + 1, :])
            acc[z] += part[j * BLK : (j + 1) * BLK, :].astype(jnp.float32)
    out[...] = acc[...].astype(out.dtype)


def finish_kernel(moved, gk_ref, gv_ref):
    dh = moved.shape[2] // 2
    for k in range(KVH):
        grad = moved[k].astype(jnp.float32)
        for z in range(1, ZL):
            grad += moved[z * KVH + k].astype(jnp.float32)
        gk_ref[:, k * dh : (k + 1) * dh] = grad[:, :dh].astype(gk_ref.dtype)
        gv_ref[:, k * dh : (k + 1) * dh] = grad[:, dh:].astype(gv_ref.dtype)


def swap(x, axis, size, mask):
    return lax.ppermute(x, axis, [(i, i ^ mask) for i in range(size)])


def local(queries, keys, values, outputs, out_grad, logsumexp, doc_lengths, block_order):
    rows, heads, dh = queries.shape
    cols = rows * heads
    wide = 2 * dh
    bf16, f32 = jnp.bfloat16, jnp.float32
    shape = jax.ShapeDtypeStruct

    own = jnp.concatenate([keys[:, 0, :], values[:, 0, :]], axis=1)
    column = [own] + [swap(own, "zl", ZL, m) for m in (1, 2, 3)]
    plan, span = call(
        functools.partial(plan_kernel, group=heads),
        (shape((24, LANES), jnp.int32), shape((4, cols), jnp.int32)),
        (block_order, doc_lengths), "plan", specs=[SMEM, SMEM],
    )
    delta = jnp.sum(out_grad.astype(f32) * outputs.astype(f32), axis=2)
    stats = jnp.stack([(logsumexp * LOG2E).T.reshape(-1), delta.reshape(-1)])
    sides = []
    for x in (queries.reshape(cols, dh), out_grad.reshape(cols, dh), stats):
        sides.append((x, swap(x, "core", NCORE, 1)))
    near, far = zip(*sides)

    pair = shape((2 * BLK, wide), bf16)
    sends = call(select_kernel, (pair,) * 4, (plan, *column), "select")
    kvs = [sends[0]] + [swap(sends[m], "y", NY, m) for m in (1, 2, 3)]
    token = jnp.zeros((8, LANES), f32)
    parts, dss = [None] * 4, [None] * 4
    for m in ORDER:
        parts[m], dss[m], token = call(
            functools.partial(class_kernel, m=m),
            (shape((2 * BLK, wide), f32 if m == 0 else bf16), shape((2 * BLK, cols), bf16), shape((8, LANES), f32)),
            (plan, *near, *far, span, kvs[m], token), "class" + str(m),
            flops=0, moved=1 << 12,
        )
    back = [parts[0]] + [swap(parts[m], "y", NY, m) for m in (1, 2, 3)]
    mine, theirs, token = call(
        query_kernel, (shape((cols, dh), f32), shape((cols, dh), bf16), shape((8, LANES), f32)),
        (*kvs, *dss, token), "query", scratch=[pltpu.VMEM((dh, 4 * BLK), bf16)],
        flops=0, moved=1<<12,
    )
    grad_q = call(join_kernel, shape((cols, dh), bf16), (mine, swap(theirs, "core", NCORE, 1)), "join", moved=1 << 21)

    total = call(
        total_kernel, shape((ZL, BLK, wide), bf16), (plan, *back, token), "total",
        scratch=[pltpu.VMEM((ZL, BLK, wide), f32)],
    )
    share = BLK // KVH
    moved = lax.all_to_all(
        total.reshape(ZL * KVH, share, wide), ("zl", "x", "zh"), split_axis=0, concat_axis=0, tiled=True
    )
    out = shape((share, KVH * dh), bf16)
    grad_keys, grad_values = call(finish_kernel, (out, out), (moved,), "finish")
    return grad_q.reshape(rows, heads, dh), grad_keys, grad_values


def solution(mesh):
    fine = Mesh(mesh.devices.reshape(ZL, NY, NCORE, NX, ZH), ("zl", "y", "core", "x", "zh"))
    ctx, kv = ("zl", "y", "core"), ("x", "zh")
    in_specs = (P(ctx, kv, None),) * 5 + (P(kv, ctx), P(), P())
    out_specs = (P(ctx, kv, None), P(ctx + kv, None), P(ctx + kv, None))
    return jax.shard_map(local, mesh=fine, in_specs=in_specs, out_specs=out_specs, check_vma=False)
```

time: 67.6 us -> 57.4 us (0.85)
  waiting for transfers between devices: 22.4 us -> 16.2 us
  local copies, waits for them, and re-layouts: 6.22 us -> 0.82 us
  Pallas kernels: 8.88 us -> 11.3 us
    ppermute x11 -> x13, waiting for transfers between devices: 16.3 us -> 5.87 us  [swap(): return lax.ppermute(x, axis, [(i, i ^ mask) for i in range(size)])]
    unnamed x30 -> x10, local copies, waits for them, and re-layouts: 5.94 us -> 0.54 us
    all_to_all x1, waiting for transfers between devices: 6.09 us -> 10.3 us  [local(): lax.all_to_all(total.reshape(ZL * KVH, share, wide), ('zl', 'x', 'zh'), s...]
    pallas_call x9 -> x10, Pallas kernels: 8.88 us -> 11.3 us  [call(): pl.pallas_call(body, out_shape=outs, in_specs=specs or [VMEM] * len(input...]
    another operation x2 -> x0, other arithmetic: 0.88 us -> none  [local(): theirs = swap(jnp.stack(column), 'core', NCORE, 1)]
    concatenate x0 -> x1, other arithmetic: none -> 0.79 us  [local(): own = jnp.concatenate([keys[:, 0, :], values[:, 0, :]], axis=1)]
    convert_element_type x1 -> x0, other arithmetic: 0.78 us -> none  [local(): mine = (keep + swap(send, 'core', NCORE, 1).astype(f32)).astype(bf16)]
    all_to_all x1, starting transfers between devices: 11.9 us -> 11.1 us  [local(): lax.all_to_all(total.reshape(ZL * KVH, share, wide), ('zl', 'x', 'zh'), s...]
  transfers between devices with their start and end apart: 12 -> 14, of which waited for: 8 -> 4; matrix products, arithmetic and copies ran while one was open for 3% -> 3% of each run, Pallas kernels for 11% -> 19%
where the time goes in v5:
time: 57.4 us; the launch traced here: 57.1 us
  starting transfers between devices  25.4 us (44%)
  waiting for transfers between devices  16.2 us (28%)
  Pallas kernels  11.3 us (20%)
  other arithmetic  2.44 us (4%)
  between operations  0.83 us (1%)
  local copies, waits for them, and re-layouts  0.82 us (1%)
    ppermute x13, starting transfers between devices, swap(): return lax.ppermute(x, axis, [(i, i ^ mask) for i in range(size)])  14.4 us
    pallas_call x10, Pallas kernels, call(): pl.pallas_call(body, out_shape=outs, in_specs=specs or [VMEM] * len(input...  11.3 us
    all_to_all x1, starting transfers between devices, local(): lax.all_to_all(total.reshape(ZL * KVH, share, wide), ('zl', 'x', 'zh'), s...  11.1 us
    all_to_all x1, waiting for transfers between devices, local(): lax.all_to_all(total.reshape(ZL * KVH, share, wide), ('zl', 'x', 'zh'), s...  10.3 us
    ppermute x13, waiting for transfers between devices, swap(): return lax.ppermute(x, axis, [(i, i ^ mask) for i in range(size)])  5.87 us
    reduce_sum x1, other arithmetic, local(): delta = jnp.sum(out_grad.astype(f32) * outputs.astype(f32), axis=2)  1.63 us
  transfers between devices with their start and end apart: 14, of which 4 were waited for; matrix products, arithmetic and copies ran while one was open for 3% of the time, Pallas kernels for 19%

profile of v5, /device:TPU:32, one launch (start us, length us, event | category | flops | bytes accessed | tf_op | source)
XLA Modules:
  0.0 57.1 jit_solution(11148295074947756548)
XLA Ops:
  0.6 0.8 %pad_maximum_fusion.own = bf16[128,256]{1,0:T(8,128)(2,1)S(1)} fusion(bf16[128,128]{1,0:T(8,128)(2,1)} %bitcast.19, bf16[128,128]{1,0:T(8,128)(2,1)} %bitcast.20), kind=kLoop, calls=%fused_computation.1 | loop fusion | flops 131072 | bytes 131072 | tf_op jit(solution)/shard_map/concatenate | solution.py:166
  1.4 2.0 %collective-permute-start.2 = (bf16[128,256]{1,0:T(8,128)(2,1)S(1)}, bf16[128,256]{1,0:T(8,128)(2,1)S(1)}, u32[]{:S(2)}, u32[]{:S(2)}) collective-permute-start(bf16[128,256]{1,0:T(8,128)(2,1)S(1)} %pad_maximum_fusion.own), channel_id=1, source_target_pairs={{0,192},{64,128},{128,64},{192,0},{1,193},{65,129},{129,65},{193,1... | collective-permute-start | bytes 196616 | tf_op jit(solution)/shard_map/ppermute | solution.py:156
  3.4 2.3 %collective-permute-start.1 = (bf16[128,256]{1,0:T(8,128)(2,1)S(1)}, bf16[128,256]{1,0:T(8,128)(2,1)S(1)}, u32[]{:S(2)}, u32[]{:S(2)}) collective-permute-start(bf16[128,256]{1,0:T(8,128)(2,1)S(1)} %pad_maximum_fusion.own), channel_id=1, source_target_pairs={{0,128},{64,192},{128,0},{192,64},{1,129},{65,193},{129,1},{193,65... | collective-permute-start | bytes 196616 | tf_op jit(solution)/shard_map/ppermute | solution.py:156
  5.7 0.5 collective-permute-start
  6.3 0.5 collective-permute-start.7
  6.8 0.1 copy.12
  6.9 0.1 stack_reshape.6
  7.0 1.6 %multiply_reduce_fusion = f32[128,16]{1,0:T(8,128)S(1)} fusion(bf16[128,16,128]{2,1,0:T(8,128)(2,1)} %param.11, bf16[128,16,128]{2,1,0:T(8,128)(2,1)} %param.12), kind=kLoop, calls=%fused_computation | loop fusion | flops 1046528 | bytes 1056768 | tf_op jit(solution)/shard_map/reduce_sum | solution.py:173
  8.6 0.1 stack_reshape.7
  8.8 0.1 collective-permute-start.8
  8.9 0.5 copy-done.2
  9.4 0.7 %plan.1 = (s32[24,128]{1,0:T(8,128)S(1)}, s32[4,2048]{1,0:T(4,128)S(1)}) custom-call(s32[32]{0:T(128)S(1)} %copy-done.2, s32[12]{0:T(128)S(1)} %copy-done.3), custom_call_target="tpu_custom_call" | custom-call | bytes 262144 | tf_op jit(solution)/shard_map/plan/pallas_call | solution.py:27
  10.1 0.8 %collective-permute-done.col1 = bf16[128,256]{1,0:T(8,128)(2,1)S(1)} collective-permute-done((bf16[128,256]{1,0:T(8,128)(2,1)S(1)}, bf16[128,256]{1,0:T(8,128)(2,1)S(1)}, u32[]{:S(2)}, u32[]{:S(2)}) %collective-permute-start) | collective-permute-done | bytes 65568 | tf_op jit(solution)/shard_map/ppermute | solution.py:156
  10.9 0.1 select.1
  11.0 3.3 %collective-permute-start.4 = (bf16[256,256]{1,0:T(8,128)(2,1)S(1)}, bf16[256,256]{1,0:T(8,128)(2,1)S(1)}, u32[]{:S(2)}, u32[]{:S(2)}) collective-permute-start(bf16[256,256]{1,0:T(8,128)(2,1)S(1)} %get-tuple-element.29), channel_id=1, source_target_pairs={{0,32},{16,48},{32,0},{48,16},{1,33},{17,49},{33,1},{49,17},{2,34}... | collective-permute-start | bytes 393224 | tf_op jit(solution)/shard_map/ppermute | solution.py:156
  14.3 0.7 %collective-permute-start.3 = (bf16[256,256]{1,0:T(8,128)(2,1)S(1)}, bf16[256,256]{1,0:T(8,128)(2,1)S(1)}, u32[]{:S(2)}, u32[]{:S(2)}) collective-permute-start(bf16[256,256]{1,0:T(8,128)(2,1)S(1)} %get-tuple-element.28), channel_id=1, source_target_pairs={{0,16},{16,0},{32,48},{48,32},{1,17},{17,1},{33,49},{49,33},{2,18}... | collective-permute-start | bytes 393224 | tf_op jit(solution)/shard_map/ppermute | solution.py:156
  15.0 0.4 collective-permute-start.5
  15.4 1.6 %class0.1 = (f32[256,256]{1,0:T(8,128)S(1)}, bf16[256,2048]{1,0:T(8,128)(2,1)S(1)}, f32[8,128]{1,0:T(8,128)S(1)}) custom-call(s32[24,128]{1,0:T(8,128)S(1)} %get-tuple-element.26.plan, bf16[2048,128]{1,0:T(8,128)(2,1)S(1)} %bitcast.14, bf16[2048,128]{1,0:T(8,128)(2,1)S(1)} %bitcast.9, f32[2,2048]{1,0:T(2,128)S(1)} %pad_maximum_fusion.1.stats0, ...), custom_call_target="tpu_custom_call" | custom-call | bytes 4096 | tf_op jit(solution)/shard_map/class0/pallas_call | solution.py:27
  16.9 1.9 %collective-permute-done.4.kv.kv2 = bf16[256,256]{1,0:T(8,128)(2,1)S(1)} collective-permute-done((bf16[256,256]{1,0:T(8,128)(2,1)S(1)}, bf16[256,256]{1,0:T(8,128)(2,1)S(1)}, u32[]{:S(2)}, u32[]{:S(2)}) %collective-permute-start.4) | collective-permute-done | bytes 131104 | tf_op jit(solution)/shard_map/ppermute | solution.py:156
  18.8 1.6 %class2.1 = (bf16[256,256]{1,0:T(8,128)(2,1)S(1)}, bf16[256,2048]{1,0:T(8,128)(2,1)S(1)}, f32[8,128]{1,0:T(8,128)S(1)}) custom-call(s32[24,128]{1,0:T(8,128)S(1)} %get-tuple-element.26.plan, bf16[2048,128]{1,0:T(8,128)(2,1)S(1)} %bitcast.15, bf16[2048,128]{1,0:T(8,128)(2,1)S(1)} %bitcast.10, f32[2,2048]{1,0:T(2,128)S(1)} %pad_maximum_fusion.1.stats0, ...), custom_call_target="tpu_custom_call" | custom-call | bytes 4096 | tf_op jit(solution)/shard_map/class2/pallas_call | solution.py:27
  20.4 3.3 %collective-permute-start.11 = (bf16[256,256]{1,0:T(8,128)(2,1)S(1)}, bf16[256,256]{1,0:T(8,128)(2,1)S(1)}, u32[]{:S(2)}, u32[]{:S(2)}) collective-permute-start(bf16[256,256]{1,0:T(8,128)(2,1)S(1)} %get-tuple-element.44), channel_id=1, source_target_pairs={{0,32},{16,48},{32,0},{48,16},{1,33},{17,49},{33,1},{49,17},{2,34}... | collective-permute-start | bytes 393224 | tf_op jit(solution)/shard_map/ppermute | solution.py:156
  23.7 1.6 %class1.1 = (bf16[256,256]{1,0:T(8,128)(2,1)S(1)}, bf16[256,2048]{1,0:T(8,128)(2,1)S(1)}, f32[8,128]{1,0:T(8,128)S(1)}) custom-call(s32[24,128]{1,0:T(8,128)S(1)} %get-tuple-element.26.plan, bf16[2048,128]{1,0:T(8,128)(2,1)S(1)} %bitcast.16, bf16[2048,128]{1,0:T(8,128)(2,1)S(1)} %bitcast.11, f32[2,2048]{1,0:T(2,128)S(1)} %pad_maximum_fusion.1.stats0, ...), custom_call_target="tpu_custom_call" | custom-call | bytes 4096 | tf_op jit(solution)/shard_map/class1/pallas_call | solution.py:27
  25.3 1.6 %class3.1 = (bf16[256,256]{1,0:T(8,128)(2,1)S(1)}, bf16[256,2048]{1,0:T(8,128)(2,1)S(1)}, f32[8,128]{1,0:T(8,128)S(1)}) custom-call(s32[24,128]{1,0:T(8,128)S(1)} %get-tuple-element.26.plan, bf16[2048,128]{1,0:T(8,128)(2,1)S(1)} %bitcast.17, bf16[2048,128]{1,0:T(8,128)(2,1)S(1)} %bitcast.12, f32[2,2048]{1,0:T(2,128)S(1)} %pad_maximum_fusion.1.stats0, ...), custom_call_target="tpu_custom_call" | custom-call | bytes 4096 | tf_op jit(solution)/shard_map/class3/pallas_call | solution.py:27
  26.8 1.2 %collective-permute-start.12 = (bf16[256,256]{1,0:T(8,128)(2,1)S(1)}, bf16[256,256]{1,0:T(8,128)(2,1)S(1)}, u32[]{:S(2)}, u32[]{:S(2)}) collective-permute-start(bf16[256,256]{1,0:T(8,128)(2,1)S(1)} %get-tuple-element.45), channel_id=1, source_target_pairs={{0,48},{16,32},{32,16},{48,0},{1,49},{17,33},{33,17},{49,1},{2,50}... | collective-permute-start | bytes 393224 | tf_op jit(solution)/shard_map/ppermute | solution.py:156
  28.0 1.8 %query.1 = (f32[2048,128]{1,0:T(8,128)S(1)}, bf16[2048,128]{1,0:T(8,128)(2,1)S(1)}, f32[8,128]{1,0:T(8,128)S(1)}) custom-call(bf16[256,256]{1,0:T(8,128)(2,1)S(1)} %get-tuple-element.27.kv.kv0, bf16[256,256]{1,0:T(8,128)(2,1)S(1)} %collective-permute-done.3.kv.kv1, bf16[256,256]{1,0:T(8,128)(2,1)S(1)} %collective-permute-done.4.kv.kv2, ...), custom_call_target="tpu_custom_call" | custom-call | bytes 4096 | tf_op jit(solution)/shard_map/query/pallas_call | solution.py:27
  29.8 0.1 collective-permute-start.9
  29.9 3.2 %collective-permute-done.12.part3 = bf16[256,256]{1,0:T(8,128)(2,1)S(1)} collective-permute-done((bf16[256,256]{1,0:T(8,128)(2,1)S(1)}, bf16[256,256]{1,0:T(8,128)(2,1)S(1)}, u32[]{:S(2)}, u32[]{:S(2)}) %collective-permute-start.12) | collective-permute-done | bytes 131104 | tf_op jit(solution)/shard_map/ppermute | solution.py:156
  33.1 1.0 %total.1 = bf16[4,128,256]{2,1,0:T(8,128)(2,1)} custom-call(s32[24,128]{1,0:T(8,128)S(1)} %get-tuple-element.26.plan, f32[256,256]{1,0:T(8,128)S(1)} %get-tuple-element.42.part0, bf16[256,256]{1,0:T(8,128)(2,1)S(1)} %collective-permute-done.10.part1, bf16[256,256]{1,0:T(8,128)(2,1)S(1)} %collective-permute-done.11.part2, ...), custom_call_target="tpu_custom_call" | custom-call | bytes 262144 | tf_op jit(solution)/shard_map/total/pallas_call | solution.py:27
  34.1 11.1 %all-to-all-start = ((bf16[32,16,256]{2,1,0:T(8,128)(2,1)}), bf16[32,16,256]{2,1,0:T(8,128)(2,1)S(1)}, u32[]{:S(2)}, u32[]{:S(2)}) async-start(bf16[32,16,256]{2,1,0:T(8,128)(2,1)} %bitcast.6), calls=%async_computation | async-start | bytes 524288 | tf_op jit(solution)/shard_map/all_to_all | solution.py:205
  45.2 0.9 %join.1 = bf16[2048,128]{1,0:T(8,128)(2,1)} custom-call(f32[2048,128]{1,0:T(8,128)S(1)} %get-tuple-element.40.mine, bf16[2048,128]{1,0:T(8,128)(2,1)S(1)} %collective-permute-done.9.theirs), custom_call_target="tpu_custom_call" | custom-call | bytes 2097152 | tf_op jit(solution)/shard_map/join/pallas_call | solution.py:27
  46.1 10.3 %all-to-all-done.moved = bf16[32,16,256]{2,1,0:T(8,128)(2,1)S(1)} async-done(((bf16[32,16,256]{2,1,0:T(8,128)(2,1)}), bf16[32,16,256]{2,1,0:T(8,128)(2,1)S(1)}, u32[]{:S(2)}, u32[]{:S(2)}) %all-to-all-start) | async-done | bytes 262176 | tf_op jit(solution)/shard_map/all_to_all | solution.py:205
  56.4 0.7 %finish.1 = (bf16[16,1024]{1,0:T(8,128)(2,1)}, bf16[16,1024]{1,0:T(8,128)(2,1)}) custom-call(bf16[32,16,256]{2,1,0:T(8,128)(2,1)S(1)} %all-to-all-done.moved), custom_call_target="tpu_custom_call" | custom-call | bytes 262144 | tf_op jit(solution)/shard_map/finish/pallas_call | solution.py:27
  (24 shorter events, 0.1 us)
Async XLA Ops:
  0.6 6.1 %copy-start.4 = (f32[16,128]{1,0:T(8,128)S(1)}, f32[16,128]{1,0:T(8,128)}, u32[]{:S(2)}) copy-start(f32[16,128]{1,0:T(8,128)} %param.13) | copy-start | bytes 24580
  1.4 7.3 %collective-permute-start.2 = (bf16[128,256]{1,0:T(8,128)(2,1)S(1)}, bf16[128,256]{1,0:T(8,128)(2,1)S(1)}, u32[]{:S(2)}, u32[]{:S(2)}) collective-permute-start(bf16[128,256]{1,0:T(8,128)(2,1)S(1)} %pad_maximum_fusion.own), channel_id=1, source_target_pairs={{0,192},{64,128},{128,64},{192,0},{1,193},{65,129},{129,65},{193,1... | collective-permute-start | bytes 196616 | tf_op jit(solution)/shard_map/ppermute | solution.py:156
  3.4 6.7 %collective-permute-start.1 = (bf16[128,256]{1,0:T(8,128)(2,1)S(1)}, bf16[128,256]{1,0:T(8,128)(2,1)S(1)}, u32[]{:S(2)}, u32[]{:S(2)}) collective-permute-start(bf16[128,256]{1,0:T(8,128)(2,1)S(1)} %pad_maximum_fusion.own), channel_id=1, source_target_pairs={{0,128},{64,192},{128,0},{192,64},{1,129},{65,193},{129,1},{193,65... | collective-permute-start | bytes 196616 | tf_op jit(solution)/shard_map/ppermute | solution.py:156
  5.7 5.2 %collective-permute-start = (bf16[128,256]{1,0:T(8,128)(2,1)S(1)}, bf16[128,256]{1,0:T(8,128)(2,1)S(1)}, u32[]{:S(2)}, u32[]{:S(2)}) collective-permute-start(bf16[128,256]{1,0:T(8,128)(2,1)S(1)} %pad_maximum_fusion.own), channel_id=1, source_target_pairs={{0,64},{64,0},{128,192},{192,128},{1,65},{65,1},{129,193},{193,129... | collective-permute-start | bytes 196616 | tf_op jit(solution)/shard_map/ppermute | solution.py:156
  6.2 9.1 %collective-permute-start.6 = (bf16[2048,128]{1,0:T(8,128)(2,1)}, bf16[2048,128]{1,0:T(8,128)(2,1)S(1)}, u32[]{:S(2)}, u32[]{:S(2)}) collective-permute-start(bf16[2048,128]{1,0:T(8,128)(2,1)} %bitcast.13), channel_id=1, source_target_pairs={{0,8},{8,0},{1,9},{9,1},{2,10},{10,2},{3,11},{11,3},{4,12},{12,4},... | collective-permute-start | bytes 1572872 | tf_op jit(solution)/shard_map/ppermute | solution.py:156
  6.3 9.1 %collective-permute-start.7 = (bf16[2048,128]{1,0:T(8,128)(2,1)}, bf16[2048,128]{1,0:T(8,128)(2,1)S(1)}, u32[]{:S(2)}, u32[]{:S(2)}) collective-permute-start(bf16[2048,128]{1,0:T(8,128)(2,1)} %bitcast.8), channel_id=1, source_target_pairs={{0,8},{8,0},{1,9},{9,1},{2,10},{10,2},{3,11},{11,3},{4,12},{12,4},... | collective-permute-start | bytes 1572872 | tf_op jit(solution)/shard_map/ppermute | solution.py:156
  7.0 8.4 %copy-start = (bf16[128,16,128]{2,1,0:T(8,128)(2,1)S(1)}, bf16[128,16,128]{2,1,0:T(8,128)(2,1)}, u32[]{:S(2)}) copy-start(bf16[128,16,128]{2,1,0:T(8,128)(2,1)} %param.12) | copy-start | bytes 1572868
  7.0 8.4 %copy-start.1 = (bf16[128,16,128]{2,1,0:T(8,128)(2,1)S(1)}, bf16[128,16,128]{2,1,0:T(8,128)(2,1)}, u32[]{:S(2)}) copy-start(bf16[128,16,128]{2,1,0:T(8,128)(2,1)} %param.8) | copy-start | bytes 1572868
  8.7 0.7 %copy-start.2 = (s32[32]{0:T(128)S(1)}, s32[32]{0:T(128)}, u32[]{:S(2)}) copy-start(s32[32]{0:T(128)} %order.1) | copy-start | bytes 388
  8.7 0.7 %copy-start.3 = (s32[12]{0:T(128)S(1)}, s32[12]{0:T(128)}, u32[]{:S(2)}) copy-start(s32[12]{0:T(128)} %lengths.1) | copy-start | bytes 148
  8.8 6.2 %collective-permute-start.8 = (f32[2,2048]{1,0:T(2,128)S(1)}, f32[2,2048]{1,0:T(2,128)S(1)}, u32[]{:S(2)}, u32[]{:S(2)}) collective-permute-start(f32[2,2048]{1,0:T(2,128)S(1)} %pad_maximum_fusion.1.stats0), channel_id=1, source_target_pairs={{0,8},{8,0},{1,9},{9,1},{2,10},{10,2},{3,11},{11,3},{4,12},{12,4},... | collective-permute-start | bytes 49160 | tf_op jit(solution)/shard_map/ppermute | solution.py:156
  11.0 7.8 %collective-permute-start.4 = (bf16[256,256]{1,0:T(8,128)(2,1)S(1)}, bf16[256,256]{1,0:T(8,128)(2,1)S(1)}, u32[]{:S(2)}, u32[]{:S(2)}) collective-permute-start(bf16[256,256]{1,0:T(8,128)(2,1)S(1)} %get-tuple-element.29), channel_id=1, source_target_pairs={{0,32},{16,48},{32,0},{48,16},{1,33},{17,49},{33,1},{49,17},{2,34}... | collective-permute-start | bytes 393224 | tf_op jit(solution)/shard_map/ppermute | solution.py:156
  14.3 9.4 %collective-permute-start.3 = (bf16[256,256]{1,0:T(8,128)(2,1)S(1)}, bf16[256,256]{1,0:T(8,128)(2,1)S(1)}, u32[]{:S(2)}, u32[]{:S(2)}) collective-permute-start(bf16[256,256]{1,0:T(8,128)(2,1)S(1)} %get-tuple-element.28), channel_id=1, source_target_pairs={{0,16},{16,0},{32,48},{48,32},{1,17},{17,1},{33,49},{49,33},{2,18}... | collective-permute-start | bytes 393224 | tf_op jit(solution)/shard_map/ppermute | solution.py:156
  15.0 10.3 %collective-permute-start.5 = (bf16[256,256]{1,0:T(8,128)(2,1)S(1)}, bf16[256,256]{1,0:T(8,128)(2,1)S(1)}, u32[]{:S(2)}, u32[]{:S(2)}) collective-permute-start(bf16[256,256]{1,0:T(8,128)(2,1)S(1)} %get-tuple-element.30), channel_id=1, source_target_pairs={{0,48},{16,32},{32,16},{48,0},{1,49},{17,33},{33,17},{49,1},{2,50}... | collective-permute-start | bytes 393224 | tf_op jit(solution)/shard_map/ppermute | solution.py:156
  20.4 9.5 %collective-permute-start.11 = (bf16[256,256]{1,0:T(8,128)(2,1)S(1)}, bf16[256,256]{1,0:T(8,128)(2,1)S(1)}, u32[]{:S(2)}, u32[]{:S(2)}) collective-permute-start(bf16[256,256]{1,0:T(8,128)(2,1)S(1)} %get-tuple-element.44), channel_id=1, source_target_pairs={{0,32},{16,48},{32,0},{48,16},{1,33},{17,49},{33,1},{49,17},{2,34}... | collective-permute-start | bytes 393224 | tf_op jit(solution)/shard_map/ppermute | solution.py:156
  26.8 6.3 %collective-permute-start.12 = (bf16[256,256]{1,0:T(8,128)(2,1)S(1)}, bf16[256,256]{1,0:T(8,128)(2,1)S(1)}, u32[]{:S(2)}, u32[]{:S(2)}) collective-permute-start(bf16[256,256]{1,0:T(8,128)(2,1)S(1)} %get-tuple-element.45), channel_id=1, source_target_pairs={{0,48},{16,32},{32,16},{48,0},{1,49},{17,33},{33,17},{49,1},{2,50}... | collective-permute-start | bytes 393224 | tf_op jit(solution)/shard_map/ppermute | solution.py:156
  28.0 5.1 %collective-permute-start.10 = (bf16[256,256]{1,0:T(8,128)(2,1)S(1)}, bf16[256,256]{1,0:T(8,128)(2,1)S(1)}, u32[]{:S(2)}, u32[]{:S(2)}) collective-permute-start(bf16[256,256]{1,0:T(8,128)(2,1)S(1)} %get-tuple-element.43), channel_id=1, source_target_pairs={{0,16},{16,0},{32,48},{48,32},{1,17},{17,1},{33,49},{49,33},{2,18}... | collective-permute-start | bytes 393224 | tf_op jit(solution)/shard_map/ppermute | solution.py:156
  29.8 15.4 %collective-permute-start.9 = (bf16[2048,128]{1,0:T(8,128)(2,1)S(1)}, bf16[2048,128]{1,0:T(8,128)(2,1)S(1)}, u32[]{:S(2)}, u32[]{:S(2)}) collective-permute-start(bf16[2048,128]{1,0:T(8,128)(2,1)S(1)} %get-tuple-element.41), channel_id=1, source_target_pairs={{0,8},{8,0},{1,9},{9,1},{2,10},{10,2},{3,11},{11,3},{4,12},{12,4},... | collective-permute-start | bytes 1572872 | tf_op jit(solution)/shard_map/ppermute | solution.py:156
  34.1 22.3 %all-to-all-start = ((bf16[32,16,256]{2,1,0:T(8,128)(2,1)}), bf16[32,16,256]{2,1,0:T(8,128)(2,1)S(1)}, u32[]{:S(2)}, u32[]{:S(2)}) async-start(bf16[32,16,256]{2,1,0:T(8,128)(2,1)} %bitcast.6), calls=%async_computation | async-start | bytes 524288 | tf_op jit(solution)/shard_map/all_to_all | solution.py:205

commit v6 on v5

--- a/solution.py
+++ b/solution.py
@@ -67,6 +67,20 @@
             start = jnp.where(end <= pos, end, start)
         span_ref[2 * j : 2 * j + 1, :] = start
         span_ref[2 * j + 1 : 2 * j + 2, :] = pos
+
+
+def stats_kernel(outputs, out_grad, lse, stats):
+    rows, dh = outputs.shape
+    ones = jnp.ones((8, dh), jnp.bfloat16)
+    stats[0:1, :] = lse[...]
+    for c in range(rows // CHUNK):
+        cols = slice(c * CHUNK, (c + 1) * CHUNK)
+        product = outputs[cols, :].astype(jnp.float32) * out_grad[cols, :].astype(jnp.float32)
+        high = product.astype(jnp.bfloat16)
+        low = (product - high.astype(jnp.float32)).astype(jnp.bfloat16)
+        delta = lax.dot_general(ones, high, NT, preferred_element_type=jnp.float32)
+        delta += lax.dot_general(ones, low, NT, preferred_element_type=jnp.float32)
+        stats[1:2, cols] = delta[0:1, :]
 
 
 def select_kernel(plan, own, col1, col2, col3, *outs):
@@ -139,15 +153,16 @@
             row = WANT + 2 * m + j
             z = jnp.max(plan[row : row + 1, :])
             acc[z] += part[j * BLK : (j + 1) * BLK, :].astype(jnp.float32)
-    out[...] = acc[...].astype(out.dtype)
+    for z in range(ZL):
+        out[:, z] = acc[z].reshape(KVH, BLK // KVH, acc.shape[2]).astype(out.dtype)
 
 
 def finish_kernel(moved, gk_ref, gv_ref):
     dh = moved.shape[2] // 2
     for k in range(KVH):
-        grad = moved[k].astype(jnp.float32)
+        grad = moved[k * ZL].astype(jnp.float32)
         for z in range(1, ZL):
-            grad += moved[z * KVH + k].astype(jnp.float32)
+            grad += moved[k * ZL + z].astype(jnp.float32)
         gk_ref[:, k * dh : (k + 1) * dh] = grad[:, :dh].astype(gk_ref.dtype)
         gv_ref[:, k * dh : (k + 1) * dh] = grad[:, dh:].astype(gv_ref.dtype)
 
@@ -170,8 +185,10 @@
         (shape((24, LANES), jnp.int32), shape((4, cols), jnp.int32)),
         (block_order, doc_lengths), "plan", specs=[SMEM, SMEM],
     )
-    delta = jnp.sum(out_grad.astype(f32) * outputs.astype(f32), axis=2)
-    stats = jnp.stack([(logsumexp * LOG2E).T.reshape(-1), delta.reshape(-1)])
+    stats = call(
+        stats_kernel, shape((2, cols), f32),
+        (outputs.reshape(cols, dh), out_grad.reshape(cols, dh), (logsumexp * LOG2E).T.reshape(1, cols)), "stats",
+    )
     sides = []
     for x in (queries.reshape(cols, dh), out_grad.reshape(cols, dh), stats):
         sides.append((x, swap(x, "core", NCORE, 1)))
@@ -198,12 +215,12 @@
     grad_q = call(join_kernel, shape((cols, dh), bf16), (mine, swap(theirs, "core", NCORE, 1)), "join", moved=1 << 21)
 
     total = call(
-        total_kernel, shape((ZL, BLK, wide), bf16), (plan, *back, token), "total",
+        total_kernel, shape((KVH, ZL, BLK // KVH, wide), bf16), (plan, *back, token), "total",
         scratch=[pltpu.VMEM((ZL, BLK, wide), f32)],
     )
     share = BLK // KVH
     moved = lax.all_to_all(
-        total.reshape(ZL * KVH, share, wide), ("zl", "x", "zh"), split_axis=0, concat_axis=0, tiled=True
+        total.reshape(ZL * KVH, share, wide), ("x", "zh", "zl"), split_axis=0, concat_axis=0, tiled=True
     )
     out = shape((share, KVH * dh), bf16)
     grad_keys, grad_values = call(finish_kernel, (out, out), (moved,), "finish")

time: 57.4 us -> 57.9 us (level)
  other arithmetic: 2.44 us -> 0.8 us
  local copies, waits for them, and re-layouts: 0.82 us -> 2.41 us
  Pallas kernels: 11.3 us -> 11.9 us
    unnamed x10 -> x14, local copies, waits for them, and re-layouts: 0.54 us -> 2.21 us
    reduce_sum x1 -> x0, other arithmetic: 1.63 us -> none  [local(): delta = jnp.sum(out_grad.astype(f32) * outputs.astype(f32), axis=2)]
    pallas_call x10 -> x11, Pallas kernels: 11.3 us -> 11.9 us  [call(): pl.pallas_call(body, out_shape=outs, in_specs=specs or [VMEM] * len(input...]
  transfers between devices with their start and end apart: 14 -> 14, of which waited for: 4 -> 4; matrix products, arithmetic and copies ran while one was open for 3% -> 2% of each run, Pallas kernels for 19% -> 20%
where the time goes in v6:
time: 57.9 us; the launch traced here: 57.6 us
  starting transfers between devices  25.1 us (43%)
  waiting for transfers between devices  16.5 us (28%)
  Pallas kernels  11.9 us (21%)
  local copies, waits for them, and re-layouts  2.41 us (4%)
  other arithmetic  0.8 us (1%)
  between operations  0.8 us (1%)
    ppermute x13, starting transfers between devices, swap(): return lax.ppermute(x, axis, [(i, i ^ mask) for i in range(size)])  14.3 us
    pallas_call x11, Pallas kernels, call(): pl.pallas_call(body, out_shape=outs, in_specs=specs or [VMEM] * len(input...  11.9 us
    all_to_all x1, starting transfers between devices, local(): lax.all_to_all(total.reshape(ZL * KVH, share, wide), ('x', 'zh', 'zl'), s...  10.8 us
    all_to_all x1, waiting for transfers between devices, local(): lax.all_to_all(total.reshape(ZL * KVH, share, wide), ('x', 'zh', 'zl'), s...  10.2 us
    ppermute x13, waiting for transfers between devices, swap(): return lax.ppermute(x, axis, [(i, i ^ mask) for i in range(size)])  6.38 us
    unnamed x14, local copies, waits for them, and re-layouts  2.21 us
  transfers between devices with their start and end apart: 14, of which 4 were waited for; matrix products, arithmetic and copies ran while one was open for 2% of the time, Pallas kernels for 20%

profile of v6, /device:TPU:32, one launch (start us, length us, event | category | flops | bytes accessed | tf_op | source)
XLA Modules:
  0.0 57.6 jit_solution(15227284789935139987)
XLA Ops:
  0.6 0.1 collective-permute-start.6
  0.7 0.5 collective-permute-start.7
  1.2 0.8 %pad_maximum_fusion.own = bf16[128,256]{1,0:T(8,128)(2,1)S(1)} fusion(bf16[128,128]{1,0:T(8,128)(2,1)} %bitcast.22, bf16[128,128]{1,0:T(8,128)(2,1)} %bitcast.23), kind=kLoop, calls=%fused_computation | loop fusion | flops 131072 | bytes 131072 | tf_op jit(solution)/shard_map/concatenate | solution.py:181
  2.0 2.0 %collective-permute-start.2 = (bf16[128,256]{1,0:T(8,128)(2,1)S(1)}, bf16[128,256]{1,0:T(8,128)(2,1)S(1)}, u32[]{:S(2)}, u32[]{:S(2)}) collective-permute-start(bf16[128,256]{1,0:T(8,128)(2,1)S(1)} %pad_maximum_fusion.own), channel_id=1, source_target_pairs={{0,192},{64,128},{128,64},{192,0},{1,193},{65,129},{129,65},{193,1... | collective-permute-start | bytes 196616 | tf_op jit(solution)/shard_map/ppermute | solution.py:171
  4.0 2.3 %collective-permute-start.1 = (bf16[128,256]{1,0:T(8,128)(2,1)S(1)}, bf16[128,256]{1,0:T(8,128)(2,1)S(1)}, u32[]{:S(2)}, u32[]{:S(2)}) collective-permute-start(bf16[128,256]{1,0:T(8,128)(2,1)S(1)} %pad_maximum_fusion.own), channel_id=1, source_target_pairs={{0,128},{64,192},{128,0},{192,64},{1,129},{65,193},{129,1},{193,65... | collective-permute-start | bytes 196616 | tf_op jit(solution)/shard_map/ppermute | solution.py:171
  6.3 0.5 collective-permute-start
  6.9 0.1 copy.12
  7.1 1.0 %copy-done = bf16[128,16,128]{2,1,0:T(8,128)(2,1)S(1)} copy-done((bf16[128,16,128]{2,1,0:T(8,128)(2,1)S(1)}, bf16[128,16,128]{2,1,0:T(8,128)(2,1)}, u32[]{:S(2)}) %copy-start) | copy-done | bytes 524312
  8.1 1.0 %copy-done.3 = bf16[128,16,128]{2,1,0:T(8,128)(2,1)S(1)} copy-done((bf16[128,16,128]{2,1,0:T(8,128)(2,1)S(1)}, bf16[128,16,128]{2,1,0:T(8,128)(2,1)}, u32[]{:S(2)}) %copy-start.3) | copy-done | bytes 524312
  9.1 0.4 stats.1.stats0
  9.6 0.1 collective-permute-start.8
  9.7 0.1 copy-done.4
  9.8 0.7 %plan.1 = (s32[24,128]{1,0:T(8,128)S(1)}, s32[4,2048]{1,0:T(4,128)S(1)}) custom-call(s32[32]{0:T(128)S(1)} %copy-done.4, s32[12]{0:T(128)S(1)} %copy-done.5), custom_call_target="tpu_custom_call" | custom-call | bytes 262144 | tf_op jit(solution)/shard_map/plan/pallas_call | solution.py:27
  10.5 1.3 %collective-permute-done.col1 = bf16[128,256]{1,0:T(8,128)(2,1)S(1)} collective-permute-done((bf16[128,256]{1,0:T(8,128)(2,1)S(1)}, bf16[128,256]{1,0:T(8,128)(2,1)S(1)}, u32[]{:S(2)}, u32[]{:S(2)}) %collective-permute-start) | collective-permute-done | bytes 65568 | tf_op jit(solution)/shard_map/ppermute | solution.py:171
  11.9 3.3 %collective-permute-start.4 = (bf16[256,256]{1,0:T(8,128)(2,1)S(1)}, bf16[256,256]{1,0:T(8,128)(2,1)S(1)}, u32[]{:S(2)}, u32[]{:S(2)}) collective-permute-start(bf16[256,256]{1,0:T(8,128)(2,1)S(1)} %get-tuple-element.29), channel_id=1, source_target_pairs={{0,32},{16,48},{32,0},{48,16},{1,33},{17,49},{33,1},{49,17},{2,34}... | collective-permute-start | bytes 393224 | tf_op jit(solution)/shard_map/ppermute | solution.py:171
  15.1 0.7 %collective-permute-start.3 = (bf16[256,256]{1,0:T(8,128)(2,1)S(1)}, bf16[256,256]{1,0:T(8,128)(2,1)S(1)}, u32[]{:S(2)}, u32[]{:S(2)}) collective-permute-start(bf16[256,256]{1,0:T(8,128)(2,1)S(1)} %get-tuple-element.28), channel_id=1, source_target_pairs={{0,16},{16,0},{32,48},{48,32},{1,17},{17,1},{33,49},{49,33},{2,18}... | collective-permute-start | bytes 393224 | tf_op jit(solution)/shard_map/ppermute | solution.py:171
  15.8 0.4 collective-permute-start.5
  16.2 1.6 %class0.1 = (f32[256,256]{1,0:T(8,128)S(1)}, bf16[256,2048]{1,0:T(8,128)(2,1)S(1)}, f32[8,128]{1,0:T(8,128)S(1)}) custom-call(s32[24,128]{1,0:T(8,128)S(1)} %get-tuple-element.26.plan, bf16[2048,128]{1,0:T(8,128)(2,1)S(1)} %bitcast.16, bf16[2048,128]{1,0:T(8,128)(2,1)S(1)} %bitcast.11, f32[2,2048]{1,0:T(2,128)S(1)} %stats.1.stats0, ...), custom_call_target="tpu_custom_call" | custom-call | bytes 4096 | tf_op jit(solution)/shard_map/class0/pallas_call | solution.py:27
  17.8 1.9 %collective-permute-done.4.kv.kv2 = bf16[256,256]{1,0:T(8,128)(2,1)S(1)} collective-permute-done((bf16[256,256]{1,0:T(8,128)(2,1)S(1)}, bf16[256,256]{1,0:T(8,128)(2,1)S(1)}, u32[]{:S(2)}, u32[]{:S(2)}) %collective-permute-start.4) | collective-permute-done | bytes 131104 | tf_op jit(solution)/shard_map/ppermute | solution.py:171
  19.8 1.6 %class2.1 = (bf16[256,256]{1,0:T(8,128)(2,1)S(1)}, bf16[256,2048]{1,0:T(8,128)(2,1)S(1)}, f32[8,128]{1,0:T(8,128)S(1)}) custom-call(s32[24,128]{1,0:T(8,128)S(1)} %get-tuple-element.26.plan, bf16[2048,128]{1,0:T(8,128)(2,1)S(1)} %bitcast.17, bf16[2048,128]{1,0:T(8,128)(2,1)S(1)} %bitcast.12, f32[2,2048]{1,0:T(2,128)S(1)} %stats.1.stats0, ...), custom_call_target="tpu_custom_call" | custom-call | bytes 4096 | tf_op jit(solution)/shard_map/class2/pallas_call | solution.py:27
  21.4 3.2 %collective-permute-start.11 = (bf16[256,256]{1,0:T(8,128)(2,1)S(1)}, bf16[256,256]{1,0:T(8,128)(2,1)S(1)}, u32[]{:S(2)}, u32[]{:S(2)}) collective-permute-start(bf16[256,256]{1,0:T(8,128)(2,1)S(1)} %get-tuple-element.44), channel_id=1, source_target_pairs={{0,32},{16,48},{32,0},{48,16},{1,33},{17,49},{33,1},{49,17},{2,34}... | collective-permute-start | bytes 393224 | tf_op jit(solution)/shard_map/ppermute | solution.py:171
  24.5 1.6 %class1.1 = (bf16[256,256]{1,0:T(8,128)(2,1)S(1)}, bf16[256,2048]{1,0:T(8,128)(2,1)S(1)}, f32[8,128]{1,0:T(8,128)S(1)}) custom-call(s32[24,128]{1,0:T(8,128)S(1)} %get-tuple-element.26.plan, bf16[2048,128]{1,0:T(8,128)(2,1)S(1)} %bitcast.18, bf16[2048,128]{1,0:T(8,128)(2,1)S(1)} %bitcast.13, f32[2,2048]{1,0:T(2,128)S(1)} %stats.1.stats0, ...), custom_call_target="tpu_custom_call" | custom-call | bytes 4096 | tf_op jit(solution)/shard_map/class1/pallas_call | solution.py:27
  26.1 1.6 %class3.1 = (bf16[256,256]{1,0:T(8,128)(2,1)S(1)}, bf16[256,2048]{1,0:T(8,128)(2,1)S(1)}, f32[8,128]{1,0:T(8,128)S(1)}) custom-call(s32[24,128]{1,0:T(8,128)S(1)} %get-tuple-element.26.plan, bf16[2048,128]{1,0:T(8,128)(2,1)S(1)} %bitcast.19, bf16[2048,128]{1,0:T(8,128)(2,1)S(1)} %bitcast.14, f32[2,2048]{1,0:T(2,128)S(1)} %stats.1.stats0, ...), custom_call_target="tpu_custom_call" | custom-call | bytes 4096 | tf_op jit(solution)/shard_map/class3/pallas_call | solution.py:27
  27.7 1.2 %collective-permute-start.12 = (bf16[256,256]{1,0:T(8,128)(2,1)S(1)}, bf16[256,256]{1,0:T(8,128)(2,1)S(1)}, u32[]{:S(2)}, u32[]{:S(2)}) collective-permute-start(bf16[256,256]{1,0:T(8,128)(2,1)S(1)} %get-tuple-element.45), channel_id=1, source_target_pairs={{0,48},{16,32},{32,16},{48,0},{1,49},{17,33},{33,17},{49,1},{2,50}... | collective-permute-start | bytes 393224 | tf_op jit(solution)/shard_map/ppermute | solution.py:171
  28.9 1.8 %query.1 = (f32[2048,128]{1,0:T(8,128)S(1)}, bf16[2048,128]{1,0:T(8,128)(2,1)S(1)}, f32[8,128]{1,0:T(8,128)S(1)}) custom-call(bf16[256,256]{1,0:T(8,128)(2,1)S(1)} %get-tuple-element.27.kv.kv0, bf16[256,256]{1,0:T(8,128)(2,1)S(1)} %collective-permute-done.3.kv.kv1, bf16[256,256]{1,0:T(8,128)(2,1)S(1)} %collective-permute-done.4.kv.kv2, ...), custom_call_target="tpu_custom_call" | custom-call | bytes 4096 | tf_op jit(solution)/shard_map/query/pallas_call | solution.py:27
  30.7 0.1 collective-permute-start.9
  30.8 3.2 %collective-permute-done.12.part3 = bf16[256,256]{1,0:T(8,128)(2,1)S(1)} collective-permute-done((bf16[256,256]{1,0:T(8,128)(2,1)S(1)}, bf16[256,256]{1,0:T(8,128)(2,1)S(1)}, u32[]{:S(2)}, u32[]{:S(2)}) %collective-permute-start.12) | collective-permute-done | bytes 131104 | tf_op jit(solution)/shard_map/ppermute | solution.py:171
  34.0 1.0 %total.1 = bf16[8,4,16,256]{3,2,1,0:T(8,128)(2,1)} custom-call(s32[24,128]{1,0:T(8,128)S(1)} %get-tuple-element.26.plan, f32[256,256]{1,0:T(8,128)S(1)} %get-tuple-element.42.part0, bf16[256,256]{1,0:T(8,128)(2,1)S(1)} %collective-permute-done.10.part1, bf16[256,256]{1,0:T(8,128)(2,1)S(1)} %collective-permute-done.11.part2, ...), custom_call_target="tpu_custom_call" | custom-call | bytes 262144 | tf_op jit(solution)/shard_map/total/pallas_call | solution.py:27
  35.0 10.8 %all-to-all-start = ((bf16[32,16,256]{2,1,0:T(8,128)(2,1)}), bf16[32,16,256]{2,1,0:T(8,128)(2,1)S(1)}, u32[]{:S(2)}, u32[]{:S(2)}) async-start(bf16[32,16,256]{2,1,0:T(8,128)(2,1)} %bitcast.7), calls=%async_computation | async-start | bytes 524288 | tf_op jit(solution)/shard_map/all_to_all | solution.py:222
  45.9 0.9 %join.1 = bf16[2048,128]{1,0:T(8,128)(2,1)} custom-call(f32[2048,128]{1,0:T(8,128)S(1)} %get-tuple-element.40.mine, bf16[2048,128]{1,0:T(8,128)(2,1)S(1)} %collective-permute-done.9.theirs), custom_call_target="tpu_custom_call" | custom-call | bytes 2097152 | tf_op jit(solution)/shard_map/join/pallas_call | solution.py:27
  46.8 10.2 %all-to-all-done.moved = bf16[32,16,256]{2,1,0:T(8,128)(2,1)S(1)} async-done(((bf16[32,16,256]{2,1,0:T(8,128)(2,1)}), bf16[32,16,256]{2,1,0:T(8,128)(2,1)S(1)}, u32[]{:S(2)}, u32[]{:S(2)}) %all-to-all-start) | async-done | bytes 262176 | tf_op jit(solution)/shard_map/all_to_all | solution.py:222
  56.9 0.7 %finish.1 = (bf16[16,1024]{1,0:T(8,128)(2,1)}, bf16[16,1024]{1,0:T(8,128)(2,1)}) custom-call(bf16[32,16,256]{2,1,0:T(8,128)(2,1)S(1)} %all-to-all-done.moved), custom_call_target="tpu_custom_call" | custom-call | bytes 262144 | tf_op jit(solution)/shard_map/finish/pallas_call | solution.py:27
  (26 shorter events, 0.3 us)
Async XLA Ops:
  0.6 15.6 %collective-permute-start.6 = (bf16[2048,128]{1,0:T(8,128)(2,1)}, bf16[2048,128]{1,0:T(8,128)(2,1)S(1)}, u32[]{:S(2)}, u32[]{:S(2)}) collective-permute-start(bf16[2048,128]{1,0:T(8,128)(2,1)} %bitcast.15), channel_id=1, source_target_pairs={{0,8},{8,0},{1,9},{9,1},{2,10},{10,2},{3,11},{11,3},{4,12},{12,4},... | collective-permute-start | bytes 1572872 | tf_op jit(solution)/shard_map/ppermute | solution.py:171
  0.7 15.5 %collective-permute-start.7 = (bf16[2048,128]{1,0:T(8,128)(2,1)}, bf16[2048,128]{1,0:T(8,128)(2,1)S(1)}, u32[]{:S(2)}, u32[]{:S(2)}) collective-permute-start(bf16[2048,128]{1,0:T(8,128)(2,1)} %bitcast.9), channel_id=1, source_target_pairs={{0,8},{8,0},{1,9},{9,1},{2,10},{10,2},{3,11},{11,3},{4,12},{12,4},... | collective-permute-start | bytes 1572872 | tf_op jit(solution)/shard_map/ppermute | solution.py:171
  1.2 5.6 %copy-start.6 = (f32[16,128]{1,0:T(8,128)S(1)}, f32[16,128]{1,0:T(8,128)}, u32[]{:S(2)}) copy-start(f32[16,128]{1,0:T(8,128)} %param.13) | copy-start | bytes 24580
  2.0 7.5 %collective-permute-start.2 = (bf16[128,256]{1,0:T(8,128)(2,1)S(1)}, bf16[128,256]{1,0:T(8,128)(2,1)S(1)}, u32[]{:S(2)}, u32[]{:S(2)}) collective-permute-start(bf16[128,256]{1,0:T(8,128)(2,1)S(1)} %pad_maximum_fusion.own), channel_id=1, source_target_pairs={{0,192},{64,128},{128,64},{192,0},{1,193},{65,129},{129,65},{193,1... | collective-permute-start | bytes 196616 | tf_op jit(solution)/shard_map/ppermute | solution.py:171
  4.0 6.5 %collective-permute-start.1 = (bf16[128,256]{1,0:T(8,128)(2,1)S(1)}, bf16[128,256]{1,0:T(8,128)(2,1)S(1)}, u32[]{:S(2)}, u32[]{:S(2)}) collective-permute-start(bf16[128,256]{1,0:T(8,128)(2,1)S(1)} %pad_maximum_fusion.own), channel_id=1, source_target_pairs={{0,128},{64,192},{128,0},{192,64},{1,129},{65,193},{129,1},{193,65... | collective-permute-start | bytes 196616 | tf_op jit(solution)/shard_map/ppermute | solution.py:171
  6.3 5.5 %collective-permute-start = (bf16[128,256]{1,0:T(8,128)(2,1)S(1)}, bf16[128,256]{1,0:T(8,128)(2,1)S(1)}, u32[]{:S(2)}, u32[]{:S(2)}) collective-permute-start(bf16[128,256]{1,0:T(8,128)(2,1)S(1)} %pad_maximum_fusion.own), channel_id=1, source_target_pairs={{0,64},{64,0},{128,192},{192,128},{1,65},{65,1},{129,193},{193,129... | collective-permute-start | bytes 196616 | tf_op jit(solution)/shard_map/ppermute | solution.py:171
  7.0 1.0 %copy-start = (bf16[128,16,128]{2,1,0:T(8,128)(2,1)S(1)}, bf16[128,16,128]{2,1,0:T(8,128)(2,1)}, u32[]{:S(2)}) copy-start(bf16[128,16,128]{2,1,0:T(8,128)(2,1)} %param.12) | copy-start | bytes 1572868
  8.1 1.0 %copy-start.3 = (bf16[128,16,128]{2,1,0:T(8,128)(2,1)S(1)}, bf16[128,16,128]{2,1,0:T(8,128)(2,1)}, u32[]{:S(2)}) copy-start(bf16[128,16,128]{2,1,0:T(8,128)(2,1)} %param.11) | copy-start | bytes 1572868
  9.1 0.7 %copy-start.4 = (s32[32]{0:T(128)S(1)}, s32[32]{0:T(128)}, u32[]{:S(2)}) copy-start(s32[32]{0:T(128)} %order.1) | copy-start | bytes 388
  9.1 0.7 %copy-start.5 = (s32[12]{0:T(128)S(1)}, s32[12]{0:T(128)}, u32[]{:S(2)}) copy-start(s32[12]{0:T(128)} %lengths.1) | copy-start | bytes 148
  9.1 7.1 %copy-start.1 = (bf16[128,16,128]{2,1,0:T(8,128)(2,1)S(1)}, bf16[128,16,128]{2,1,0:T(8,128)(2,1)}, u32[]{:S(2)}) copy-start(bf16[128,16,128]{2,1,0:T(8,128)(2,1)} %param.12) | copy-start | bytes 1572868
  9.1 7.1 %copy-start.2 = (bf16[128,16,128]{2,1,0:T(8,128)(2,1)S(1)}, bf16[128,16,128]{2,1,0:T(8,128)(2,1)}, u32[]{:S(2)}) copy-start(bf16[128,16,128]{2,1,0:T(8,128)(2,1)} %param.8) | copy-start | bytes 1572868
  9.6 6.2 %collective-permute-start.8 = (f32[2,2048]{1,0:T(2,128)S(1)}, f32[2,2048]{1,0:T(2,128)S(1)}, u32[]{:S(2)}, u32[]{:S(2)}) collective-permute-start(f32[2,2048]{1,0:T(2,128)S(1)} %stats.1.stats0), channel_id=1, source_target_pairs={{0,8},{8,0},{1,9},{9,1},{2,10},{10,2},{3,11},{11,3},{4,12},{12,4},... | collective-permute-start | bytes 49160 | tf_op jit(solution)/shard_map/ppermute | solution.py:171
  11.9 7.9 %collective-permute-start.4 = (bf16[256,256]{1,0:T(8,128)(2,1)S(1)}, bf16[256,256]{1,0:T(8,128)(2,1)S(1)}, u32[]{:S(2)}, u32[]{:S(2)}) collective-permute-start(bf16[256,256]{1,0:T(8,128)(2,1)S(1)} %get-tuple-element.29), channel_id=1, source_target_pairs={{0,32},{16,48},{32,0},{48,16},{1,33},{17,49},{33,1},{49,17},{2,34}... | collective-permute-start | bytes 393224 | tf_op jit(solution)/shard_map/ppermute | solution.py:171
  15.1 9.4 %collective-permute-start.3 = (bf16[256,256]{1,0:T(8,128)(2,1)S(1)}, bf16[256,256]{1,0:T(8,128)(2,1)S(1)}, u32[]{:S(2)}, u32[]{:S(2)}) collective-permute-start(bf16[256,256]{1,0:T(8,128)(2,1)S(1)} %get-tuple-element.28), channel_id=1, source_target_pairs={{0,16},{16,0},{32,48},{48,32},{1,17},{17,1},{33,49},{49,33},{2,18}... | collective-permute-start | bytes 393224 | tf_op jit(solution)/shard_map/ppermute | solution.py:171
  15.8 10.3 %collective-permute-start.5 = (bf16[256,256]{1,0:T(8,128)(2,1)S(1)}, bf16[256,256]{1,0:T(8,128)(2,1)S(1)}, u32[]{:S(2)}, u32[]{:S(2)}) collective-permute-start(bf16[256,256]{1,0:T(8,128)(2,1)S(1)} %get-tuple-element.30), channel_id=1, source_target_pairs={{0,48},{16,32},{32,16},{48,0},{1,49},{17,33},{33,17},{49,1},{2,50}... | collective-permute-start | bytes 393224 | tf_op jit(solution)/shard_map/ppermute | solution.py:171
  21.4 9.5 %collective-permute-start.11 = (bf16[256,256]{1,0:T(8,128)(2,1)S(1)}, bf16[256,256]{1,0:T(8,128)(2,1)S(1)}, u32[]{:S(2)}, u32[]{:S(2)}) collective-permute-start(bf16[256,256]{1,0:T(8,128)(2,1)S(1)} %get-tuple-element.44), channel_id=1, source_target_pairs={{0,32},{16,48},{32,0},{48,16},{1,33},{17,49},{33,1},{49,17},{2,34}... | collective-permute-start | bytes 393224 | tf_op jit(solution)/shard_map/ppermute | solution.py:171
  27.7 6.3 %collective-permute-start.12 = (bf16[256,256]{1,0:T(8,128)(2,1)S(1)}, bf16[256,256]{1,0:T(8,128)(2,1)S(1)}, u32[]{:S(2)}, u32[]{:S(2)}) collective-permute-start(bf16[256,256]{1,0:T(8,128)(2,1)S(1)} %get-tuple-element.45), channel_id=1, source_target_pairs={{0,48},{16,32},{32,16},{48,0},{1,49},{17,33},{33,17},{49,1},{2,50}... | collective-permute-start | bytes 393224 | tf_op jit(solution)/shard_map/ppermute | solution.py:171
  28.9 5.1 %collective-permute-start.10 = (bf16[256,256]{1,0:T(8,128)(2,1)S(1)}, bf16[256,256]{1,0:T(8,128)(2,1)S(1)}, u32[]{:S(2)}, u32[]{:S(2)}) collective-permute-start(bf16[256,256]{1,0:T(8,128)(2,1)S(1)} %get-tuple-element.43), channel_id=1, source_target_pairs={{0,16},{16,0},{32,48},{48,32},{1,17},{17,1},{33,49},{49,33},{2,18}... | collective-permute-start | bytes 393224 | tf_op jit(solution)/shard_map/ppermute | solution.py:171
  30.7 15.2 %collective-permute-start.9 = (bf16[2048,128]{1,0:T(8,128)(2,1)S(1)}, bf16[2048,128]{1,0:T(8,128)(2,1)S(1)}, u32[]{:S(2)}, u32[]{:S(2)}) collective-permute-start(bf16[2048,128]{1,0:T(8,128)(2,1)S(1)} %get-tuple-element.41), channel_id=1, source_target_pairs={{0,8},{8,0},{1,9},{9,1},{2,10},{10,2},{3,11},{11,3},{4,12},{12,4},... | collective-permute-start | bytes 1572872 | tf_op jit(solution)/shard_map/ppermute | solution.py:171
  35.0 21.9 %all-to-all-start = ((bf16[32,16,256]{2,1,0:T(8,128)(2,1)}), bf16[32,16,256]{2,1,0:T(8,128)(2,1)S(1)}, u32[]{:S(2)}, u32[]{:S(2)}) async-start(bf16[32,16,256]{2,1,0:T(8,128)(2,1)} %bitcast.7), calls=%async_computation | async-start | bytes 524288 | tf_op jit(solution)/shard_map/all_to_all | solution.py:222

commit v7 on v6

--- a/solution.py
+++ b/solution.py
@@ -69,13 +69,22 @@
         span_ref[2 * j + 1 : 2 * j + 2, :] = pos
 
 
-def stats_kernel(outputs, out_grad, lse, stats):
+def stats_kernel(outputs, out_grad, lse, stats, loaded, sems):
     rows, dh = outputs.shape
+    copies = []
+    for c in range(rows // CHUNK):
+        cols = pl.ds(c * CHUNK, CHUNK)
+        for i, ref in enumerate((outputs, out_grad)):
+            copy = pltpu.make_async_copy(ref.at[cols, :], loaded.at[i, cols, :], sems.at[c, i])
+            copy.start()
+            copies.append(copy)
     ones = jnp.ones((8, dh), jnp.bfloat16)
     stats[0:1, :] = lse[...]
     for c in range(rows // CHUNK):
         cols = slice(c * CHUNK, (c + 1) * CHUNK)
-        product = outputs[cols, :].astype(jnp.float32) * out_grad[cols, :].astype(jnp.float32)
+        copies[2 * c].wait()
+        copies[2 * c + 1].wait()
+        product = loaded[0, cols, :].astype(jnp.float32) * loaded[1, cols, :].astype(jnp.float32)
         high = product.astype(jnp.bfloat16)
         low = (product - high.astype(jnp.float32)).astype(jnp.bfloat16)
         delta = lax.dot_general(ones, high, NT, preferred_element_type=jnp.float32)
@@ -188,6 +197,8 @@
     stats = call(
         stats_kernel, shape((2, cols), f32),
         (outputs.reshape(cols, dh), out_grad.reshape(cols, dh), (logsumexp * LOG2E).T.reshape(1, cols)), "stats",
+        scratch=[pltpu.VMEM((2, cols, dh), bf16), pltpu.SemaphoreType.DMA((cols // CHUNK, 2))],
+        specs=[pl.BlockSpec(memory_space=pl.ANY)] * 2 + [VMEM], moved=1 << 22,
     )
     sides = []
     for x in (queries.reshape(cols, dh), out_grad.reshape(cols, dh), stats):

time: 57.9 us -> 57.9 us (level)
  no operation moved by 1% of the time
where the time goes in v7:
time: 57.9 us; the launch traced here: 57.6 us
  starting transfers between devices  25.3 us (44%)
  waiting for transfers between devices  16.1 us (28%)
  Pallas kernels  12.2 us (21%)
  local copies, waits for them, and re-layouts  2.29 us (4%)
  between operations  0.82 us (1%)
  other arithmetic  0.8 us (1%)
    ppermute x13, starting transfers between devices, swap(): return lax.ppermute(x, axis, [(i, i ^ mask) for i in range(size)])  14.8 us
    pallas_call x11, Pallas kernels, call(): pl.pallas_call(body, out_shape=outs, in_specs=specs or [VMEM] * len(input...  12.2 us
    all_to_all x1, starting transfers between devices, local(): lax.all_to_all(total.reshape(ZL * KVH, share, wide), ('x', 'zh', 'zl'), s...  10.6 us
    all_to_all x1, waiting for transfers between devices, local(): lax.all_to_all(total.reshape(ZL * KVH, share, wide), ('x', 'zh', 'zl'), s...  10.2 us
    ppermute x13, waiting for transfers between devices, swap(): return lax.ppermute(x, axis, [(i, i ^ mask) for i in range(size)])  5.96 us
    unnamed x14, local copies, waits for them, and re-layouts  2.1 us
  transfers between devices with their start and end apart: 14, of which 4 were waited for; matrix products, arithmetic and copies ran while one was open for 2% of the time, Pallas kernels for 20%

profile of v7, /device:TPU:32, one launch (start us, length us, event | category | flops | bytes accessed | tf_op | source)
XLA Modules:
  0.0 57.6 jit_solution(2045552647907271835)
XLA Ops:
  0.6 0.1 collective-permute-start.6
  0.7 0.5 collective-permute-start.7
  1.2 0.8 %pad_maximum_fusion.own = bf16[128,256]{1,0:T(8,128)(2,1)S(1)} fusion(bf16[128,128]{1,0:T(8,128)(2,1)} %bitcast.22, bf16[128,128]{1,0:T(8,128)(2,1)} %bitcast.23), kind=kLoop, calls=%fused_computation | loop fusion | flops 131072 | bytes 131072 | tf_op jit(solution)/shard_map/concatenate | solution.py:190
  2.0 2.0 %collective-permute-start.2 = (bf16[128,256]{1,0:T(8,128)(2,1)S(1)}, bf16[128,256]{1,0:T(8,128)(2,1)S(1)}, u32[]{:S(2)}, u32[]{:S(2)}) collective-permute-start(bf16[128,256]{1,0:T(8,128)(2,1)S(1)} %pad_maximum_fusion.own), channel_id=1, source_target_pairs={{0,192},{64,128},{128,64},{192,0},{1,193},{65,129},{129,65},{193,1... | collective-permute-start | bytes 196616 | tf_op jit(solution)/shard_map/ppermute | solution.py:180
  4.0 2.3 %collective-permute-start.1 = (bf16[128,256]{1,0:T(8,128)(2,1)S(1)}, bf16[128,256]{1,0:T(8,128)(2,1)S(1)}, u32[]{:S(2)}, u32[]{:S(2)}) collective-permute-start(bf16[128,256]{1,0:T(8,128)(2,1)S(1)} %pad_maximum_fusion.own), channel_id=1, source_target_pairs={{0,128},{64,192},{128,0},{192,64},{1,129},{65,193},{129,1},{193,65... | collective-permute-start | bytes 196616 | tf_op jit(solution)/shard_map/ppermute | solution.py:180
  6.3 0.5 collective-permute-start
  6.9 0.1 copy.12
  7.0 0.1 reshape.28.lse
  7.1 1.0 %copy-done = bf16[128,16,128]{2,1,0:T(8,128)(2,1)S(1)} copy-done((bf16[128,16,128]{2,1,0:T(8,128)(2,1)S(1)}, bf16[128,16,128]{2,1,0:T(8,128)(2,1)}, u32[]{:S(2)}) %copy-start) | copy-done | bytes 524312
  8.1 1.0 %copy-done.3 = bf16[128,16,128]{2,1,0:T(8,128)(2,1)S(1)} copy-done((bf16[128,16,128]{2,1,0:T(8,128)(2,1)S(1)}, bf16[128,16,128]{2,1,0:T(8,128)(2,1)}, u32[]{:S(2)}) %copy-start.3) | copy-done | bytes 524312
  9.1 0.7 %stats.1.stats0 = f32[2,2048]{1,0:T(2,128)S(1)} custom-call(bf16[2048,128]{1,0:T(8,128)(2,1)S(1)} %bitcast.20, bf16[2048,128]{1,0:T(8,128)(2,1)S(1)} %bitcast.10, f32[1,2048]{1,0:T(1,128)S(1)} %reshape.28.lse), custom_call_target="tpu_custom_call" | custom-call | bytes 4194304 | tf_op jit(solution)/shard_map/stats/pallas_call | solution.py:27
  9.9 0.1 collective-permute-start.8
  10.0 0.7 %plan.1 = (s32[24,128]{1,0:T(8,128)S(1)}, s32[4,2048]{1,0:T(4,128)S(1)}) custom-call(s32[32]{0:T(128)S(1)} %copy-done.4, s32[12]{0:T(128)S(1)} %copy-done.5), custom_call_target="tpu_custom_call" | custom-call | bytes 262144 | tf_op jit(solution)/shard_map/plan/pallas_call | solution.py:27
  10.7 1.1 %collective-permute-done.col1 = bf16[128,256]{1,0:T(8,128)(2,1)S(1)} collective-permute-done((bf16[128,256]{1,0:T(8,128)(2,1)S(1)}, bf16[128,256]{1,0:T(8,128)(2,1)S(1)}, u32[]{:S(2)}, u32[]{:S(2)}) %collective-permute-start) | collective-permute-done | bytes 65568 | tf_op jit(solution)/shard_map/ppermute | solution.py:180
  11.9 3.3 %collective-permute-start.4 = (bf16[256,256]{1,0:T(8,128)(2,1)S(1)}, bf16[256,256]{1,0:T(8,128)(2,1)S(1)}, u32[]{:S(2)}, u32[]{:S(2)}) collective-permute-start(bf16[256,256]{1,0:T(8,128)(2,1)S(1)} %get-tuple-element.29), channel_id=1, source_target_pairs={{0,32},{16,48},{32,0},{48,16},{1,33},{17,49},{33,1},{49,17},{2,34}... | collective-permute-start | bytes 393224 | tf_op jit(solution)/shard_map/ppermute | solution.py:180
  15.1 0.7 %collective-permute-start.3 = (bf16[256,256]{1,0:T(8,128)(2,1)S(1)}, bf16[256,256]{1,0:T(8,128)(2,1)S(1)}, u32[]{:S(2)}, u32[]{:S(2)}) collective-permute-start(bf16[256,256]{1,0:T(8,128)(2,1)S(1)} %get-tuple-element.28), channel_id=1, source_target_pairs={{0,16},{16,0},{32,48},{48,32},{1,17},{17,1},{33,49},{49,33},{2,18}... | collective-permute-start | bytes 393224 | tf_op jit(solution)/shard_map/ppermute | solution.py:180
  15.8 0.4 collective-permute-start.5
  16.2 1.6 %class0.1 = (f32[256,256]{1,0:T(8,128)S(1)}, bf16[256,2048]{1,0:T(8,128)(2,1)S(1)}, f32[8,128]{1,0:T(8,128)S(1)}) custom-call(s32[24,128]{1,0:T(8,128)S(1)} %get-tuple-element.26.plan, bf16[2048,128]{1,0:T(8,128)(2,1)S(1)} %bitcast.16, bf16[2048,128]{1,0:T(8,128)(2,1)S(1)} %bitcast.11, f32[2,2048]{1,0:T(2,128)S(1)} %stats.1.stats0, ...), custom_call_target="tpu_custom_call" | custom-call | bytes 4096 | tf_op jit(solution)/shard_map/class0/pallas_call | solution.py:27
  17.8 1.7 %collective-permute-done.4.kv.kv2 = bf16[256,256]{1,0:T(8,128)(2,1)S(1)} collective-permute-done((bf16[256,256]{1,0:T(8,128)(2,1)S(1)}, bf16[256,256]{1,0:T(8,128)(2,1)S(1)}, u32[]{:S(2)}, u32[]{:S(2)}) %collective-permute-start.4) | collective-permute-done | bytes 131104 | tf_op jit(solution)/shard_map/ppermute | solution.py:180
  19.6 1.6 %class2.1 = (bf16[256,256]{1,0:T(8,128)(2,1)S(1)}, bf16[256,2048]{1,0:T(8,128)(2,1)S(1)}, f32[8,128]{1,0:T(8,128)S(1)}) custom-call(s32[24,128]{1,0:T(8,128)S(1)} %get-tuple-element.26.plan, bf16[2048,128]{1,0:T(8,128)(2,1)S(1)} %bitcast.17, bf16[2048,128]{1,0:T(8,128)(2,1)S(1)} %bitcast.12, f32[2,2048]{1,0:T(2,128)S(1)} %stats.1.stats0, ...), custom_call_target="tpu_custom_call" | custom-call | bytes 4096 | tf_op jit(solution)/shard_map/class2/pallas_call | solution.py:27
  21.2 3.6 %collective-permute-start.11 = (bf16[256,256]{1,0:T(8,128)(2,1)S(1)}, bf16[256,256]{1,0:T(8,128)(2,1)S(1)}, u32[]{:S(2)}, u32[]{:S(2)}) collective-permute-start(bf16[256,256]{1,0:T(8,128)(2,1)S(1)} %get-tuple-element.44), channel_id=1, source_target_pairs={{0,32},{16,48},{32,0},{48,16},{1,33},{17,49},{33,1},{49,17},{2,34}... | collective-permute-start | bytes 393224 | tf_op jit(solution)/shard_map/ppermute | solution.py:180
  24.8 1.6 %class1.1 = (bf16[256,256]{1,0:T(8,128)(2,1)S(1)}, bf16[256,2048]{1,0:T(8,128)(2,1)S(1)}, f32[8,128]{1,0:T(8,128)S(1)}) custom-call(s32[24,128]{1,0:T(8,128)S(1)} %get-tuple-element.26.plan, bf16[2048,128]{1,0:T(8,128)(2,1)S(1)} %bitcast.18, bf16[2048,128]{1,0:T(8,128)(2,1)S(1)} %bitcast.13, f32[2,2048]{1,0:T(2,128)S(1)} %stats.1.stats0, ...), custom_call_target="tpu_custom_call" | custom-call | bytes 4096 | tf_op jit(solution)/shard_map/class1/pallas_call | solution.py:27
  26.4 1.6 %class3.1 = (bf16[256,256]{1,0:T(8,128)(2,1)S(1)}, bf16[256,2048]{1,0:T(8,128)(2,1)S(1)}, f32[8,128]{1,0:T(8,128)S(1)}) custom-call(s32[24,128]{1,0:T(8,128)S(1)} %get-tuple-element.26.plan, bf16[2048,128]{1,0:T(8,128)(2,1)S(1)} %bitcast.19, bf16[2048,128]{1,0:T(8,128)(2,1)S(1)} %bitcast.14, f32[2,2048]{1,0:T(2,128)S(1)} %stats.1.stats0, ...), custom_call_target="tpu_custom_call" | custom-call | bytes 4096 | tf_op jit(solution)/shard_map/class3/pallas_call | solution.py:27
  28.0 1.2 %collective-permute-start.12 = (bf16[256,256]{1,0:T(8,128)(2,1)S(1)}, bf16[256,256]{1,0:T(8,128)(2,1)S(1)}, u32[]{:S(2)}, u32[]{:S(2)}) collective-permute-start(bf16[256,256]{1,0:T(8,128)(2,1)S(1)} %get-tuple-element.45), channel_id=1, source_target_pairs={{0,48},{16,32},{32,16},{48,0},{1,49},{17,33},{33,17},{49,1},{2,50}... | collective-permute-start | bytes 393224 | tf_op jit(solution)/shard_map/ppermute | solution.py:180
  29.2 1.8 %query.1 = (f32[2048,128]{1,0:T(8,128)S(1)}, bf16[2048,128]{1,0:T(8,128)(2,1)S(1)}, f32[8,128]{1,0:T(8,128)S(1)}) custom-call(bf16[256,256]{1,0:T(8,128)(2,1)S(1)} %get-tuple-element.27.kv.kv0, bf16[256,256]{1,0:T(8,128)(2,1)S(1)} %collective-permute-done.3.kv.kv1, bf16[256,256]{1,0:T(8,128)(2,1)S(1)} %collective-permute-done.4.kv.kv2, ...), custom_call_target="tpu_custom_call" | custom-call | bytes 4096 | tf_op jit(solution)/shard_map/query/pallas_call | solution.py:27
  31.0 0.1 collective-permute-start.9
  31.1 3.2 %collective-permute-done.12.part3 = bf16[256,256]{1,0:T(8,128)(2,1)S(1)} collective-permute-done((bf16[256,256]{1,0:T(8,128)(2,1)S(1)}, bf16[256,256]{1,0:T(8,128)(2,1)S(1)}, u32[]{:S(2)}, u32[]{:S(2)}) %collective-permute-start.12) | collective-permute-done | bytes 131104 | tf_op jit(solution)/shard_map/ppermute | solution.py:180
  34.3 1.0 %total.1 = bf16[8,4,16,256]{3,2,1,0:T(8,128)(2,1)} custom-call(s32[24,128]{1,0:T(8,128)S(1)} %get-tuple-element.26.plan, f32[256,256]{1,0:T(8,128)S(1)} %get-tuple-element.42.part0, bf16[256,256]{1,0:T(8,128)(2,1)S(1)} %collective-permute-done.10.part1, bf16[256,256]{1,0:T(8,128)(2,1)S(1)} %collective-permute-done.11.part2, ...), custom_call_target="tpu_custom_call" | custom-call | bytes 262144 | tf_op jit(solution)/shard_map/total/pallas_call | solution.py:27
  35.3 10.6 %all-to-all-start = ((bf16[32,16,256]{2,1,0:T(8,128)(2,1)}), bf16[32,16,256]{2,1,0:T(8,128)(2,1)S(1)}, u32[]{:S(2)}, u32[]{:S(2)}) async-start(bf16[32,16,256]{2,1,0:T(8,128)(2,1)} %bitcast.7), calls=%async_computation | async-start | bytes 524288 | tf_op jit(solution)/shard_map/all_to_all | solution.py:233
  45.9 0.9 %join.1 = bf16[2048,128]{1,0:T(8,128)(2,1)} custom-call(f32[2048,128]{1,0:T(8,128)S(1)} %get-tuple-element.40.mine, bf16[2048,128]{1,0:T(8,128)(2,1)S(1)} %collective-permute-done.9.theirs), custom_call_target="tpu_custom_call" | custom-call | bytes 2097152 | tf_op jit(solution)/shard_map/join/pallas_call | solution.py:27
  46.8 10.2 %all-to-all-done.moved = bf16[32,16,256]{2,1,0:T(8,128)(2,1)S(1)} async-done(((bf16[32,16,256]{2,1,0:T(8,128)(2,1)}), bf16[32,16,256]{2,1,0:T(8,128)(2,1)S(1)}, u32[]{:S(2)}, u32[]{:S(2)}) %all-to-all-start) | async-done | bytes 262176 | tf_op jit(solution)/shard_map/all_to_all | solution.py:233
  56.9 0.7 %finish.1 = (bf16[16,1024]{1,0:T(8,128)(2,1)}, bf16[16,1024]{1,0:T(8,128)(2,1)}) custom-call(bf16[32,16,256]{2,1,0:T(8,128)(2,1)S(1)} %all-to-all-done.moved), custom_call_target="tpu_custom_call" | custom-call | bytes 262144 | tf_op jit(solution)/shard_map/finish/pallas_call | solution.py:27
  (26 shorter events, 0.1 us)
Async XLA Ops:
  0.6 15.6 %collective-permute-start.6 = (bf16[2048,128]{1,0:T(8,128)(2,1)}, bf16[2048,128]{1,0:T(8,128)(2,1)S(1)}, u32[]{:S(2)}, u32[]{:S(2)}) collective-permute-start(bf16[2048,128]{1,0:T(8,128)(2,1)} %bitcast.15), channel_id=1, source_target_pairs={{0,8},{8,0},{1,9},{9,1},{2,10},{10,2},{3,11},{11,3},{4,12},{12,4},... | collective-permute-start | bytes 1572872 | tf_op jit(solution)/shard_map/ppermute | solution.py:180
  0.7 15.5 %collective-permute-start.7 = (bf16[2048,128]{1,0:T(8,128)(2,1)}, bf16[2048,128]{1,0:T(8,128)(2,1)S(1)}, u32[]{:S(2)}, u32[]{:S(2)}) collective-permute-start(bf16[2048,128]{1,0:T(8,128)(2,1)} %bitcast.9), channel_id=1, source_target_pairs={{0,8},{8,0},{1,9},{9,1},{2,10},{10,2},{3,11},{11,3},{4,12},{12,4},... | collective-permute-start | bytes 1572872 | tf_op jit(solution)/shard_map/ppermute | solution.py:180
  1.2 5.6 %copy-start.6 = (f32[16,128]{1,0:T(8,128)S(1)}, f32[16,128]{1,0:T(8,128)}, u32[]{:S(2)}) copy-start(f32[16,128]{1,0:T(8,128)} %param.13) | copy-start | bytes 24580
  2.0 7.8 %collective-permute-start.2 = (bf16[128,256]{1,0:T(8,128)(2,1)S(1)}, bf16[128,256]{1,0:T(8,128)(2,1)S(1)}, u32[]{:S(2)}, u32[]{:S(2)}) collective-permute-start(bf16[128,256]{1,0:T(8,128)(2,1)S(1)} %pad_maximum_fusion.own), channel_id=1, source_target_pairs={{0,192},{64,128},{128,64},{192,0},{1,193},{65,129},{129,65},{193,1... | collective-permute-start | bytes 196616 | tf_op jit(solution)/shard_map/ppermute | solution.py:180
  4.0 6.7 %collective-permute-start.1 = (bf16[128,256]{1,0:T(8,128)(2,1)S(1)}, bf16[128,256]{1,0:T(8,128)(2,1)S(1)}, u32[]{:S(2)}, u32[]{:S(2)}) collective-permute-start(bf16[128,256]{1,0:T(8,128)(2,1)S(1)} %pad_maximum_fusion.own), channel_id=1, source_target_pairs={{0,128},{64,192},{128,0},{192,64},{1,129},{65,193},{129,1},{193,65... | collective-permute-start | bytes 196616 | tf_op jit(solution)/shard_map/ppermute | solution.py:180
  6.3 5.5 %collective-permute-start = (bf16[128,256]{1,0:T(8,128)(2,1)S(1)}, bf16[128,256]{1,0:T(8,128)(2,1)S(1)}, u32[]{:S(2)}, u32[]{:S(2)}) collective-permute-start(bf16[128,256]{1,0:T(8,128)(2,1)S(1)} %pad_maximum_fusion.own), channel_id=1, source_target_pairs={{0,64},{64,0},{128,192},{192,128},{1,65},{65,1},{129,193},{193,129... | collective-permute-start | bytes 196616 | tf_op jit(solution)/shard_map/ppermute | solution.py:180
  7.0 1.0 %copy-start = (bf16[128,16,128]{2,1,0:T(8,128)(2,1)S(1)}, bf16[128,16,128]{2,1,0:T(8,128)(2,1)}, u32[]{:S(2)}) copy-start(bf16[128,16,128]{2,1,0:T(8,128)(2,1)} %param.12) | copy-start | bytes 1572868
  8.1 1.0 %copy-start.3 = (bf16[128,16,128]{2,1,0:T(8,128)(2,1)S(1)}, bf16[128,16,128]{2,1,0:T(8,128)(2,1)}, u32[]{:S(2)}) copy-start(bf16[128,16,128]{2,1,0:T(8,128)(2,1)} %param.11) | copy-start | bytes 1572868
  9.1 0.8 %copy-start.4 = (s32[32]{0:T(128)S(1)}, s32[32]{0:T(128)}, u32[]{:S(2)}) copy-start(s32[32]{0:T(128)} %order.1) | copy-start | bytes 388
  9.1 0.8 %copy-start.5 = (s32[12]{0:T(128)S(1)}, s32[12]{0:T(128)}, u32[]{:S(2)}) copy-start(s32[12]{0:T(128)} %lengths.1) | copy-start | bytes 148
  9.1 7.1 %copy-start.1 = (bf16[128,16,128]{2,1,0:T(8,128)(2,1)S(1)}, bf16[128,16,128]{2,1,0:T(8,128)(2,1)}, u32[]{:S(2)}) copy-start(bf16[128,16,128]{2,1,0:T(8,128)(2,1)} %param.12) | copy-start | bytes 1572868
  9.1 7.1 %copy-start.2 = (bf16[128,16,128]{2,1,0:T(8,128)(2,1)S(1)}, bf16[128,16,128]{2,1,0:T(8,128)(2,1)}, u32[]{:S(2)}) copy-start(bf16[128,16,128]{2,1,0:T(8,128)(2,1)} %param.8) | copy-start | bytes 1572868
  9.9 5.9 %collective-permute-start.8 = (f32[2,2048]{1,0:T(2,128)S(1)}, f32[2,2048]{1,0:T(2,128)S(1)}, u32[]{:S(2)}, u32[]{:S(2)}) collective-permute-start(f32[2,2048]{1,0:T(2,128)S(1)} %stats.1.stats0), channel_id=1, source_target_pairs={{0,8},{8,0},{1,9},{9,1},{2,10},{10,2},{3,11},{11,3},{4,12},{12,4},... | collective-permute-start | bytes 49160 | tf_op jit(solution)/shard_map/ppermute | solution.py:180
  11.9 7.7 %collective-permute-start.4 = (bf16[256,256]{1,0:T(8,128)(2,1)S(1)}, bf16[256,256]{1,0:T(8,128)(2,1)S(1)}, u32[]{:S(2)}, u32[]{:S(2)}) collective-permute-start(bf16[256,256]{1,0:T(8,128)(2,1)S(1)} %get-tuple-element.29), channel_id=1, source_target_pairs={{0,32},{16,48},{32,0},{48,16},{1,33},{17,49},{33,1},{49,17},{2,34}... | collective-permute-start | bytes 393224 | tf_op jit(solution)/shard_map/ppermute | solution.py:180
  15.1 9.6 %collective-permute-start.3 = (bf16[256,256]{1,0:T(8,128)(2,1)S(1)}, bf16[256,256]{1,0:T(8,128)(2,1)S(1)}, u32[]{:S(2)}, u32[]{:S(2)}) collective-permute-start(bf16[256,256]{1,0:T(8,128)(2,1)S(1)} %get-tuple-element.28), channel_id=1, source_target_pairs={{0,16},{16,0},{32,48},{48,32},{1,17},{17,1},{33,49},{49,33},{2,18}... | collective-permute-start | bytes 393224 | tf_op jit(solution)/shard_map/ppermute | solution.py:180
  15.8 10.6 %collective-permute-start.5 = (bf16[256,256]{1,0:T(8,128)(2,1)S(1)}, bf16[256,256]{1,0:T(8,128)(2,1)S(1)}, u32[]{:S(2)}, u32[]{:S(2)}) collective-permute-start(bf16[256,256]{1,0:T(8,128)(2,1)S(1)} %get-tuple-element.30), channel_id=1, source_target_pairs={{0,48},{16,32},{32,16},{48,0},{1,49},{17,33},{33,17},{49,1},{2,50}... | collective-permute-start | bytes 393224 | tf_op jit(solution)/shard_map/ppermute | solution.py:180
  21.2 9.9 %collective-permute-start.11 = (bf16[256,256]{1,0:T(8,128)(2,1)S(1)}, bf16[256,256]{1,0:T(8,128)(2,1)S(1)}, u32[]{:S(2)}, u32[]{:S(2)}) collective-permute-start(bf16[256,256]{1,0:T(8,128)(2,1)S(1)} %get-tuple-element.44), channel_id=1, source_target_pairs={{0,32},{16,48},{32,0},{48,16},{1,33},{17,49},{33,1},{49,17},{2,34}... | collective-permute-start | bytes 393224 | tf_op jit(solution)/shard_map/ppermute | solution.py:180
  28.0 6.3 %collective-permute-start.12 = (bf16[256,256]{1,0:T(8,128)(2,1)S(1)}, bf16[256,256]{1,0:T(8,128)(2,1)S(1)}, u32[]{:S(2)}, u32[]{:S(2)}) collective-permute-start(bf16[256,256]{1,0:T(8,128)(2,1)S(1)} %get-tuple-element.45), channel_id=1, source_target_pairs={{0,48},{16,32},{32,16},{48,0},{1,49},{17,33},{33,17},{49,1},{2,50}... | collective-permute-start | bytes 393224 | tf_op jit(solution)/shard_map/ppermute | solution.py:180
  29.2 5.0 %collective-permute-start.10 = (bf16[256,256]{1,0:T(8,128)(2,1)S(1)}, bf16[256,256]{1,0:T(8,128)(2,1)S(1)}, u32[]{:S(2)}, u32[]{:S(2)}) collective-permute-start(bf16[256,256]{1,0:T(8,128)(2,1)S(1)} %get-tuple-element.43), channel_id=1, source_target_pairs={{0,16},{16,0},{32,48},{48,32},{1,17},{17,1},{33,49},{49,33},{2,18}... | collective-permute-start | bytes 393224 | tf_op jit(solution)/shard_map/ppermute | solution.py:180
  31.0 14.9 %collective-permute-start.9 = (bf16[2048,128]{1,0:T(8,128)(2,1)S(1)}, bf16[2048,128]{1,0:T(8,128)(2,1)S(1)}, u32[]{:S(2)}, u32[]{:S(2)}) collective-permute-start(bf16[2048,128]{1,0:T(8,128)(2,1)S(1)} %get-tuple-element.41), channel_id=1, source_target_pairs={{0,8},{8,0},{1,9},{9,1},{2,10},{10,2},{3,11},{11,3},{4,12},{12,4},... | collective-permute-start | bytes 1572872 | tf_op jit(solution)/shard_map/ppermute | solution.py:180
  35.3 21.6 %all-to-all-start = ((bf16[32,16,256]{2,1,0:T(8,128)(2,1)}), bf16[32,16,256]{2,1,0:T(8,128)(2,1)S(1)}, u32[]{:S(2)}, u32[]{:S(2)}) async-start(bf16[32,16,256]{2,1,0:T(8,128)(2,1)} %bitcast.7), calls=%async_computation | async-start | bytes 524288 | tf_op jit(solution)/shard_map/all_to_all | solution.py:233

commit v8 on v5

--- a/solution.py
+++ b/solution.py
@@ -139,15 +139,16 @@
             row = WANT + 2 * m + j
             z = jnp.max(plan[row : row + 1, :])
             acc[z] += part[j * BLK : (j + 1) * BLK, :].astype(jnp.float32)
-    out[...] = acc[...].astype(out.dtype)
+    for z in range(ZL):
+        out[:, z] = acc[z].reshape(KVH, BLK // KVH, acc.shape[2]).astype(out.dtype)
 
 
 def finish_kernel(moved, gk_ref, gv_ref):
     dh = moved.shape[2] // 2
     for k in range(KVH):
-        grad = moved[k].astype(jnp.float32)
+        grad = moved[k * ZL].astype(jnp.float32)
         for z in range(1, ZL):
-            grad += moved[z * KVH + k].astype(jnp.float32)
+            grad += moved[k * ZL + z].astype(jnp.float32)
         gk_ref[:, k * dh : (k + 1) * dh] = grad[:, :dh].astype(gk_ref.dtype)
         gv_ref[:, k * dh : (k + 1) * dh] = grad[:, dh:].astype(gv_ref.dtype)
 
@@ -198,12 +199,12 @@
     grad_q = call(join_kernel, shape((cols, dh), bf16), (mine, swap(theirs, "core", NCORE, 1)), "join", moved=1 << 21)
 
     total = call(
-        total_kernel, shape((ZL, BLK, wide), bf16), (plan, *back, token), "total",
+        total_kernel, shape((KVH, ZL, BLK // KVH, wide), bf16), (plan, *back, token), "total",
         scratch=[pltpu.VMEM((ZL, BLK, wide), f32)],
     )
     share = BLK // KVH
     moved = lax.all_to_all(
-        total.reshape(ZL * KVH, share, wide), ("zl", "x", "zh"), split_axis=0, concat_axis=0, tiled=True
+        total.reshape(ZL * KVH, share, wide), ("x", "zh", "zl"), split_axis=0, concat_axis=0, tiled=True
     )
     out = shape((share, KVH * dh), bf16)
     grad_keys, grad_values = call(finish_kernel, (out, out), (moved,), "finish")

time: 57.4 us -> 57.2 us (level)
  no operation moved by 1% of the time
where the time goes in v8:
time: 57.2 us; the launch traced here: 56.9 us
  starting transfers between devices  25.4 us (44%)
  waiting for transfers between devices  16 us (28%)
  Pallas kernels  11.3 us (20%)
  other arithmetic  2.44 us (4%)
  between operations  0.83 us (1%)
  local copies, waits for them, and re-layouts  0.82 us (1%)
    ppermute x13, starting transfers between devices, swap(): return lax.ppermute(x, axis, [(i, i ^ mask) for i in range(size)])  14.4 us
    pallas_call x10, Pallas kernels, call(): pl.pallas_call(body, out_shape=outs, in_specs=specs or [VMEM] * len(input...  11.3 us
    all_to_all x1, starting transfers between devices, local(): lax.all_to_all(total.reshape(ZL * KVH, share, wide), ('x', 'zh', 'zl'), s...  11.1 us
    all_to_all x1, waiting for transfers between devices, local(): lax.all_to_all(total.reshape(ZL * KVH, share, wide), ('x', 'zh', 'zl'), s...  10.2 us
    ppermute x13, waiting for transfers between devices, swap(): return lax.ppermute(x, axis, [(i, i ^ mask) for i in range(size)])  5.87 us
    reduce_sum x1, other arithmetic, local(): delta = jnp.sum(out_grad.astype(f32) * outputs.astype(f32), axis=2)  1.63 us
  transfers between devices with their start and end apart: 14, of which 4 were waited for; matrix products, arithmetic and copies ran while one was open for 3% of the time, Pallas kernels for 19%

profile of v8, /device:TPU:32, one launch (start us, length us, event | category | flops | bytes accessed | tf_op | source)
XLA Modules:
  0.0 56.9 jit_solution(1887457768116279924)
XLA Ops:
  0.6 0.8 %pad_maximum_fusion.own = bf16[128,256]{1,0:T(8,128)(2,1)S(1)} fusion(bf16[128,128]{1,0:T(8,128)(2,1)} %bitcast.19, bf16[128,128]{1,0:T(8,128)(2,1)} %bitcast.20), kind=kLoop, calls=%fused_computation.1 | loop fusion | flops 131072 | bytes 131072 | tf_op jit(solution)/shard_map/concatenate | solution.py:167
  1.4 2.0 %collective-permute-start.2 = (bf16[128,256]{1,0:T(8,128)(2,1)S(1)}, bf16[128,256]{1,0:T(8,128)(2,1)S(1)}, u32[]{:S(2)}, u32[]{:S(2)}) collective-permute-start(bf16[128,256]{1,0:T(8,128)(2,1)S(1)} %pad_maximum_fusion.own), channel_id=1, source_target_pairs={{0,192},{64,128},{128,64},{192,0},{1,193},{65,129},{129,65},{193,1... | collective-permute-start | bytes 196616 | tf_op jit(solution)/shard_map/ppermute | solution.py:157
  3.4 2.3 %collective-permute-start.1 = (bf16[128,256]{1,0:T(8,128)(2,1)S(1)}, bf16[128,256]{1,0:T(8,128)(2,1)S(1)}, u32[]{:S(2)}, u32[]{:S(2)}) collective-permute-start(bf16[128,256]{1,0:T(8,128)(2,1)S(1)} %pad_maximum_fusion.own), channel_id=1, source_target_pairs={{0,128},{64,192},{128,0},{192,64},{1,129},{65,193},{129,1},{193,65... | collective-permute-start | bytes 196616 | tf_op jit(solution)/shard_map/ppermute | solution.py:157
  5.7 0.5 collective-permute-start
  6.3 0.5 collective-permute-start.7
  6.8 0.1 copy.12
  6.9 0.1 stack_reshape.6
  7.0 1.6 %multiply_reduce_fusion = f32[128,16]{1,0:T(8,128)S(1)} fusion(bf16[128,16,128]{2,1,0:T(8,128)(2,1)} %param.11, bf16[128,16,128]{2,1,0:T(8,128)(2,1)} %param.12), kind=kLoop, calls=%fused_computation | loop fusion | flops 1046528 | bytes 1056768 | tf_op jit(solution)/shard_map/reduce_sum | solution.py:174
  8.6 0.1 stack_reshape.7
  8.8 0.1 collective-permute-start.8
  8.9 0.5 copy-done.2
  9.4 0.7 %plan.1 = (s32[24,128]{1,0:T(8,128)S(1)}, s32[4,2048]{1,0:T(4,128)S(1)}) custom-call(s32[32]{0:T(128)S(1)} %copy-done.2, s32[12]{0:T(128)S(1)} %copy-done.3), custom_call_target="tpu_custom_call" | custom-call | bytes 262144 | tf_op jit(solution)/shard_map/plan/pallas_call | solution.py:27
  10.1 0.8 %collective-permute-done.col1 = bf16[128,256]{1,0:T(8,128)(2,1)S(1)} collective-permute-done((bf16[128,256]{1,0:T(8,128)(2,1)S(1)}, bf16[128,256]{1,0:T(8,128)(2,1)S(1)}, u32[]{:S(2)}, u32[]{:S(2)}) %collective-permute-start) | collective-permute-done | bytes 65568 | tf_op jit(solution)/shard_map/ppermute | solution.py:157
  10.9 0.1 select.1
  11.0 3.3 %collective-permute-start.4 = (bf16[256,256]{1,0:T(8,128)(2,1)S(1)}, bf16[256,256]{1,0:T(8,128)(2,1)S(1)}, u32[]{:S(2)}, u32[]{:S(2)}) collective-permute-start(bf16[256,256]{1,0:T(8,128)(2,1)S(1)} %get-tuple-element.29), channel_id=1, source_target_pairs={{0,32},{16,48},{32,0},{48,16},{1,33},{17,49},{33,1},{49,17},{2,34}... | collective-permute-start | bytes 393224 | tf_op jit(solution)/shard_map/ppermute | solution.py:157
  14.3 0.7 %collective-permute-start.3 = (bf16[256,256]{1,0:T(8,128)(2,1)S(1)}, bf16[256,256]{1,0:T(8,128)(2,1)S(1)}, u32[]{:S(2)}, u32[]{:S(2)}) collective-permute-start(bf16[256,256]{1,0:T(8,128)(2,1)S(1)} %get-tuple-element.28), channel_id=1, source_target_pairs={{0,16},{16,0},{32,48},{48,32},{1,17},{17,1},{33,49},{49,33},{2,18}... | collective-permute-start | bytes 393224 | tf_op jit(solution)/shard_map/ppermute | solution.py:157
  15.0 0.4 collective-permute-start.5
  15.4 1.6 %class0.1 = (f32[256,256]{1,0:T(8,128)S(1)}, bf16[256,2048]{1,0:T(8,128)(2,1)S(1)}, f32[8,128]{1,0:T(8,128)S(1)}) custom-call(s32[24,128]{1,0:T(8,128)S(1)} %get-tuple-element.26.plan, bf16[2048,128]{1,0:T(8,128)(2,1)S(1)} %bitcast.14, bf16[2048,128]{1,0:T(8,128)(2,1)S(1)} %bitcast.9, f32[2,2048]{1,0:T(2,128)S(1)} %pad_maximum_fusion.1.stats0, ...), custom_call_target="tpu_custom_call" | custom-call | bytes 4096 | tf_op jit(solution)/shard_map/class0/pallas_call | solution.py:27
  16.9 1.9 %collective-permute-done.4.kv.kv2 = bf16[256,256]{1,0:T(8,128)(2,1)S(1)} collective-permute-done((bf16[256,256]{1,0:T(8,128)(2,1)S(1)}, bf16[256,256]{1,0:T(8,128)(2,1)S(1)}, u32[]{:S(2)}, u32[]{:S(2)}) %collective-permute-start.4) | collective-permute-done | bytes 131104 | tf_op jit(solution)/shard_map/ppermute | solution.py:157
  18.8 1.6 %class2.1 = (bf16[256,256]{1,0:T(8,128)(2,1)S(1)}, bf16[256,2048]{1,0:T(8,128)(2,1)S(1)}, f32[8,128]{1,0:T(8,128)S(1)}) custom-call(s32[24,128]{1,0:T(8,128)S(1)} %get-tuple-element.26.plan, bf16[2048,128]{1,0:T(8,128)(2,1)S(1)} %bitcast.15, bf16[2048,128]{1,0:T(8,128)(2,1)S(1)} %bitcast.10, f32[2,2048]{1,0:T(2,128)S(1)} %pad_maximum_fusion.1.stats0, ...), custom_call_target="tpu_custom_call" | custom-call | bytes 4096 | tf_op jit(solution)/shard_map/class2/pallas_call | solution.py:27
  20.4 3.3 %collective-permute-start.11 = (bf16[256,256]{1,0:T(8,128)(2,1)S(1)}, bf16[256,256]{1,0:T(8,128)(2,1)S(1)}, u32[]{:S(2)}, u32[]{:S(2)}) collective-permute-start(bf16[256,256]{1,0:T(8,128)(2,1)S(1)} %get-tuple-element.44), channel_id=1, source_target_pairs={{0,32},{16,48},{32,0},{48,16},{1,33},{17,49},{33,1},{49,17},{2,34}... | collective-permute-start | bytes 393224 | tf_op jit(solution)/shard_map/ppermute | solution.py:157
  23.7 1.6 %class1.1 = (bf16[256,256]{1,0:T(8,128)(2,1)S(1)}, bf16[256,2048]{1,0:T(8,128)(2,1)S(1)}, f32[8,128]{1,0:T(8,128)S(1)}) custom-call(s32[24,128]{1,0:T(8,128)S(1)} %get-tuple-element.26.plan, bf16[2048,128]{1,0:T(8,128)(2,1)S(1)} %bitcast.16, bf16[2048,128]{1,0:T(8,128)(2,1)S(1)} %bitcast.11, f32[2,2048]{1,0:T(2,128)S(1)} %pad_maximum_fusion.1.stats0, ...), custom_call_target="tpu_custom_call" | custom-call | bytes 4096 | tf_op jit(solution)/shard_map/class1/pallas_call | solution.py:27
  25.3 1.6 %class3.1 = (bf16[256,256]{1,0:T(8,128)(2,1)S(1)}, bf16[256,2048]{1,0:T(8,128)(2,1)S(1)}, f32[8,128]{1,0:T(8,128)S(1)}) custom-call(s32[24,128]{1,0:T(8,128)S(1)} %get-tuple-element.26.plan, bf16[2048,128]{1,0:T(8,128)(2,1)S(1)} %bitcast.17, bf16[2048,128]{1,0:T(8,128)(2,1)S(1)} %bitcast.12, f32[2,2048]{1,0:T(2,128)S(1)} %pad_maximum_fusion.1.stats0, ...), custom_call_target="tpu_custom_call" | custom-call | bytes 4096 | tf_op jit(solution)/shard_map/class3/pallas_call | solution.py:27
  26.8 1.2 %collective-permute-start.12 = (bf16[256,256]{1,0:T(8,128)(2,1)S(1)}, bf16[256,256]{1,0:T(8,128)(2,1)S(1)}, u32[]{:S(2)}, u32[]{:S(2)}) collective-permute-start(bf16[256,256]{1,0:T(8,128)(2,1)S(1)} %get-tuple-element.45), channel_id=1, source_target_pairs={{0,48},{16,32},{32,16},{48,0},{1,49},{17,33},{33,17},{49,1},{2,50}... | collective-permute-start | bytes 393224 | tf_op jit(solution)/shard_map/ppermute | solution.py:157
  28.0 1.8 %query.1 = (f32[2048,128]{1,0:T(8,128)S(1)}, bf16[2048,128]{1,0:T(8,128)(2,1)S(1)}, f32[8,128]{1,0:T(8,128)S(1)}) custom-call(bf16[256,256]{1,0:T(8,128)(2,1)S(1)} %get-tuple-element.27.kv.kv0, bf16[256,256]{1,0:T(8,128)(2,1)S(1)} %collective-permute-done.3.kv.kv1, bf16[256,256]{1,0:T(8,128)(2,1)S(1)} %collective-permute-done.4.kv.kv2, ...), custom_call_target="tpu_custom_call" | custom-call | bytes 4096 | tf_op jit(solution)/shard_map/query/pallas_call | solution.py:27
  29.8 0.1 collective-permute-start.9
  29.9 3.2 %collective-permute-done.12.part3 = bf16[256,256]{1,0:T(8,128)(2,1)S(1)} collective-permute-done((bf16[256,256]{1,0:T(8,128)(2,1)S(1)}, bf16[256,256]{1,0:T(8,128)(2,1)S(1)}, u32[]{:S(2)}, u32[]{:S(2)}) %collective-permute-start.12) | collective-permute-done | bytes 131104 | tf_op jit(solution)/shard_map/ppermute | solution.py:157
  33.1 1.0 %total.1 = bf16[8,4,16,256]{3,2,1,0:T(8,128)(2,1)} custom-call(s32[24,128]{1,0:T(8,128)S(1)} %get-tuple-element.26.plan, f32[256,256]{1,0:T(8,128)S(1)} %get-tuple-element.42.part0, bf16[256,256]{1,0:T(8,128)(2,1)S(1)} %collective-permute-done.10.part1, bf16[256,256]{1,0:T(8,128)(2,1)S(1)} %collective-permute-done.11.part2, ...), custom_call_target="tpu_custom_call" | custom-call | bytes 262144 | tf_op jit(solution)/shard_map/total/pallas_call | solution.py:27
  34.1 11.1 %all-to-all-start = ((bf16[32,16,256]{2,1,0:T(8,128)(2,1)}), bf16[32,16,256]{2,1,0:T(8,128)(2,1)S(1)}, u32[]{:S(2)}, u32[]{:S(2)}) async-start(bf16[32,16,256]{2,1,0:T(8,128)(2,1)} %bitcast.6), calls=%async_computation | async-start | bytes 524288 | tf_op jit(solution)/shard_map/all_to_all | solution.py:206
  45.2 0.9 %join.1 = bf16[2048,128]{1,0:T(8,128)(2,1)} custom-call(f32[2048,128]{1,0:T(8,128)S(1)} %get-tuple-element.40.mine, bf16[2048,128]{1,0:T(8,128)(2,1)S(1)} %collective-permute-done.9.theirs), custom_call_target="tpu_custom_call" | custom-call | bytes 2097152 | tf_op jit(solution)/shard_map/join/pallas_call | solution.py:27
  46.1 10.2 %all-to-all-done.moved = bf16[32,16,256]{2,1,0:T(8,128)(2,1)S(1)} async-done(((bf16[32,16,256]{2,1,0:T(8,128)(2,1)}), bf16[32,16,256]{2,1,0:T(8,128)(2,1)S(1)}, u32[]{:S(2)}, u32[]{:S(2)}) %all-to-all-start) | async-done | bytes 262176 | tf_op jit(solution)/shard_map/all_to_all | solution.py:206
  56.3 0.7 %finish.1 = (bf16[16,1024]{1,0:T(8,128)(2,1)}, bf16[16,1024]{1,0:T(8,128)(2,1)}) custom-call(bf16[32,16,256]{2,1,0:T(8,128)(2,1)S(1)} %all-to-all-done.moved), custom_call_target="tpu_custom_call" | custom-call | bytes 262144 | tf_op jit(solution)/shard_map/finish/pallas_call | solution.py:27
  (24 shorter events, 0.1 us)
Async XLA Ops:
  0.6 6.1 %copy-start.4 = (f32[16,128]{1,0:T(8,128)S(1)}, f32[16,128]{1,0:T(8,128)}, u32[]{:S(2)}) copy-start(f32[16,128]{1,0:T(8,128)} %param.13) | copy-start | bytes 24580
  1.4 7.3 %collective-permute-start.2 = (bf16[128,256]{1,0:T(8,128)(2,1)S(1)}, bf16[128,256]{1,0:T(8,128)(2,1)S(1)}, u32[]{:S(2)}, u32[]{:S(2)}) collective-permute-start(bf16[128,256]{1,0:T(8,128)(2,1)S(1)} %pad_maximum_fusion.own), channel_id=1, source_target_pairs={{0,192},{64,128},{128,64},{192,0},{1,193},{65,129},{129,65},{193,1... | collective-permute-start | bytes 196616 | tf_op jit(solution)/shard_map/ppermute | solution.py:157
  3.4 6.7 %collective-permute-start.1 = (bf16[128,256]{1,0:T(8,128)(2,1)S(1)}, bf16[128,256]{1,0:T(8,128)(2,1)S(1)}, u32[]{:S(2)}, u32[]{:S(2)}) collective-permute-start(bf16[128,256]{1,0:T(8,128)(2,1)S(1)} %pad_maximum_fusion.own), channel_id=1, source_target_pairs={{0,128},{64,192},{128,0},{192,64},{1,129},{65,193},{129,1},{193,65... | collective-permute-start | bytes 196616 | tf_op jit(solution)/shard_map/ppermute | solution.py:157
  5.7 5.2 %collective-permute-start = (bf16[128,256]{1,0:T(8,128)(2,1)S(1)}, bf16[128,256]{1,0:T(8,128)(2,1)S(1)}, u32[]{:S(2)}, u32[]{:S(2)}) collective-permute-start(bf16[128,256]{1,0:T(8,128)(2,1)S(1)} %pad_maximum_fusion.own), channel_id=1, source_target_pairs={{0,64},{64,0},{128,192},{192,128},{1,65},{65,1},{129,193},{193,129... | collective-permute-start | bytes 196616 | tf_op jit(solution)/shard_map/ppermute | solution.py:157
  6.2 9.1 %collective-permute-start.6 = (bf16[2048,128]{1,0:T(8,128)(2,1)}, bf16[2048,128]{1,0:T(8,128)(2,1)S(1)}, u32[]{:S(2)}, u32[]{:S(2)}) collective-permute-start(bf16[2048,128]{1,0:T(8,128)(2,1)} %bitcast.13), channel_id=1, source_target_pairs={{0,8},{8,0},{1,9},{9,1},{2,10},{10,2},{3,11},{11,3},{4,12},{12,4},... | collective-permute-start | bytes 1572872 | tf_op jit(solution)/shard_map/ppermute | solution.py:157
  6.3 9.1 %collective-permute-start.7 = (bf16[2048,128]{1,0:T(8,128)(2,1)}, bf16[2048,128]{1,0:T(8,128)(2,1)S(1)}, u32[]{:S(2)}, u32[]{:S(2)}) collective-permute-start(bf16[2048,128]{1,0:T(8,128)(2,1)} %bitcast.8), channel_id=1, source_target_pairs={{0,8},{8,0},{1,9},{9,1},{2,10},{10,2},{3,11},{11,3},{4,12},{12,4},... | collective-permute-start | bytes 1572872 | tf_op jit(solution)/shard_map/ppermute | solution.py:157
  7.0 8.4 %copy-start = (bf16[128,16,128]{2,1,0:T(8,128)(2,1)S(1)}, bf16[128,16,128]{2,1,0:T(8,128)(2,1)}, u32[]{:S(2)}) copy-start(bf16[128,16,128]{2,1,0:T(8,128)(2,1)} %param.12) | copy-start | bytes 1572868
  7.0 8.4 %copy-start.1 = (bf16[128,16,128]{2,1,0:T(8,128)(2,1)S(1)}, bf16[128,16,128]{2,1,0:T(8,128)(2,1)}, u32[]{:S(2)}) copy-start(bf16[128,16,128]{2,1,0:T(8,128)(2,1)} %param.8) | copy-start | bytes 1572868
  8.7 0.7 %copy-start.2 = (s32[32]{0:T(128)S(1)}, s32[32]{0:T(128)}, u32[]{:S(2)}) copy-start(s32[32]{0:T(128)} %order.1) | copy-start | bytes 388
  8.7 0.7 %copy-start.3 = (s32[12]{0:T(128)S(1)}, s32[12]{0:T(128)}, u32[]{:S(2)}) copy-start(s32[12]{0:T(128)} %lengths.1) | copy-start | bytes 148
  8.8 6.2 %collective-permute-start.8 = (f32[2,2048]{1,0:T(2,128)S(1)}, f32[2,2048]{1,0:T(2,128)S(1)}, u32[]{:S(2)}, u32[]{:S(2)}) collective-permute-start(f32[2,2048]{1,0:T(2,128)S(1)} %pad_maximum_fusion.1.stats0), channel_id=1, source_target_pairs={{0,8},{8,0},{1,9},{9,1},{2,10},{10,2},{3,11},{11,3},{4,12},{12,4},... | collective-permute-start | bytes 49160 | tf_op jit(solution)/shard_map/ppermute | solution.py:157
  11.0 7.8 %collective-permute-start.4 = (bf16[256,256]{1,0:T(8,128)(2,1)S(1)}, bf16[256,256]{1,0:T(8,128)(2,1)S(1)}, u32[]{:S(2)}, u32[]{:S(2)}) collective-permute-start(bf16[256,256]{1,0:T(8,128)(2,1)S(1)} %get-tuple-element.29), channel_id=1, source_target_pairs={{0,32},{16,48},{32,0},{48,16},{1,33},{17,49},{33,1},{49,17},{2,34}... | collective-permute-start | bytes 393224 | tf_op jit(solution)/shard_map/ppermute | solution.py:157
  14.3 9.4 %collective-permute-start.3 = (bf16[256,256]{1,0:T(8,128)(2,1)S(1)}, bf16[256,256]{1,0:T(8,128)(2,1)S(1)}, u32[]{:S(2)}, u32[]{:S(2)}) collective-permute-start(bf16[256,256]{1,0:T(8,128)(2,1)S(1)} %get-tuple-element.28), channel_id=1, source_target_pairs={{0,16},{16,0},{32,48},{48,32},{1,17},{17,1},{33,49},{49,33},{2,18}... | collective-permute-start | bytes 393224 | tf_op jit(solution)/shard_map/ppermute | solution.py:157
  15.0 10.3 %collective-permute-start.5 = (bf16[256,256]{1,0:T(8,128)(2,1)S(1)}, bf16[256,256]{1,0:T(8,128)(2,1)S(1)}, u32[]{:S(2)}, u32[]{:S(2)}) collective-permute-start(bf16[256,256]{1,0:T(8,128)(2,1)S(1)} %get-tuple-element.30), channel_id=1, source_target_pairs={{0,48},{16,32},{32,16},{48,0},{1,49},{17,33},{33,17},{49,1},{2,50}... | collective-permute-start | bytes 393224 | tf_op jit(solution)/shard_map/ppermute | solution.py:157
  20.4 9.5 %collective-permute-start.11 = (bf16[256,256]{1,0:T(8,128)(2,1)S(1)}, bf16[256,256]{1,0:T(8,128)(2,1)S(1)}, u32[]{:S(2)}, u32[]{:S(2)}) collective-permute-start(bf16[256,256]{1,0:T(8,128)(2,1)S(1)} %get-tuple-element.44), channel_id=1, source_target_pairs={{0,32},{16,48},{32,0},{48,16},{1,33},{17,49},{33,1},{49,17},{2,34}... | collective-permute-start | bytes 393224 | tf_op jit(solution)/shard_map/ppermute | solution.py:157
  26.8 6.3 %collective-permute-start.12 = (bf16[256,256]{1,0:T(8,128)(2,1)S(1)}, bf16[256,256]{1,0:T(8,128)(2,1)S(1)}, u32[]{:S(2)}, u32[]{:S(2)}) collective-permute-start(bf16[256,256]{1,0:T(8,128)(2,1)S(1)} %get-tuple-element.45), channel_id=1, source_target_pairs={{0,48},{16,32},{32,16},{48,0},{1,49},{17,33},{33,17},{49,1},{2,50}... | collective-permute-start | bytes 393224 | tf_op jit(solution)/shard_map/ppermute | solution.py:157
  28.0 5.1 %collective-permute-start.10 = (bf16[256,256]{1,0:T(8,128)(2,1)S(1)}, bf16[256,256]{1,0:T(8,128)(2,1)S(1)}, u32[]{:S(2)}, u32[]{:S(2)}) collective-permute-start(bf16[256,256]{1,0:T(8,128)(2,1)S(1)} %get-tuple-element.43), channel_id=1, source_target_pairs={{0,16},{16,0},{32,48},{48,32},{1,17},{17,1},{33,49},{49,33},{2,18}... | collective-permute-start | bytes 393224 | tf_op jit(solution)/shard_map/ppermute | solution.py:157
  29.8 15.4 %collective-permute-start.9 = (bf16[2048,128]{1,0:T(8,128)(2,1)S(1)}, bf16[2048,128]{1,0:T(8,128)(2,1)S(1)}, u32[]{:S(2)}, u32[]{:S(2)}) collective-permute-start(bf16[2048,128]{1,0:T(8,128)(2,1)S(1)} %get-tuple-element.41), channel_id=1, source_target_pairs={{0,8},{8,0},{1,9},{9,1},{2,10},{10,2},{3,11},{11,3},{4,12},{12,4},... | collective-permute-start | bytes 1572872 | tf_op jit(solution)/shard_map/ppermute | solution.py:157
  34.1 22.1 %all-to-all-start = ((bf16[32,16,256]{2,1,0:T(8,128)(2,1)}), bf16[32,16,256]{2,1,0:T(8,128)(2,1)S(1)}, u32[]{:S(2)}, u32[]{:S(2)}) async-start(bf16[32,16,256]{2,1,0:T(8,128)(2,1)} %bitcast.6), calls=%async_computation | async-start | bytes 524288 | tf_op jit(solution)/shard_map/all_to_all | solution.py:206

commit v9 on v8

--- a/solution.py
+++ b/solution.py
@@ -140,15 +140,17 @@
             z = jnp.max(plan[row : row + 1, :])
             acc[z] += part[j * BLK : (j + 1) * BLK, :].astype(jnp.float32)
     for z in range(ZL):
-        out[:, z] = acc[z].reshape(KVH, BLK // KVH, acc.shape[2]).astype(out.dtype)
+        for k in range(KVH):
+            share = acc.shape[1] // KVH
+            out[k % ZH * NX + k // ZH, z] = acc[z, k * share : (k + 1) * share, :].astype(out.dtype)
 
 
 def finish_kernel(moved, gk_ref, gv_ref):
     dh = moved.shape[2] // 2
     for k in range(KVH):
-        grad = moved[k * ZL].astype(jnp.float32)
+        grad = moved[(k % ZH * NX + k // ZH) * ZL].astype(jnp.float32)
         for z in range(1, ZL):
-            grad += moved[k * ZL + z].astype(jnp.float32)
+            grad += moved[(k % ZH * NX + k // ZH) * ZL + z].astype(jnp.float32)
         gk_ref[:, k * dh : (k + 1) * dh] = grad[:, :dh].astype(gk_ref.dtype)
         gv_ref[:, k * dh : (k + 1) * dh] = grad[:, dh:].astype(gv_ref.dtype)
 
@@ -204,7 +206,7 @@
     )
     share = BLK // KVH
     moved = lax.all_to_all(
-        total.reshape(ZL * KVH, share, wide), ("x", "zh", "zl"), split_axis=0, concat_axis=0, tiled=True
+        total.reshape(ZL * KVH, share, wide), ("zh", "x", "zl"), split_axis=0, concat_axis=0, tiled=True
     )
     out = shape((share, KVH * dh), bf16)
     grad_keys, grad_values = call(finish_kernel, (out, out), (moved,), "finish")

time: 57.2 us -> 57.7 us (level)
  the two profiles are of different devices: /device:TPU:32 before, /device:TPU:16 now
where the time goes in v9:
time: 57.7 us; the launch traced here: 57.5 us
  starting transfers between devices  25.9 us (45%)
  waiting for transfers between devices  16.1 us (28%)
  Pallas kernels  11.3 us (20%)
  other arithmetic  2.44 us (4%)
  between operations  0.83 us (1%)
  local copies, waits for them, and re-layouts  0.82 us (1%)
    ppermute x13, starting transfers between devices, swap(): return lax.ppermute(x, axis, [(i, i ^ mask) for i in range(size)])  15.3 us
    all_to_all x1, waiting for transfers between devices, local(): lax.all_to_all(total.reshape(ZL * KVH, share, wide), ('zh', 'x', 'zl'), s...  12.2 us
    pallas_call x10, Pallas kernels, call(): pl.pallas_call(body, out_shape=outs, in_specs=specs or [VMEM] * len(input...  11.3 us
    all_to_all x1, starting transfers between devices, local(): lax.all_to_all(total.reshape(ZL * KVH, share, wide), ('zh', 'x', 'zl'), s...  10.6 us
    ppermute x13, waiting for transfers between devices, swap(): return lax.ppermute(x, axis, [(i, i ^ mask) for i in range(size)])  3.84 us
    reduce_sum x1, other arithmetic, local(): delta = jnp.sum(out_grad.astype(f32) * outputs.astype(f32), axis=2)  1.63 us
  transfers between devices with their start and end apart: 14, of which 5 were waited for; matrix products, arithmetic and copies ran while one was open for 3% of the time, Pallas kernels for 19%

profile of v9, /device:TPU:16, one launch (start us, length us, event | category | flops | bytes accessed | tf_op | source)
XLA Modules:
  0.0 57.5 jit_solution(2903641038948084252)
XLA Ops:
  0.6 0.8 %pad_maximum_fusion.own = bf16[128,256]{1,0:T(8,128)(2,1)S(1)} fusion(bf16[128,128]{1,0:T(8,128)(2,1)} %bitcast.19, bf16[128,128]{1,0:T(8,128)(2,1)} %bitcast.20), kind=kLoop, calls=%fused_computation.1 | loop fusion | flops 131072 | bytes 131072 | tf_op jit(solution)/shard_map/concatenate | solution.py:169
  1.4 4.7 %collective-permute-start.2 = (bf16[128,256]{1,0:T(8,128)(2,1)S(1)}, bf16[128,256]{1,0:T(8,128)(2,1)S(1)}, u32[]{:S(2)}, u32[]{:S(2)}) collective-permute-start(bf16[128,256]{1,0:T(8,128)(2,1)S(1)} %pad_maximum_fusion.own), channel_id=1, source_target_pairs={{0,192},{64,128},{128,64},{192,0},{1,193},{65,129},{129,65},{193,1... | collective-permute-start | bytes 196616 | tf_op jit(solution)/shard_map/ppermute | solution.py:159
  6.1 0.7 %collective-permute-start = (bf16[128,256]{1,0:T(8,128)(2,1)S(1)}, bf16[128,256]{1,0:T(8,128)(2,1)S(1)}, u32[]{:S(2)}, u32[]{:S(2)}) collective-permute-start(bf16[128,256]{1,0:T(8,128)(2,1)S(1)} %pad_maximum_fusion.own), channel_id=1, source_target_pairs={{0,64},{64,0},{128,192},{192,128},{1,65},{65,1},{129,193},{193,129... | collective-permute-start | bytes 196616 | tf_op jit(solution)/shard_map/ppermute | solution.py:159
  6.8 0.5 collective-permute-start.7
  7.3 0.1 copy.12
  7.4 0.1 stack_reshape.6
  7.5 1.6 %multiply_reduce_fusion = f32[128,16]{1,0:T(8,128)S(1)} fusion(bf16[128,16,128]{2,1,0:T(8,128)(2,1)} %param.11, bf16[128,16,128]{2,1,0:T(8,128)(2,1)} %param.12), kind=kLoop, calls=%fused_computation | loop fusion | flops 1046528 | bytes 1056768 | tf_op jit(solution)/shard_map/reduce_sum | solution.py:176
  9.2 0.1 stack_reshape.7
  9.3 0.1 collective-permute-start.8
  9.4 0.5 copy-done.2
  9.9 0.7 %plan.1 = (s32[24,128]{1,0:T(8,128)S(1)}, s32[4,2048]{1,0:T(4,128)S(1)}) custom-call(s32[32]{0:T(128)S(1)} %copy-done.2, s32[12]{0:T(128)S(1)} %copy-done.3), custom_call_target="tpu_custom_call" | custom-call | bytes 262144 | tf_op jit(solution)/shard_map/plan/pallas_call | solution.py:27
  10.6 0.8 %collective-permute-done.1.col2 = bf16[128,256]{1,0:T(8,128)(2,1)S(1)} collective-permute-done((bf16[128,256]{1,0:T(8,128)(2,1)S(1)}, bf16[128,256]{1,0:T(8,128)(2,1)S(1)}, u32[]{:S(2)}, u32[]{:S(2)}) %collective-permute-start.1) | collective-permute-done | bytes 65568 | tf_op jit(solution)/shard_map/ppermute | solution.py:159
  11.5 0.3 collective-permute-done.col1
  11.9 0.4 collective-permute-start.4
  12.3 2.2 %collective-permute-start.3 = (bf16[256,256]{1,0:T(8,128)(2,1)S(1)}, bf16[256,256]{1,0:T(8,128)(2,1)S(1)}, u32[]{:S(2)}, u32[]{:S(2)}) collective-permute-start(bf16[256,256]{1,0:T(8,128)(2,1)S(1)} %get-tuple-element.28), channel_id=1, source_target_pairs={{0,16},{16,0},{32,48},{48,32},{1,17},{17,1},{33,49},{49,33},{2,18}... | collective-permute-start | bytes 393224 | tf_op jit(solution)/shard_map/ppermute | solution.py:159
  14.5 1.6 %collective-permute-start.5 = (bf16[256,256]{1,0:T(8,128)(2,1)S(1)}, bf16[256,256]{1,0:T(8,128)(2,1)S(1)}, u32[]{:S(2)}, u32[]{:S(2)}) collective-permute-start(bf16[256,256]{1,0:T(8,128)(2,1)S(1)} %get-tuple-element.30), channel_id=1, source_target_pairs={{0,48},{16,32},{32,16},{48,0},{1,49},{17,33},{33,17},{49,1},{2,50}... | collective-permute-start | bytes 393224 | tf_op jit(solution)/shard_map/ppermute | solution.py:159
  16.1 1.6 %class0.1 = (f32[256,256]{1,0:T(8,128)S(1)}, bf16[256,2048]{1,0:T(8,128)(2,1)S(1)}, f32[8,128]{1,0:T(8,128)S(1)}) custom-call(s32[24,128]{1,0:T(8,128)S(1)} %get-tuple-element.26.plan, bf16[2048,128]{1,0:T(8,128)(2,1)S(1)} %bitcast.14, bf16[2048,128]{1,0:T(8,128)(2,1)S(1)} %bitcast.9, f32[2,2048]{1,0:T(2,128)S(1)} %pad_maximum_fusion.1.stats0, ...), custom_call_target="tpu_custom_call" | custom-call | bytes 4096 | tf_op jit(solution)/shard_map/class0/pallas_call | solution.py:27
  17.7 1.6 %collective-permute-done.4.kv.kv2 = bf16[256,256]{1,0:T(8,128)(2,1)S(1)} collective-permute-done((bf16[256,256]{1,0:T(8,128)(2,1)S(1)}, bf16[256,256]{1,0:T(8,128)(2,1)S(1)}, u32[]{:S(2)}, u32[]{:S(2)}) %collective-permute-start.4) | collective-permute-done | bytes 131104 | tf_op jit(solution)/shard_map/ppermute | solution.py:159
  19.3 1.6 %class2.1 = (bf16[256,256]{1,0:T(8,128)(2,1)S(1)}, bf16[256,2048]{1,0:T(8,128)(2,1)S(1)}, f32[8,128]{1,0:T(8,128)S(1)}) custom-call(s32[24,128]{1,0:T(8,128)S(1)} %get-tuple-element.26.plan, bf16[2048,128]{1,0:T(8,128)(2,1)S(1)} %bitcast.15, bf16[2048,128]{1,0:T(8,128)(2,1)S(1)} %bitcast.10, f32[2,2048]{1,0:T(2,128)S(1)} %pad_maximum_fusion.1.stats0, ...), custom_call_target="tpu_custom_call" | custom-call | bytes 4096 | tf_op jit(solution)/shard_map/class2/pallas_call | solution.py:27
  20.8 1.2 %collective-permute-start.11 = (bf16[256,256]{1,0:T(8,128)(2,1)S(1)}, bf16[256,256]{1,0:T(8,128)(2,1)S(1)}, u32[]{:S(2)}, u32[]{:S(2)}) collective-permute-start(bf16[256,256]{1,0:T(8,128)(2,1)S(1)} %get-tuple-element.44), channel_id=1, source_target_pairs={{0,32},{16,48},{32,0},{48,16},{1,33},{17,49},{33,1},{49,17},{2,34}... | collective-permute-start | bytes 393224 | tf_op jit(solution)/shard_map/ppermute | solution.py:159
  22.1 1.6 %class1.1 = (bf16[256,256]{1,0:T(8,128)(2,1)S(1)}, bf16[256,2048]{1,0:T(8,128)(2,1)S(1)}, f32[8,128]{1,0:T(8,128)S(1)}) custom-call(s32[24,128]{1,0:T(8,128)S(1)} %get-tuple-element.26.plan, bf16[2048,128]{1,0:T(8,128)(2,1)S(1)} %bitcast.16, bf16[2048,128]{1,0:T(8,128)(2,1)S(1)} %bitcast.11, f32[2,2048]{1,0:T(2,128)S(1)} %pad_maximum_fusion.1.stats0, ...), custom_call_target="tpu_custom_call" | custom-call | bytes 4096 | tf_op jit(solution)/shard_map/class1/pallas_call | solution.py:27
  23.6 1.6 %class3.1 = (bf16[256,256]{1,0:T(8,128)(2,1)S(1)}, bf16[256,2048]{1,0:T(8,128)(2,1)S(1)}, f32[8,128]{1,0:T(8,128)S(1)}) custom-call(s32[24,128]{1,0:T(8,128)S(1)} %get-tuple-element.26.plan, bf16[2048,128]{1,0:T(8,128)(2,1)S(1)} %bitcast.17, bf16[2048,128]{1,0:T(8,128)(2,1)S(1)} %bitcast.12, f32[2,2048]{1,0:T(2,128)S(1)} %pad_maximum_fusion.1.stats0, ...), custom_call_target="tpu_custom_call" | custom-call | bytes 4096 | tf_op jit(solution)/shard_map/class3/pallas_call | solution.py:27
  25.2 1.8 %collective-permute-start.12 = (bf16[256,256]{1,0:T(8,128)(2,1)S(1)}, bf16[256,256]{1,0:T(8,128)(2,1)S(1)}, u32[]{:S(2)}, u32[]{:S(2)}) collective-permute-start(bf16[256,256]{1,0:T(8,128)(2,1)S(1)} %get-tuple-element.45), channel_id=1, source_target_pairs={{0,48},{16,32},{32,16},{48,0},{1,49},{17,33},{33,17},{49,1},{2,50}... | collective-permute-start | bytes 393224 | tf_op jit(solution)/shard_map/ppermute | solution.py:159
  27.0 2.0 %collective-permute-start.10 = (bf16[256,256]{1,0:T(8,128)(2,1)S(1)}, bf16[256,256]{1,0:T(8,128)(2,1)S(1)}, u32[]{:S(2)}, u32[]{:S(2)}) collective-permute-start(bf16[256,256]{1,0:T(8,128)(2,1)S(1)} %get-tuple-element.43), channel_id=1, source_target_pairs={{0,16},{16,0},{32,48},{48,32},{1,17},{17,1},{33,49},{49,33},{2,18}... | collective-permute-start | bytes 393224 | tf_op jit(solution)/shard_map/ppermute | solution.py:159
  29.0 1.8 %query.1 = (f32[2048,128]{1,0:T(8,128)S(1)}, bf16[2048,128]{1,0:T(8,128)(2,1)S(1)}, f32[8,128]{1,0:T(8,128)S(1)}) custom-call(bf16[256,256]{1,0:T(8,128)(2,1)S(1)} %get-tuple-element.27.kv.kv0, bf16[256,256]{1,0:T(8,128)(2,1)S(1)} %collective-permute-done.3.kv.kv1, bf16[256,256]{1,0:T(8,128)(2,1)S(1)} %collective-permute-done.4.kv.kv2, ...), custom_call_target="tpu_custom_call" | custom-call | bytes 4096 | tf_op jit(solution)/shard_map/query/pallas_call | solution.py:27
  30.8 0.1 collective-permute-start.9
  30.9 1.1 %collective-permute-done.10.part1 = bf16[256,256]{1,0:T(8,128)(2,1)S(1)} collective-permute-done((bf16[256,256]{1,0:T(8,128)(2,1)S(1)}, bf16[256,256]{1,0:T(8,128)(2,1)S(1)}, u32[]{:S(2)}, u32[]{:S(2)}) %collective-permute-start.10) | collective-permute-done | bytes 131104 | tf_op jit(solution)/shard_map/ppermute | solution.py:159
  32.0 1.0 %total.1 = bf16[8,4,16,256]{3,2,1,0:T(8,128)(2,1)} custom-call(s32[24,128]{1,0:T(8,128)S(1)} %get-tuple-element.26.plan, f32[256,256]{1,0:T(8,128)S(1)} %get-tuple-element.42.part0, bf16[256,256]{1,0:T(8,128)(2,1)S(1)} %collective-permute-done.10.part1, bf16[256,256]{1,0:T(8,128)(2,1)S(1)} %collective-permute-done.11.part2, ...), custom_call_target="tpu_custom_call" | custom-call | bytes 262144 | tf_op jit(solution)/shard_map/total/pallas_call | solution.py:27
  33.0 10.6 %all-to-all-start = ((bf16[32,16,256]{2,1,0:T(8,128)(2,1)}), bf16[32,16,256]{2,1,0:T(8,128)(2,1)S(1)}, u32[]{:S(2)}, u32[]{:S(2)}) async-start(bf16[32,16,256]{2,1,0:T(8,128)(2,1)} %bitcast.6), calls=%async_computation | async-start | bytes 524288 | tf_op jit(solution)/shard_map/all_to_all | solution.py:208
  43.7 0.9 %join.1 = bf16[2048,128]{1,0:T(8,128)(2,1)} custom-call(f32[2048,128]{1,0:T(8,128)S(1)} %get-tuple-element.40.mine, bf16[2048,128]{1,0:T(8,128)(2,1)S(1)} %collective-permute-done.9.theirs), custom_call_target="tpu_custom_call" | custom-call | bytes 2097152 | tf_op jit(solution)/shard_map/join/pallas_call | solution.py:27
  44.5 12.2 %all-to-all-done.moved = bf16[32,16,256]{2,1,0:T(8,128)(2,1)S(1)} async-done(((bf16[32,16,256]{2,1,0:T(8,128)(2,1)}), bf16[32,16,256]{2,1,0:T(8,128)(2,1)S(1)}, u32[]{:S(2)}, u32[]{:S(2)}) %all-to-all-start) | async-done | bytes 262176 | tf_op jit(solution)/shard_map/all_to_all | solution.py:208
  56.8 0.7 %finish.1 = (bf16[16,1024]{1,0:T(8,128)(2,1)}, bf16[16,1024]{1,0:T(8,128)(2,1)}) custom-call(bf16[32,16,256]{2,1,0:T(8,128)(2,1)S(1)} %all-to-all-done.moved), custom_call_target="tpu_custom_call" | custom-call | bytes 262144 | tf_op jit(solution)/shard_map/finish/pallas_call | solution.py:27
  (24 shorter events, 0.2 us)
Async XLA Ops:
  0.6 6.7 %copy-start.4 = (f32[16,128]{1,0:T(8,128)S(1)}, f32[16,128]{1,0:T(8,128)}, u32[]{:S(2)}) copy-start(f32[16,128]{1,0:T(8,128)} %param.13) | copy-start | bytes 24580
  1.4 7.9 %collective-permute-start.2 = (bf16[128,256]{1,0:T(8,128)(2,1)S(1)}, bf16[128,256]{1,0:T(8,128)(2,1)S(1)}, u32[]{:S(2)}, u32[]{:S(2)}) collective-permute-start(bf16[128,256]{1,0:T(8,128)(2,1)S(1)} %pad_maximum_fusion.own), channel_id=1, source_target_pairs={{0,192},{64,128},{128,64},{192,0},{1,193},{65,129},{129,65},{193,1... | collective-permute-start | bytes 196616 | tf_op jit(solution)/shard_map/ppermute | solution.py:159
  6.1 5.3 %collective-permute-start.1 = (bf16[128,256]{1,0:T(8,128)(2,1)S(1)}, bf16[128,256]{1,0:T(8,128)(2,1)S(1)}, u32[]{:S(2)}, u32[]{:S(2)}) collective-permute-start(bf16[128,256]{1,0:T(8,128)(2,1)S(1)} %pad_maximum_fusion.own), channel_id=1, source_target_pairs={{0,128},{64,192},{128,0},{192,64},{1,129},{65,193},{129,1},{193,65... | collective-permute-start | bytes 196616 | tf_op jit(solution)/shard_map/ppermute | solution.py:159
  6.1 5.7 %collective-permute-start = (bf16[128,256]{1,0:T(8,128)(2,1)S(1)}, bf16[128,256]{1,0:T(8,128)(2,1)S(1)}, u32[]{:S(2)}, u32[]{:S(2)}) collective-permute-start(bf16[128,256]{1,0:T(8,128)(2,1)S(1)} %pad_maximum_fusion.own), channel_id=1, source_target_pairs={{0,64},{64,0},{128,192},{192,128},{1,65},{65,1},{129,193},{193,129... | collective-permute-start | bytes 196616 | tf_op jit(solution)/shard_map/ppermute | solution.py:159
  6.8 9.3 %collective-permute-start.6 = (bf16[2048,128]{1,0:T(8,128)(2,1)}, bf16[2048,128]{1,0:T(8,128)(2,1)S(1)}, u32[]{:S(2)}, u32[]{:S(2)}) collective-permute-start(bf16[2048,128]{1,0:T(8,128)(2,1)} %bitcast.13), channel_id=1, source_target_pairs={{0,8},{8,0},{1,9},{9,1},{2,10},{10,2},{3,11},{11,3},{4,12},{12,4},... | collective-permute-start | bytes 1572872 | tf_op jit(solution)/shard_map/ppermute | solution.py:159
  6.8 9.3 %collective-permute-start.7 = (bf16[2048,128]{1,0:T(8,128)(2,1)}, bf16[2048,128]{1,0:T(8,128)(2,1)S(1)}, u32[]{:S(2)}, u32[]{:S(2)}) collective-permute-start(bf16[2048,128]{1,0:T(8,128)(2,1)} %bitcast.8), channel_id=1, source_target_pairs={{0,8},{8,0},{1,9},{9,1},{2,10},{10,2},{3,11},{11,3},{4,12},{12,4},... | collective-permute-start | bytes 1572872 | tf_op jit(solution)/shard_map/ppermute | solution.py:159
  7.5 8.6 %copy-start = (bf16[128,16,128]{2,1,0:T(8,128)(2,1)S(1)}, bf16[128,16,128]{2,1,0:T(8,128)(2,1)}, u32[]{:S(2)}) copy-start(bf16[128,16,128]{2,1,0:T(8,128)(2,1)} %param.12) | copy-start | bytes 1572868
  7.5 8.6 %copy-start.1 = (bf16[128,16,128]{2,1,0:T(8,128)(2,1)S(1)}, bf16[128,16,128]{2,1,0:T(8,128)(2,1)}, u32[]{:S(2)}) copy-start(bf16[128,16,128]{2,1,0:T(8,128)(2,1)} %param.8) | copy-start | bytes 1572868
  9.3 0.7 %copy-start.2 = (s32[32]{0:T(128)S(1)}, s32[32]{0:T(128)}, u32[]{:S(2)}) copy-start(s32[32]{0:T(128)} %order.1) | copy-start | bytes 388
  9.3 0.7 %copy-start.3 = (s32[12]{0:T(128)S(1)}, s32[12]{0:T(128)}, u32[]{:S(2)}) copy-start(s32[12]{0:T(128)} %lengths.1) | copy-start | bytes 148
  9.3 5.2 %collective-permute-start.8 = (f32[2,2048]{1,0:T(2,128)S(1)}, f32[2,2048]{1,0:T(2,128)S(1)}, u32[]{:S(2)}, u32[]{:S(2)}) collective-permute-start(f32[2,2048]{1,0:T(2,128)S(1)} %pad_maximum_fusion.1.stats0), channel_id=1, source_target_pairs={{0,8},{8,0},{1,9},{9,1},{2,10},{10,2},{3,11},{11,3},{4,12},{12,4},... | collective-permute-start | bytes 49160 | tf_op jit(solution)/shard_map/ppermute | solution.py:159
  11.9 7.4 %collective-permute-start.4 = (bf16[256,256]{1,0:T(8,128)(2,1)S(1)}, bf16[256,256]{1,0:T(8,128)(2,1)S(1)}, u32[]{:S(2)}, u32[]{:S(2)}) collective-permute-start(bf16[256,256]{1,0:T(8,128)(2,1)S(1)} %get-tuple-element.29), channel_id=1, source_target_pairs={{0,32},{16,48},{32,0},{48,16},{1,33},{17,49},{33,1},{49,17},{2,34}... | collective-permute-start | bytes 393224 | tf_op jit(solution)/shard_map/ppermute | solution.py:159
  12.3 9.7 %collective-permute-start.3 = (bf16[256,256]{1,0:T(8,128)(2,1)S(1)}, bf16[256,256]{1,0:T(8,128)(2,1)S(1)}, u32[]{:S(2)}, u32[]{:S(2)}) collective-permute-start(bf16[256,256]{1,0:T(8,128)(2,1)S(1)} %get-tuple-element.28), channel_id=1, source_target_pairs={{0,16},{16,0},{32,48},{48,32},{1,17},{17,1},{33,49},{49,33},{2,18}... | collective-permute-start | bytes 393224 | tf_op jit(solution)/shard_map/ppermute | solution.py:159
  14.5 9.1 %collective-permute-start.5 = (bf16[256,256]{1,0:T(8,128)(2,1)S(1)}, bf16[256,256]{1,0:T(8,128)(2,1)S(1)}, u32[]{:S(2)}, u32[]{:S(2)}) collective-permute-start(bf16[256,256]{1,0:T(8,128)(2,1)S(1)} %get-tuple-element.30), channel_id=1, source_target_pairs={{0,48},{16,32},{32,16},{48,0},{1,49},{17,33},{33,17},{49,1},{2,50}... | collective-permute-start | bytes 393224 | tf_op jit(solution)/shard_map/ppermute | solution.py:159
  20.8 10.1 %collective-permute-start.11 = (bf16[256,256]{1,0:T(8,128)(2,1)S(1)}, bf16[256,256]{1,0:T(8,128)(2,1)S(1)}, u32[]{:S(2)}, u32[]{:S(2)}) collective-permute-start(bf16[256,256]{1,0:T(8,128)(2,1)S(1)} %get-tuple-element.44), channel_id=1, source_target_pairs={{0,32},{16,48},{32,0},{48,16},{1,33},{17,49},{33,1},{49,17},{2,34}... | collective-permute-start | bytes 393224 | tf_op jit(solution)/shard_map/ppermute | solution.py:159
  25.2 5.7 %collective-permute-start.12 = (bf16[256,256]{1,0:T(8,128)(2,1)S(1)}, bf16[256,256]{1,0:T(8,128)(2,1)S(1)}, u32[]{:S(2)}, u32[]{:S(2)}) collective-permute-start(bf16[256,256]{1,0:T(8,128)(2,1)S(1)} %get-tuple-element.45), channel_id=1, source_target_pairs={{0,48},{16,32},{32,16},{48,0},{1,49},{17,33},{33,17},{49,1},{2,50}... | collective-permute-start | bytes 393224 | tf_op jit(solution)/shard_map/ppermute | solution.py:159
  27.0 5.0 %collective-permute-start.10 = (bf16[256,256]{1,0:T(8,128)(2,1)S(1)}, bf16[256,256]{1,0:T(8,128)(2,1)S(1)}, u32[]{:S(2)}, u32[]{:S(2)}) collective-permute-start(bf16[256,256]{1,0:T(8,128)(2,1)S(1)} %get-tuple-element.43), channel_id=1, source_target_pairs={{0,16},{16,0},{32,48},{48,32},{1,17},{17,1},{33,49},{49,33},{2,18}... | collective-permute-start | bytes 393224 | tf_op jit(solution)/shard_map/ppermute | solution.py:159
  30.8 12.9 %collective-permute-start.9 = (bf16[2048,128]{1,0:T(8,128)(2,1)S(1)}, bf16[2048,128]{1,0:T(8,128)(2,1)S(1)}, u32[]{:S(2)}, u32[]{:S(2)}) collective-permute-start(bf16[2048,128]{1,0:T(8,128)(2,1)S(1)} %get-tuple-element.41), channel_id=1, source_target_pairs={{0,8},{8,0},{1,9},{9,1},{2,10},{10,2},{3,11},{11,3},{4,12},{12,4},... | collective-permute-start | bytes 1572872 | tf_op jit(solution)/shard_map/ppermute | solution.py:159
  33.0 23.8 %all-to-all-start = ((bf16[32,16,256]{2,1,0:T(8,128)(2,1)}), bf16[32,16,256]{2,1,0:T(8,128)(2,1)S(1)}, u32[]{:S(2)}, u32[]{:S(2)}) async-start(bf16[32,16,256]{2,1,0:T(8,128)(2,1)} %bitcast.6), calls=%async_computation | async-start | bytes 524288 | tf_op jit(solution)/shard_map/all_to_all | solution.py:208
